TPU v7x, 32 devices: a whole 2x2x4 slice. The times are simulated.
32 devices in a mesh: groups: 2 (over x), expert: 4 (over y, core), dp: 4 (over z).
Axes of the slice: x: 2, y: 2, z: 4, core: 2. Of those that a mesh axis runs over, the one named last changes fastest.
Arguments:
- tokens: bfloat16 [4096, 4096], P(('groups', 'expert', 'dp')), parts along dimension 0, may hold values from -6 to 6
- expert_ids: int32 [4096, 8], P(('groups', 'expert', 'dp')), parts along dimension 0, may hold values from 0 to 255, all different within a row; in each aligned block of 128 rows (0 to 127, 128 to 255, ...) at most 6 rows name the same one
- gate_codes: int32 [4096, 8], P(('groups', 'expert', 'dp')), parts along dimension 0, may hold values from 1 to 32767
- cotangent: bfloat16 [4096, 4096], P(('groups', 'expert', 'dp')), parts along dimension 0, may hold values from -6 to 6
- gate_weight: bfloat16 [4, 4096, 1024], P('expert', 'dp'), may hold values from -0.09375 to 0.09375
- up_weight: bfloat16 [4, 4096, 1024], P('expert', 'dp'), may hold values from -0.09375 to 0.09375
- down_weight: bfloat16 [4, 1024, 4096], P('expert', None, 'dp'), may hold values from -0.1875 to 0.1875
- first_moment: bfloat16 [8, 1024, 4096], P(('groups', 'expert'), None, 'dp'), parts along dimension 0, may hold values from -6 to 6
- second_moment: bfloat16 [8, 1024, 4096], P(('groups', 'expert'), None, 'dp'), parts along dimension 0, may hold values from 0.63671875 to 6.375
- selected: int32 [6], P('groups'), parts along dimension 0, may hold values from 0 to 3, as said below
Outputs:
- mixed: bfloat16 [4096, 4096], P(('groups', 'expert', 'dp')), parts along dimension 0
- input_grad: bfloat16 [4096, 4096], P(('groups', 'expert', 'dp')), parts along dimension 0
- adam_step: bfloat16 [8, 1024, 4096], P(('groups', 'expert'), None, 'dp'), parts along dimension 0
- new_first: bfloat16 [8, 1024, 4096], P(('groups', 'expert'), None, 'dp'), parts along dimension 0
- new_second: bfloat16 [8, 1024, 4096], P(('groups', 'expert'), None, 'dp'), parts along dimension 0
There are 2 independent parts, one for each index of `groups`. A program takes and returns all parts, laid end to end along the dimension named above; an argument that names none is the same for every part. Nothing has to cross between parts.
Inputs may be any that keep to these rules, and one draw needn't show every extreme that they name: `expert_ids`: each row names 8 different experts; in each aligned block of 128 rows (the rows of one device) no expert is named by more than 6 rows. `selected`: 3 different expert ids.
All inputs are finite; a program needn't handle non-finite values.
Results may differ from a plain program's by a relative error of at most 0.0066.
Values may be sent and summed in bfloat16 or wider, within the bound.
No kernel may reach another device: no remote copies, remote signals or barrier semaphores. Data moves between devices by JAX's collectives and lax.ppermute only.
A program may use at most 64 MiB of HBM per device.

v0:
```python
import jax
import jax.numpy as jnp
from jax import lax
from jax.sharding import PartitionSpec as P

CAP = 6


BETA_ONE = 0.9
BETA_TWO = 0.95
ADAM_EPS = 1e-08


def route_tables(expert_ids, gate_codes, experts):
    code_values = gate_codes.astype(jnp.float32)
    gate_values = (2.5 * code_values / jnp.sum(code_values, axis=1, keepdims=True)).astype(
        jnp.bfloat16
    )
    labels = jnp.arange(experts, dtype=jnp.int32)
    picked = expert_ids[:, :, None] == labels[None, None, :]
    counts = jnp.sum(picked.astype(jnp.int32), axis=1)
    gate_each = jnp.sum(jnp.where(picked, gate_values.astype(jnp.float32)[:, :, None], 0.0), axis=1)
    before = jnp.cumsum(counts, axis=0) - counts
    slot_range = jnp.arange(CAP, dtype=jnp.int32)
    placed = (counts[:, :, None] > 0) & (before[:, :, None] == slot_range[None, None, :])
    placed_ones = jnp.transpose(placed, (1, 2, 0)).astype(jnp.bfloat16)
    placed_gates = jnp.transpose(jnp.where(placed, gate_each[:, :, None], 0.0), (1, 2, 0)).astype(
        jnp.bfloat16
    )
    return (placed_ones, placed_gates)


def adam_update(hidden, rows_dy, first_moment, second_moment):
    down_grad = jnp.einsum("fr,rd->fd", hidden, rows_dy, preferred_element_type=jnp.float32)
    moment_one = BETA_ONE * first_moment.astype(jnp.float32) + (1.0 - BETA_ONE) * down_grad
    moment_two = (
        BETA_TWO * second_moment.astype(jnp.float32) + (1.0 - BETA_TWO) * down_grad * down_grad
    )
    direction = moment_one / (jnp.sqrt(moment_two) + ADAM_EPS)
    return (
        direction.astype(jnp.bfloat16),
        moment_one.astype(jnp.bfloat16),
        moment_two.astype(jnp.bfloat16),
    )


def local(
    tokens,
    expert_ids,
    gate_codes,
    cotangent,
    gate_weight,
    up_weight,
    down_weight,
    first_moment,
    second_moment,
    selected,
):
    experts = lax.axis_size("expert")
    groups_dp = lax.axis_size("dp")
    tok_rows = tokens.shape[0]
    slice_width = tokens.shape[1] // groups_dp
    slot_count = experts * groups_dp * CAP
    placed_ones, placed_gates = route_tables(expert_ids, gate_codes, experts)
    features = tokens.reshape(tok_rows, groups_dp, slice_width)
    cot_features = cotangent.reshape(tok_rows, groups_dp, slice_width)
    sent_x = jnp.einsum(
        "ect,tjd->ejcd", placed_ones, features, preferred_element_type=jnp.float32
    ).astype(jnp.bfloat16)
    sent_dy = jnp.einsum(
        "ect,tjd->ejcd", placed_gates, cot_features, preferred_element_type=jnp.float32
    ).astype(jnp.bfloat16)
    packed = jnp.stack([sent_x, sent_dy]).reshape(2, experts * groups_dp, CAP, slice_width)
    arrived = lax.all_to_all(packed, ("expert", "dp"), split_axis=1, concat_axis=1, tiled=True)
    rows_x = arrived[0].reshape(slot_count, slice_width)
    rows_dy = arrived[1].reshape(slot_count, slice_width)
    w_gate = gate_weight[0]
    w_up = up_weight[0]
    w_down = down_weight[0]
    part_gate = w_gate
    part_up = w_up
    shares = lax.psum_scatter(
        jnp.stack(
            [
                jnp.einsum("dc,rd->cr", part_gate, rows_x, preferred_element_type=jnp.float32),
                jnp.einsum("dc,rd->cr", part_up, rows_x, preferred_element_type=jnp.float32),
            ],
            axis=1,
        ),
        "dp",
        scatter_dimension=0,
        tiled=True,
    )
    hidden_share = (jax.nn.silu(shares[:, 0]) * shares[:, 1]).astype(jnp.bfloat16)
    hidden = lax.all_gather(hidden_share, "dp", axis=0, tiled=True)
    gate_share = shares[:, 0]
    up_share = shares[:, 1]
    out_rows = jnp.einsum("fr,fd->rd", hidden, w_down, preferred_element_type=jnp.float32).astype(
        jnp.bfloat16
    )
    returned = lax.all_to_all(
        out_rows.reshape(experts * groups_dp, CAP, slice_width),
        ("expert", "dp"),
        split_axis=0,
        concat_axis=0,
        tiled=True,
    )
    returned = returned.reshape(experts, groups_dp, CAP, slice_width)
    mixed = jnp.einsum("ect,ejcd->tjd", placed_gates, returned, preferred_element_type=jnp.float32)
    mixed = mixed.astype(jnp.bfloat16).reshape(tok_rows, groups_dp * slice_width)
    hidden_grad = lax.psum_scatter(
        jnp.einsum("cd,rd->cr", w_down, rows_dy, preferred_element_type=jnp.float32),
        "dp",
        scatter_dimension=0,
        tiled=True,
    )
    sigmoid_gate = jax.nn.sigmoid(gate_share)
    gate_grad = (
        hidden_grad * up_share * sigmoid_gate * (1.0 + gate_share * (1.0 - sigmoid_gate))
    ).astype(jnp.bfloat16)
    up_grad = (hidden_grad * gate_share * sigmoid_gate).astype(jnp.bfloat16)
    part_gate = w_gate
    part_up = w_up
    running = jnp.einsum(
        "dc,cr->rd",
        part_gate,
        lax.all_gather(gate_grad, "dp", axis=0, tiled=True),
        preferred_element_type=jnp.float32,
    )
    row_grads = (
        running
        + jnp.einsum(
            "dc,cr->rd",
            part_up,
            lax.all_gather(up_grad, "dp", axis=0, tiled=True),
            preferred_element_type=jnp.float32,
        )
    ).astype(jnp.bfloat16)
    grads_back = lax.all_to_all(
        row_grads.reshape(experts * groups_dp, CAP, slice_width),
        ("expert", "dp"),
        split_axis=0,
        concat_axis=0,
        tiled=True,
    )
    grads_back = grads_back.reshape(experts, groups_dp, CAP, slice_width)
    input_grad = jnp.einsum(
        "ect,ejcd->tjd", placed_ones, grads_back, preferred_element_type=jnp.float32
    )
    input_grad = input_grad.astype(jnp.bfloat16).reshape(tok_rows, groups_dp * slice_width)
    chosen = jnp.any(selected == lax.axis_index("expert"))
    old_one = first_moment[0]
    old_two = second_moment[0]
    direction, moment_one, moment_two = adam_update(hidden, rows_dy, old_one, old_two)
    adam_step = jnp.where(chosen, direction, jnp.zeros_like(direction))
    new_one = jnp.where(chosen, moment_one, old_one)
    new_two = jnp.where(chosen, moment_two, old_two)
    return (mixed, input_grad, adam_step[None], new_one[None], new_two[None])


def solution(mesh):
    placed = (
        P(("groups", "expert", "dp"), None),
        P(("groups", "expert", "dp"), None),
        P(("groups", "expert", "dp"), None),
        P(("groups", "expert", "dp"), None),
        P("expert", "dp", None),
        P("expert", "dp", None),
        P("expert", None, "dp"),
        P(("groups", "expert"), None, "dp"),
        P(("groups", "expert"), None, "dp"),
        P("groups"),
    )
    return jax.shard_map(
        local,
        mesh=mesh,
        in_specs=placed,
        out_specs=(
            P(("groups", "expert", "dp"), None),
            P(("groups", "expert", "dp"), None),
            P(("groups", "expert"), None, "dp"),
            P(("groups", "expert"), None, "dp"),
            P(("groups", "expert"), None, "dp"),
        ),
        check_vma=False,
    )
```

profile of v0, /device:TPU:0, one launch (start us, length us, event | category | flops | bytes accessed | tf_op | source)
XLA Modules:
  0.0 163.5 jit_solution(8616928091480462692)
XLA Ops:
  7.2 0.0 copy-start
  7.2 0.0 copy-start.3
  7.2 0.0 reduce-scatter.5.cloned.1.call-start
  7.2 0.9 convert_reduce_fusion
  8.1 0.1 copy.51
  8.2 0.7 convert_reduce_fusion.1
  8.9 0.7 fusion.56
  9.6 0.7 select_reduce_fusion
  10.3 0.2 reduce_window_sum.11
  10.5 0.1 copy.53
  10.6 1.5 convolution_convert_fusion.1
  12.1 0.3 copy.56
  12.4 0.0 copy-done.3
  12.4 0.3 convolution_convert_fusion
  12.7 0.3 copy.57
  13.0 0.9 pad_maximum_fusion.1
  13.9 20.1 %all_to_all.15 = bf16[2,16,6,1024]{3,0,2,1:T(2,128)(2,1)S(1)} all-to-all(bf16[2,16,6,1024]{3,0,2,1:T(2,128)(2,1)S(1)} %pad_maximum_fusion.1), channel_id=1, replica_groups=mesh['groups'=2,'expert'=4,'dp'=4] {'expert','dp'}, dimensions={1} | all-to-all | bytes 786432 | tf_op jit(solution)/shard_map/all_to_all | solution.py:74
  34.0 1.6 %slice_reduce_fusion = (bf16[16,6,1024]{2,1,0:T(8,128)(2,1)S(1)}, bf16[16,6,1024]{2,1,0:T(8,128)(2,1)S(1)}) fusion(bf16[2,16,6,1024]{3,0,2,1:T(2,128)(2,1)S(1)} %all_to_all.15), kind=kLoop, calls=%fused_computation.38 | loop fusion | bytes 786432 | tf_op jit(solution)/shard_map/slice | solution.py:76
  35.6 0.1 reshape_squeeze.7
  35.7 0.0 copy-done
  35.7 1.5 fusion.28
  37.2 0.0 reduce-scatter.5.cloned.1.call-update
  37.2 0.0 reduce-scatter.3.cloned.1.call-start
  37.3 0.1 reshape_squeeze.6
  37.4 0.0 copy-start.1
  37.4 2.2 %fusion.25 = f32[1024,1,96]{0,2,1:T(8,128)S(1)} fusion(bf16[96,1024]{1,0:T(8,128)(2,1)S(1)} %reshape_squeeze.6, bf16[1,1024,1024]{2,1,0:T(8,128)(2,1)} %param.15), kind=kOutput, calls=%fused_computation.27 | convolution fusion | flops 201326592 | bytes 2686976 | tf_op jit(solution)/shard_map/dc,rd->cr/dot_general | solution.py:86
  39.6 0.0 copy-done.1
  39.6 0.0 copy-start.4
  39.6 0.5 fusion.19
  40.1 1.0 pad_maximum_fusion
  41.1 0.0 reduce-scatter.3.cloned.1.call-update
  41.1 0.0 copy-done.4
  41.1 0.6 compare_reduce_fusion
  41.7 15.0 %reduce-scatter.5.cloned.1.call-done = f32[256,96]{0,1:T(8,128)} async-done(((f32[1024,96]{0,1:T(8,128)}), f32[256,96]{0,1:T(8,128)}) %reduce-scatter.5.cloned.1.call-update) | async-done | bytes 98320 | tf_op jit(solution)/shard_map/reduce_scatter | solution.py:111
  56.7 24.6 %reduce-scatter.3.cloned.1.call-done = f32[256,2,96]{0,2,1:T(8,128)} async-done(((f32[1024,2,96]{0,2,1:T(8,128)}), f32[256,2,96]{0,2,1:T(8,128)}) %reduce-scatter.3.cloned.1.call-update) | async-done | bytes 196624 | tf_op jit(solution)/shard_map/reduce_scatter | solution.py:82
  81.3 1.0 multiply_convert_fusion.1
  82.3 13.9 %all_gather.9 = bf16[1024,96]{0,1:T(8,128)(2,1)S(1)} all-gather(bf16[256,96]{0,1:T(8,128)(2,1)S(1)} %get-tuple-element.27), channel_id=1, replica_groups=mesh['groups'=2,'expert'=4,'dp'=4] {'dp'}, dimensions={0}, use_global_device_ids=true | all-gather | bytes 245760 | tf_op jit(solution)/shard_map/all_gather | solution.py:95
  96.2 0.5 fusion.34
  96.7 0.8 reshape.58
  97.5 4.1 %all-to-all-start.1 = ((bf16[16,6,1024]{2,1,0:T(8,128)(2,1)}), bf16[16,6,1024]{2,1,0:T(8,128)(2,1)S(1)}, u32[]{:S(2)}, u32[]{:S(2)}) async-start(bf16[16,6,1024]{2,1,0:T(8,128)(2,1)} %reshape.58), calls=%async_computation.2 | async-start | bytes 524288 | tf_op jit(solution)/shard_map/all_to_all | solution.py:101
  101.6 0.0 copy-start.2
  101.6 17.4 %all_gather.11 = bf16[1024,96]{0,1:T(8,128)(2,1)S(1)} all-gather(bf16[256,96]{0,1:T(8,128)(2,1)S(1)} %get-tuple-element.26), channel_id=1, replica_groups=mesh['groups'=2,'expert'=4,'dp'=4] {'dp'}, dimensions={0}, use_global_device_ids=true | all-gather | bytes 245760 | tf_op jit(solution)/shard_map/all_gather | solution.py:135
  119.0 2.4 %fusion.11 = f32[96,1024]{1,0:T(8,128)S(1)} fusion(bf16[1024,96]{0,1:T(8,128)(2,1)S(1)} %all_gather.11, bf16[1,1024,1024]{2,1,0:T(8,128)(2,1)} %param.15), kind=kOutput, calls=%fused_computation.16 | convolution fusion | flops 201326592 | bytes 2686976 | tf_op jit(solution)/shard_map/dc,cr->rd/dot_general | solution.py:132
  121.4 13.6 %all_gather.10 = bf16[1024,96]{0,1:T(8,128)(2,1)S(1)} all-gather(bf16[256,96]{0,1:T(8,128)(2,1)S(1)} %get-tuple-element.25), channel_id=1, replica_groups=mesh['groups'=2,'expert'=4,'dp'=4] {'dp'}, dimensions={0}, use_global_device_ids=true | all-gather | bytes 245760 | tf_op jit(solution)/shard_map/all_gather | solution.py:127
  135.0 0.0 copy-done.2
  135.0 0.8 fusion.31
  135.8 0.8 reshape.61
  136.5 0.0 all-to-all-done.1
  136.5 3.9 %all-to-all-start.2 = ((bf16[16,6,1024]{2,1,0:T(8,128)(2,1)}), bf16[16,6,1024]{2,1,0:T(8,128)(2,1)S(1)}, u32[]{:S(2)}, u32[]{:S(2)}) async-start(bf16[16,6,1024]{2,1,0:T(8,128)(2,1)} %reshape.61), calls=%async_computation.4 | async-start | bytes 524288 | tf_op jit(solution)/shard_map/all_to_all | solution.py:139
  140.5 7.4 %fusion.5 = (bf16[1,1024,1024]{2,1,0:T(8,128)(2,1)}, bf16[1,1024,1024]{2,1,0:T(8,128)(2,1)}, bf16[1,1024,1024]{2,1,0:T(8,128)(2,1)}) fusion(bf16[1,1024,1024]{2,1,0:T(8,128)(2,1)} %param.18, pred[]{:T(512)} %compare_reduce_fusion, bf16[1,1024,1024]{2,1,0:T(8,128)(2,1)} %param.17, bf16[1024,96]{0,1:T(8,128)(2,1)S(1)} %all_gather.9, ...), kind=kOutput, calls=%fused_computation.8 | convolution fusion | flops 219152384 | bytes 10878977 | tf_op jit(solution)/shard_map/fr,rd->fd/dot_general | solution.py:34
  147.9 1.5 bitcast_convert_fusion.1
  149.3 1.6 copy.60
  150.9 1.3 copy.64
  152.3 0.0 all-to-all-done.2
  152.3 1.5 bitcast_convert_fusion
  153.7 1.6 copy.63
  155.4 1.3 copy.65
  (2 shorter events, 0.0 us)
Async XLA Ops:
  7.2 28.5 %copy-start = (bf16[1,1024,1024]{2,1,0:T(8,128)(2,1)S(1)}, bf16[1,1024,1024]{2,1,0:T(8,128)(2,1)}, u32[]{:S(2)}) copy-start(bf16[1,1024,1024]{2,1,0:T(8,128)(2,1)} %param.16) | copy-start | bytes 6291460
  7.2 5.2 %copy-start.3 = (bf16[128,4096]{1,0:T(8,128)(2,1)S(1)}, bf16[128,4096]{1,0:T(8,128)(2,1)}, u32[]{:S(2)}) copy-start(bf16[128,4096]{1,0:T(8,128)(2,1)} %param.13) | copy-start | bytes 3145732
  7.2 49.5 %reduce-scatter.5.cloned.1.call-start = ((), (), s32[]{:S(2)}) async-start(), calls=%async_computation.6 | async-start | bytes 491520 | tf_op jit(solution)/shard_map/reduce_scatter | solution.py:111
  37.2 44.0 %reduce-scatter.3.cloned.1.call-start = ((), (), s32[]{:S(2)}) async-start(), calls=%async_computation.5 | async-start | bytes 983040 | tf_op jit(solution)/shard_map/reduce_scatter | solution.py:82
  37.4 2.2 %copy-start.1 = (bf16[1,1024,1024]{2,1,0:T(8,128)(2,1)S(1)}, bf16[1,1024,1024]{2,1,0:T(8,128)(2,1)}, u32[]{:S(2)}) copy-start(bf16[1,1024,1024]{2,1,0:T(8,128)(2,1)} %param.14) | copy-start | bytes 6291460
  39.6 1.5 copy-start.4
  97.5 39.0 %all-to-all-start.1 = ((bf16[16,6,1024]{2,1,0:T(8,128)(2,1)}), bf16[16,6,1024]{2,1,0:T(8,128)(2,1)S(1)}, u32[]{:S(2)}, u32[]{:S(2)}) async-start(bf16[16,6,1024]{2,1,0:T(8,128)(2,1)} %reshape.58), calls=%async_computation.2 | async-start | bytes 524288 | tf_op jit(solution)/shard_map/all_to_all | solution.py:101
  101.6 33.3 %copy-start.2 = (bf16[1,1024,1024]{2,1,0:T(8,128)(2,1)S(1)}, bf16[1,1024,1024]{2,1,0:T(8,128)(2,1)}, u32[]{:S(2)}) copy-start(bf16[1,1024,1024]{2,1,0:T(8,128)(2,1)} %param.14) | copy-start | bytes 6291460
  136.5 15.7 %all-to-all-start.2 = ((bf16[16,6,1024]{2,1,0:T(8,128)(2,1)}), bf16[16,6,1024]{2,1,0:T(8,128)(2,1)S(1)}, u32[]{:S(2)}, u32[]{:S(2)}) async-start(bf16[16,6,1024]{2,1,0:T(8,128)(2,1)} %reshape.61), calls=%async_computation.4 | async-start | bytes 524288 | tf_op jit(solution)/shard_map/all_to_all | solution.py:139
Sparse Core Ops, SparseCore 0:
  37.4 19.2 reduce-scatter.4
  59.6 21.5 reduce-scatter.2
where the time goes:
time: 164 us
  blocking collectives  64.9 us (40%)
  waiting for transfers between devices  39.6 us (24%)
  matrix products  19.9 us (12%)
  between operations  14.2 us (9%)
  local copies, waits for them, and re-layouts  9.99 us (6%)
  starting transfers between devices  8.17 us (5%)
  other arithmetic  6.68 us (4%)
    reduce_scatter x1, waiting for transfers between devices, local(): lax.psum_scatter(jnp.stack([jnp.einsum('dc,rd->cr', part_gate, rows_x, pr...  24.6 us
    all_to_all x1, blocking collectives, local(): lax.all_to_all(packed, ('expert', 'dp'), split_axis=1, concat_axis=1, til...  20.1 us
    all_gather x1, blocking collectives, local(): lax.all_gather(up_grad, 'dp', axis=0, tiled=True)  17.4 us
    reduce_scatter x1, waiting for transfers between devices, local(): lax.psum_scatter(jnp.einsum('cd,rd->cr', w_down, rows_dy, preferred_eleme...  15 us
    all_gather x1, blocking collectives, local(): hidden = lax.all_gather(hidden_share, 'dp', axis=0, tiled=True)  13.9 us
    all_gather x1, blocking collectives, local(): lax.all_gather(gate_grad, 'dp', axis=0, tiled=True)  13.6 us
    dot_general x1, matrix products, adam_update(): jnp.einsum('fr,rd->fd', hidden, rows_dy, preferred_element_type=jnp.float32)  7.38 us
    all_to_all x1, starting transfers between devices, local(): lax.all_to_all(out_rows.reshape(experts * groups_dp, CAP, slice_width), (...  4.14 us
  transfers between devices with their start and end apart: 4, of which 2 were waited for; matrix products, arithmetic and copies ran while one was open for 12% of the time, Pallas kernels for 0%

commit v1 on v0

v1 whole, which is shorter than its diff:
```python
import functools

import jax
import jax.numpy as jnp
from jax import lax
from jax.experimental import pallas as pl
from jax.experimental.pallas import tpu as pltpu
from jax.sharding import PartitionSpec as P

CAP = 6
CHUNKS = 4
GROUP = 8
LINES = 2 * CHUNKS * CAP
HALF = CHUNKS * CAP

BETA_ONE = 0.9
BETA_TWO = 0.95
ADAM_EPS = 1e-08

F32 = jnp.float32
BF16 = jnp.bfloat16
VMEM = pl.BlockSpec(memory_space=pltpu.VMEM)
SMEM = pl.BlockSpec(memory_space=pltpu.SMEM)
MIB = 1 << 20


def iota(shape, dim):
    return lax.broadcasted_iota(jnp.int32, shape, dim)


def dot(a, b, contract=((1,), (0,))):
    return lax.dot_general(a, b, (contract, ((), ())), preferred_element_type=F32)


def shuffle(backward):
    size = GROUP * LINES
    a, b = iota((size, size), 0), iota((size, size), 1)
    if backward:
        a, b = b, a
    per = GROUP * CAP
    chunk, rest = a // (2 * per), a % (2 * per)
    half, rest = rest // per, rest % per
    source, slot = rest // CAP, rest % CAP
    return (b == source * LINES + half * HALF + chunk * CAP + slot).astype(F32).astype(BF16)


def dispatch_kernel(experts, dp, ids_ref, codes_ref, tok_ref, cot_ref, sent_ref, ones_ref, gates_ref):
    rows = tok_ref.shape[0]
    width = tok_ref.shape[1] // dp // CHUNKS
    codes = codes_ref[...].astype(F32)
    gates = (2.5 * codes / jnp.sum(codes, axis=0, keepdims=True)).astype(BF16).astype(F32)
    ids = ids_ref[...]
    matched = [ids == e for e in range(experts)]
    counts = jnp.concatenate(
        [jnp.sum(m.astype(F32), axis=0, keepdims=True) for m in matched], axis=0
    )
    gate_each = [jnp.sum(jnp.where(m, gates, 0.0), axis=0, keepdims=True) for m in matched]
    earlier = (iota((rows, rows), 0) < iota((rows, rows), 1)).astype(F32).astype(BF16)
    before = dot(counts.astype(BF16), earlier)
    slot8 = iota((8, rows), 0).astype(F32)
    line = iota((HALF, rows), 0)
    slot_of, chunk_of = (line % CAP).astype(F32), line // CAP
    x_rows, dy_rows = [], []
    for e in range(experts):
        taken = counts[e : e + 1] > 0
        at8 = taken & (before[e : e + 1] == slot8)
        ones_ref[e * 8 : e * 8 + 8, :] = at8.astype(F32)
        gates_ref[e * 8 : e * 8 + 8, :] = jnp.where(at8, gate_each[e], 0.0)
        at = taken & (before[e : e + 1] == slot_of)
        x_rows.append(
            jnp.concatenate([(at & (chunk_of == c)).astype(F32) for c in range(CHUNKS)], axis=1)
        )
        dy_rows.append(
            jnp.concatenate(
                [jnp.where(at & (chunk_of == c), gate_each[e], 0.0) for c in range(CHUNKS)], axis=1
            )
        )
    x_rows = jnp.concatenate(x_rows, axis=0).astype(BF16)
    dy_rows = jnp.concatenate(dy_rows, axis=0).astype(BF16)
    for j in range(dp):
        base = j * width * CHUNKS
        pieces = [slice(base + c * width, base + (c + 1) * width) for c in range(CHUNKS)]
        out_x = dot(x_rows, jnp.concatenate([tok_ref[:, p] for p in pieces], axis=0))
        out_dy = dot(dy_rows, jnp.concatenate([cot_ref[:, p] for p in pieces], axis=0))
        for e in range(experts):
            part = slice(e * HALF, (e + 1) * HALF)
            sent_ref[e * dp + j] = jnp.concatenate([out_x[part], out_dy[part]], axis=0).astype(BF16)


def partial_kernel(dp, arrived_ref, gate_w, up_w, down_w, own_ref, *refs):
    sent = refs[: dp - 1]
    rows_dy, rows_x, total = refs[dp - 1 :]
    me = lax.axis_index("dp")
    sources, _, width = arrived_ref.shape
    block = total.shape[2] // dp
    order = shuffle(False)
    per = GROUP * CAP
    for g in range(sources // GROUP):
        lines = jnp.concatenate(
            [arrived_ref[g * GROUP + i] for i in range(GROUP)], axis=0
        )
        sorted_lines = dot(order, lines).astype(BF16)
        for c in range(CHUNKS):
            for half, target in ((0, rows_x), (1, rows_dy)):
                start = (c * 2 + half) * per
                target[g * per : (g + 1) * per, c * width : (c + 1) * width] = sorted_lines[
                    start : start + per
                ]
    total[0] = dot(rows_x[...], gate_w[0])
    total[1] = dot(rows_x[...], up_w[0])
    total[2] = dot(rows_dy[...], down_w[0], ((1,), (1,)))
    for k in range(dp):
        at = pl.multiple_of(jnp.bitwise_xor(me, k) * block, block)
        part = total[:, :, pl.ds(at, block)]
        if k == 0:
            own_ref[...] = part
        else:
            sent[k - 1][...] = part.astype(BF16)


def hidden_kernel(own_ref, *refs):
    arrived, share_ref = refs[:-1], refs[-1]
    gate, up, grad = [
        sum([r[i].astype(F32) for r in arrived], own_ref[i]) for i in range(3)
    ]
    sig = jax.nn.sigmoid(gate)
    share_ref[0] = (gate * sig * up).astype(BF16)
    share_ref[1] = (grad * up * sig * (1.0 + gate * (1.0 - sig))).astype(BF16)
    share_ref[2] = (grad * gate * sig).astype(BF16)


def result_kernel(dp, share_ref, *refs):
    arrived = (share_ref,) + refs[: dp - 1]
    gate_w, up_w, down_w, sent_ref, hidden_ref, full = refs[dp - 1 :]
    me = lax.axis_index("dp")
    sources, _, width = sent_ref.shape
    block = share_ref.shape[2]
    for k in range(dp):
        at = pl.multiple_of(jnp.bitwise_xor(me, k) * block, block)
        hidden_ref[:, pl.ds(at, block)] = arrived[k][0]
        full[0, :, pl.ds(at, block)] = arrived[k][1]
        full[1, :, pl.ds(at, block)] = arrived[k][2]
    out = dot(hidden_ref[...], down_w[0]).astype(BF16)
    grad = (
        dot(full[0], gate_w[0], ((1,), (1,))) + dot(full[1], up_w[0], ((1,), (1,)))
    ).astype(BF16)
    order = shuffle(True)
    per = GROUP * CAP
    for g in range(sources // GROUP):
        lines = jnp.concatenate(
            [
                value[g * per : (g + 1) * per, c * width : (c + 1) * width]
                for c in range(CHUNKS)
                for value in (out, grad)
            ],
            axis=0,
        )
        sorted_lines = dot(order, lines).astype(BF16)
        for i in range(GROUP):
            sent_ref[g * GROUP + i] = sorted_lines[i * LINES : (i + 1) * LINES]


def adam_kernel(selected_ref, hidden_ref, dy_ref, first_ref, second_ref, step_ref, one_ref, two_ref):
    me = lax.axis_index("expert")
    chosen = selected_ref[0] == me
    for i in range(1, selected_ref.shape[0]):
        chosen = chosen | (selected_ref[i] == me)

    @pl.when(chosen)
    def _():
        grad = dot(hidden_ref[...], dy_ref[...], ((0,), (0,)))
        one = BETA_ONE * first_ref[0].astype(F32) + (1.0 - BETA_ONE) * grad
        two = BETA_TWO * second_ref[0].astype(F32) + (1.0 - BETA_TWO) * grad * grad
        step_ref[0] = (one / (jnp.sqrt(two) + ADAM_EPS)).astype(BF16)
        one_ref[0] = one.astype(BF16)
        two_ref[0] = two.astype(BF16)

    @pl.when(jnp.logical_not(chosen))
    def _():
        step_ref[...] = jnp.zeros_like(step_ref)
        one_ref[...] = first_ref[...]
        two_ref[...] = second_ref[...]


def combine_kernel(experts, dp, ones_ref, gates_ref, back_ref, mixed_ref, grad_ref):
    width = back_ref.shape[2]
    small = (experts * 8, experts * LINES)
    source, target = iota(small, 0), iota(small, 1)
    same = (source // 8 == target // LINES) & (source % 8 < CAP)
    within = target % LINES
    ones, gates = ones_ref[...].astype(BF16), gates_ref[...].astype(BF16)
    spreads = []
    for half, value in ((0, gates), (1, ones)):
        for c in range(CHUNKS):
            spot = same & (within == half * HALF + c * CAP + source % 8)
            spreads.append(dot(value, spot.astype(F32).astype(BF16), ((0,), (0,))).astype(BF16))
    for j in range(dp):
        lines = jnp.concatenate([back_ref[e * dp + j] for e in range(experts)], axis=0)
        for half, ref in ((0, mixed_ref), (1, grad_ref)):
            for c in range(CHUNKS):
                at = (j * CHUNKS + c) * width
                ref[:, at : at + width] = dot(spreads[half * CHUNKS + c], lines).astype(BF16)


def call(kernel, outs, operands, in_specs=None, scratch=(), limit=40, flops=0, traffic=0):
    return pl.pallas_call(
        kernel,
        out_shape=outs,
        in_specs=in_specs or [VMEM] * len(operands),
        out_specs=jax.tree.map(lambda _: VMEM, outs),
        scratch_shapes=scratch,
        compiler_params=pltpu.CompilerParams(vmem_limit_bytes=limit * MIB),
        cost_estimate=pl.CostEstimate(flops=flops, bytes_accessed=traffic, transcendentals=0),
    )(*operands)


def local(
    tokens,
    expert_ids,
    gate_codes,
    cotangent,
    gate_weight,
    up_weight,
    down_weight,
    first_moment,
    second_moment,
    selected,
):
    experts = lax.axis_size("expert")
    dp = lax.axis_size("dp")
    tok_rows, model = tokens.shape
    slice_width = model // dp
    width = slice_width // CHUNKS
    hidden_units = gate_weight.shape[2]
    block = hidden_units // dp
    sources = experts * dp
    slots = sources * CAP
    shape = jax.ShapeDtypeStruct
    cube = slots * slice_width * hidden_units

    sent, ones, gates = call(
        functools.partial(dispatch_kernel, experts, dp),
        (
            shape((sources, LINES, width), BF16),
            shape((experts * 8, tok_rows), F32),
            shape((experts * 8, tok_rows), F32),
        ),
        (expert_ids.T, gate_codes.T, tokens, cotangent),
        traffic=6 * MIB,
    )
    arrived = lax.all_to_all(sent, ("expert", "dp"), split_axis=0, concat_axis=0, tiled=True)

    def swap(value, k):
        return lax.ppermute(value, "dp", [(i, i ^ k) for i in range(dp)])

    own, *rest = call(
        functools.partial(partial_kernel, dp),
        (shape((3, slots, block), F32),)
        + (shape((3, slots, block), BF16),) * (dp - 1)
        + (shape((slots, slice_width), BF16),),
        (arrived, gate_weight, up_weight, down_weight),
        scratch=[
            pltpu.VMEM((slots, slice_width), BF16),
            pltpu.VMEM((3, slots, hidden_units), F32),
        ],
        flops=6 * cube,
        traffic=8 * MIB,
    )
    rows_dy = rest[-1]
    sums = [swap(rest[k - 1], k) for k in range(1, dp)]
    share = call(
        hidden_kernel, shape((3, slots, block), BF16), (own, *sums), traffic=2 * MIB
    )
    shares = [swap(share, k) for k in range(1, dp)]
    results, hidden = call(
        functools.partial(result_kernel, dp),
        (shape((sources, LINES, width), BF16), shape((slots, hidden_units), BF16)),
        (share, *shares, gate_weight, up_weight, down_weight),
        scratch=[pltpu.VMEM((2, slots, hidden_units), BF16)],
        flops=6 * cube,
        traffic=8 * MIB,
    )
    back = lax.all_to_all(results, ("expert", "dp"), split_axis=0, concat_axis=0, tiled=True)

    strip = hidden_units // 8
    moments = pl.BlockSpec((1, strip, slice_width), lambda i: (0, i, 0))
    adam = pl.pallas_call(
        adam_kernel,
        grid=(hidden_units // strip,),
        in_specs=[
            SMEM,
            pl.BlockSpec((slots, strip), lambda i: (0, i)),
            pl.BlockSpec((slots, slice_width), lambda i: (0, 0)),
            moments,
            moments,
        ],
        out_specs=(moments, moments, moments),
        out_shape=(shape(first_moment.shape, BF16),) * 3,
        compiler_params=pltpu.CompilerParams(vmem_limit_bytes=40 * MIB),
        cost_estimate=pl.CostEstimate(
            flops=2 * cube, bytes_accessed=10 * MIB, transcendentals=hidden_units * slice_width
        ),
    )(selected, hidden, rows_dy, first_moment, second_moment)

    mixed, input_grad = call(
        functools.partial(combine_kernel, experts, dp),
        (shape((tok_rows, model), BF16), shape((tok_rows, model), BF16)),
        (ones, gates, back),
        traffic=4 * MIB,
    )
    return (mixed, input_grad, *adam)


def solution(mesh):
    placed = (
        P(("groups", "expert", "dp"), None),
        P(("groups", "expert", "dp"), None),
        P(("groups", "expert", "dp"), None),
        P(("groups", "expert", "dp"), None),
        P("expert", "dp", None),
        P("expert", "dp", None),
        P("expert", None, "dp"),
        P(("groups", "expert"), None, "dp"),
        P(("groups", "expert"), None, "dp"),
        P("groups"),
    )
    return jax.shard_map(
        local,
        mesh=mesh,
        in_specs=placed,
        out_specs=(
            P(("groups", "expert", "dp"), None),
            P(("groups", "expert", "dp"), None),
            P(("groups", "expert"), None, "dp"),
            P(("groups", "expert"), None, "dp"),
            P(("groups", "expert"), None, "dp"),
        ),
        check_vma=False,
    )
```

time: 164 us -> 81.7 us (0.50)
  blocking collectives: 64.9 us -> 20.1 us
  matrix products: 19.9 us -> 0 us
  waiting for transfers between devices: 39.6 us -> 24.6 us
  Pallas kernels: 0 us -> 14.6 us
  between operations: 14.2 us -> 0.73 us
  other arithmetic: 6.68 us -> 0 us
  starting transfers between devices: 8.17 us -> 12.5 us
    all_gather x3 -> x0, blocking collectives: 44.9 us -> none  [the longest x1 17.4 us: local(): lax.all_gather(up_grad, 'dp', axis=0, tiled=True)]
    reduce_scatter x2 -> x0, waiting for transfers between devices: 39.6 us -> none  [the longest x1 24.6 us: local(): lax.psum_scatter(jnp.stack([jnp.einsum('dc,rd->cr', part_gate, rows_x, pr...]
    ppermute x0 -> x6, waiting for transfers between devices: none -> 20.1 us  [swap(): return lax.ppermute(value, 'dp', [(i, i ^ k) for i in range(dp)])]
    dot_general x11 -> x0, matrix products: 19.9 us -> none  [the longest x1 7.38 us: adam_update(): jnp.einsum('fr,rd->fd', hidden, rows_dy, preferred_element_type=jnp.float32)]
    pallas_call x0 -> x6, Pallas kernels: none -> 14.6 us  [the longest x5 7.81 us: call(): pl.pallas_call(kernel, out_shape=outs, in_specs=in_specs or [VMEM] * len(...]
    ppermute x0 -> x6, starting transfers between devices: none -> 8.9 us  [swap(): return lax.ppermute(value, 'dp', [(i, i ^ k) for i in range(dp)])]
    unnamed x12 -> x22, local copies, waits for them, and re-layouts: 2.66 us -> 8.75 us
    all_to_all x2 -> x1, waiting for transfers between devices: 0.01 us -> 4.45 us  [local(): lax.all_to_all(results, ('expert', 'dp'), split_axis=0, concat_axis=0, ti...]
  transfers between devices with their start and end apart: 4 -> 7, of which waited for: 2 -> 5; matrix products, arithmetic and copies ran while one was open for 12% -> 0% of each run, Pallas kernels for 0% -> 8%
where the time goes in v1:
time: 81.7 us; the launch traced here: 81.3 us
  waiting for transfers between devices  24.6 us (30%)
  blocking collectives  20.1 us (25%)
  Pallas kernels  14.6 us (18%)
  starting transfers between devices  12.5 us (15%)
  local copies, waits for them, and re-layouts  8.75 us (11%)
    ppermute x6, waiting for transfers between devices, swap(): return lax.ppermute(value, 'dp', [(i, i ^ k) for i in range(dp)])  20.1 us
    all_to_all x1, blocking collectives, local(): lax.all_to_all(sent, ('expert', 'dp'), split_axis=0, concat_axis=0, tiled...  20.1 us
    ppermute x6, starting transfers between devices, swap(): return lax.ppermute(value, 'dp', [(i, i ^ k) for i in range(dp)])  8.9 us
    unnamed x22, local copies, waits for them, and re-layouts  8.75 us
    pallas_call x5, Pallas kernels, call(): pl.pallas_call(kernel, out_shape=outs, in_specs=in_specs or [VMEM] * len(...  7.81 us
    pallas_call x1, Pallas kernels, local(): pl.pallas_call(adam_kernel, grid=(hidden_units // strip,), in_specs=[SMEM...  6.81 us
    all_to_all x1, waiting for transfers between devices, local(): lax.all_to_all(results, ('expert', 'dp'), split_axis=0, concat_axis=0, ti...  4.45 us
    all_to_all x1, starting transfers between devices, local(): lax.all_to_all(results, ('expert', 'dp'), split_axis=0, concat_axis=0, ti...  3.65 us
  transfers between devices with their start and end apart: 7, of which 5 were waited for; matrix products, arithmetic and copies ran while one was open for 0% of the time, Pallas kernels for 8%

profile of v1, /device:TPU:0, one launch (start us, length us, event | category | flops | bytes accessed | tf_op | source)
XLA Modules:
  0.0 81.3 jit_solution(5196936687721628819)
XLA Ops:
  0.6 0.0 copy-start
  0.6 0.0 copy-start.6
  0.7 1.4 %copy-done.6 = bf16[128,4096]{1,0:T(8,128)(2,1)S(1)} copy-done((bf16[128,4096]{1,0:T(8,128)(2,1)S(1)}, bf16[128,4096]{1,0:T(8,128)(2,1)}, u32[]{:S(2)}) %copy-start.6) | copy-done | bytes 1048600
  2.0 0.0 copy-start.7
  2.0 1.2 %copy-done.7 = bf16[128,4096]{1,0:T(8,128)(2,1)S(1)} copy-done((bf16[128,4096]{1,0:T(8,128)(2,1)S(1)}, bf16[128,4096]{1,0:T(8,128)(2,1)}, u32[]{:S(2)}) %copy-start.7) | copy-done | bytes 1048600
  3.2 0.0 copy-start.8
  3.2 0.7 copy-done.8
  3.9 0.0 copy-start.9
  3.9 0.7 copy-done.9
  4.6 0.6 shard_map.137
  5.2 20.1 %all_to_all.10.arrived_ref = bf16[16,48,256]{2,1,0:T(8,128)(2,1)S(1)} all-to-all(bf16[16,48,256]{2,1,0:T(8,128)(2,1)S(1)} %get-tuple-element.22), channel_id=1, replica_groups=mesh['groups'=2,'expert'=4,'dp'=4] {'expert','dp'}, dimensions={0} | all-to-all | bytes 786432 | tf_op jit(solution)/shard_map/all_to_all | solution.py:251
  25.3 0.0 copy-done
  25.3 0.0 copy-start.1
  25.3 1.6 %copy-done.1 = bf16[1,1024,1024]{2,1,0:T(8,128)(2,1)S(1)} copy-done((bf16[1,1024,1024]{2,1,0:T(8,128)(2,1)S(1)}, bf16[1,1024,1024]{2,1,0:T(8,128)(2,1)}, u32[]{:S(2)}) %copy-start.1) | copy-done | bytes 2097176
  26.9 0.0 copy-start.3
  26.9 1.6 %copy-done.3 = bf16[1,1024,1024]{2,1,0:T(8,128)(2,1)S(1)} copy-done((bf16[1,1024,1024]{2,1,0:T(8,128)(2,1)S(1)}, bf16[1,1024,1024]{2,1,0:T(8,128)(2,1)}, u32[]{:S(2)}) %copy-start.3) | copy-done | bytes 2097176
  28.5 0.0 copy-start.2
  28.5 2.2 %shard_map.138 = (f32[3,96,256]{2,1,0:T(8,128)S(1)}, bf16[3,96,256]{2,1,0:T(8,128)(2,1)S(1)}, bf16[3,96,256]{2,1,0:T(8,128)(2,1)S(1)}, bf16[3,96,256]{2,1,0:T(8,128)(2,1)S(1)}, bf16[96,1024]{1,0:T(8,128)(2,1)S(1)}) custom-call(bf16[16,48,256]{2,1,0:T(8,128)(2,1)S(1)} %all_to_all.10.arrived_ref, bf16[1,1024,1024]{2,1,0:T(8,128)(2,1)S(1)} %copy-done, ...), custom_call_target="tpu_custom_call" | custom-call | flops 603979776 | bytes 8388608 | tf_op jit(solution)/shard_map/pallas_call | solution.py:206
  30.6 0.1 collective-permute-start
  30.7 1.4 %collective-permute-start.1 = (bf16[3,96,256]{2,1,0:T(8,128)(2,1)S(1)}, bf16[3,96,256]{2,1,0:T(8,128)(2,1)S(1)}, u32[]{:S(2)}, u32[]{:S(2)}) collective-permute-start(bf16[3,96,256]{2,1,0:T(8,128)(2,1)S(1)} %get-tuple-element.25), channel_id=1, source_target_pairs={{0,2},{1,3},{2,0},{3,1},{4,6},{5,7},{6,4},{7,5},{8,10},{9,11},{10,... | collective-permute-start | bytes 442376 | tf_op jit(solution)/shard_map/ppermute | solution.py:254
  32.1 2.9 %collective-permute-start.2 = (bf16[3,96,256]{2,1,0:T(8,128)(2,1)S(1)}, bf16[3,96,256]{2,1,0:T(8,128)(2,1)S(1)}, u32[]{:S(2)}, u32[]{:S(2)}) collective-permute-start(bf16[3,96,256]{2,1,0:T(8,128)(2,1)S(1)} %get-tuple-element.26), channel_id=1, source_target_pairs={{0,3},{1,2},{2,1},{3,0},{4,7},{5,6},{6,5},{7,4},{8,11},{9,10},{10,... | collective-permute-start | bytes 442376 | tf_op jit(solution)/shard_map/ppermute | solution.py:254
  35.1 3.2 %collective-permute-done.refs_0_ = bf16[3,96,256]{2,1,0:T(8,128)(2,1)S(1)} collective-permute-done((bf16[3,96,256]{2,1,0:T(8,128)(2,1)S(1)}, bf16[3,96,256]{2,1,0:T(8,128)(2,1)S(1)}, u32[]{:S(2)}, u32[]{:S(2)}) %collective-permute-start) | collective-permute-done | bytes 147488 | tf_op jit(solution)/shard_map/ppermute | solution.py:254
  38.3 6.4 %collective-permute-done.1.refs_1_ = bf16[3,96,256]{2,1,0:T(8,128)(2,1)S(1)} collective-permute-done((bf16[3,96,256]{2,1,0:T(8,128)(2,1)S(1)}, bf16[3,96,256]{2,1,0:T(8,128)(2,1)S(1)}, u32[]{:S(2)}, u32[]{:S(2)}) %collective-permute-start.1) | collective-permute-done | bytes 147488 | tf_op jit(solution)/shard_map/ppermute | solution.py:254
  44.7 0.0 collective-permute-done.2.refs_2_
  44.7 0.1 shard_map.139.share_ref
  44.8 0.0 copy-start.10
  44.8 1.5 %collective-permute-start.5 = (bf16[3,96,256]{2,1,0:T(8,128)(2,1)S(1)}, bf16[3,96,256]{2,1,0:T(8,128)(2,1)S(1)}, u32[]{:S(2)}, u32[]{:S(2)}) collective-permute-start(bf16[3,96,256]{2,1,0:T(8,128)(2,1)S(1)} %shard_map.139.share_ref), channel_id=1, source_target_pairs={{0,3},{1,2},{2,1},{3,0},{4,7},{5,6},{6,5},{7,4},{8,11},{9,10},{10,... | collective-permute-start | bytes 442376 | tf_op jit(solution)/shard_map/ppermute | solution.py:254
  46.4 2.7 %collective-permute-start.4 = (bf16[3,96,256]{2,1,0:T(8,128)(2,1)S(1)}, bf16[3,96,256]{2,1,0:T(8,128)(2,1)S(1)}, u32[]{:S(2)}, u32[]{:S(2)}) collective-permute-start(bf16[3,96,256]{2,1,0:T(8,128)(2,1)S(1)} %shard_map.139.share_ref), channel_id=1, source_target_pairs={{0,2},{1,3},{2,0},{3,1},{4,6},{5,7},{6,4},{7,5},{8,10},{9,11},{10,... | collective-permute-start | bytes 442376 | tf_op jit(solution)/shard_map/ppermute | solution.py:254
  49.1 0.2 collective-permute-start.3
  49.3 4.3 %collective-permute-done.5.refs_2_ = bf16[3,96,256]{2,1,0:T(8,128)(2,1)S(1)} collective-permute-done((bf16[3,96,256]{2,1,0:T(8,128)(2,1)S(1)}, bf16[3,96,256]{2,1,0:T(8,128)(2,1)S(1)}, u32[]{:S(2)}, u32[]{:S(2)}) %collective-permute-start.5) | collective-permute-done | bytes 147488 | tf_op jit(solution)/shard_map/ppermute | solution.py:254
  53.6 6.2 %collective-permute-done.4.refs_1_ = bf16[3,96,256]{2,1,0:T(8,128)(2,1)S(1)} collective-permute-done((bf16[3,96,256]{2,1,0:T(8,128)(2,1)S(1)}, bf16[3,96,256]{2,1,0:T(8,128)(2,1)S(1)}, u32[]{:S(2)}, u32[]{:S(2)}) %collective-permute-start.4) | collective-permute-done | bytes 147488 | tf_op jit(solution)/shard_map/ppermute | solution.py:254
  59.8 0.0 collective-permute-done.3.refs_0_
  59.8 0.0 copy-done.2
  59.8 0.0 copy-start.4
  59.8 2.8 %shard_map.140 = (bf16[16,48,256]{2,1,0:T(8,128)(2,1)}, bf16[96,1024]{1,0:T(8,128)(2,1)S(1)}) custom-call(bf16[3,96,256]{2,1,0:T(8,128)(2,1)S(1)} %shard_map.139.share_ref, bf16[3,96,256]{2,1,0:T(8,128)(2,1)S(1)} %collective-permute-done.3.refs_0_, bf16[3,96,256]{2,1,0:T(8,128)(2,1)S(1)} %collective-permute-done.4.refs_1_, ...), custom_call_target="tpu_custom_call" | custom-call | flops 603979776 | bytes 8388608 | tf_op jit(solution)/shard_map/pallas_call | solution.py:206
  62.7 3.6 %all-to-all-start.1 = ((bf16[16,48,256]{2,1,0:T(8,128)(2,1)}), bf16[16,48,256]{2,1,0:T(8,128)(2,1)S(1)}, u32[]{:S(2)}, u32[]{:S(2)}) async-start(bf16[16,48,256]{2,1,0:T(8,128)(2,1)} %get-tuple-element.27), calls=%async_computation.1 | async-start | bytes 786432 | tf_op jit(solution)/shard_map/all_to_all | solution.py:283
  66.3 0.0 copy-done.10
  66.3 0.0 copy-done.4
  66.3 0.0 copy-start.5
  66.3 1.6 %copy-done.5 = bf16[1,1024,1024]{2,1,0:T(8,128)(2,1)S(1)} copy-done((bf16[1,1024,1024]{2,1,0:T(8,128)(2,1)S(1)}, bf16[1,1024,1024]{2,1,0:T(8,128)(2,1)}, u32[]{:S(2)}) %copy-start.5) | copy-done | bytes 2097176
  67.9 6.8 %shard_map.142 = (bf16[1,1024,1024]{2,1,0:T(8,128)(2,1)}, bf16[1,1024,1024]{2,1,0:T(8,128)(2,1)}, bf16[1,1024,1024]{2,1,0:T(8,128)(2,1)}) custom-call(s32[3]{0:T(128)S(1)} %copy-done.10, bf16[96,1024]{1,0:T(8,128)(2,1)S(1)} %get-tuple-element.30.hidden_ref, bf16[96,1024]{1,0:T(8,128)(2,1)S(1)} %get-tuple-element.31.dy_ref, ...), custom_call_target="tpu_custom_call" | custom-call | flops 201326592 | bytes 10485760 | tf_op jit(solution)/shard_map/pallas_call | solution.py:287
  74.7 4.4 %all-to-all-done.1.back_ref = bf16[16,48,256]{2,1,0:T(8,128)(2,1)S(1)} async-done(((bf16[16,48,256]{2,1,0:T(8,128)(2,1)}), bf16[16,48,256]{2,1,0:T(8,128)(2,1)S(1)}, u32[]{:S(2)}, u32[]{:S(2)}) %all-to-all-start.1) | async-done | bytes 393248 | tf_op jit(solution)/shard_map/all_to_all | solution.py:283
  79.2 2.1 %shard_map.141 = (bf16[128,4096]{1,0:T(8,128)(2,1)}, bf16[128,4096]{1,0:T(8,128)(2,1)}) custom-call(f32[32,128]{1,0:T(8,128)S(1)} %get-tuple-element.20.ones_ref, f32[32,128]{1,0:T(8,128)S(1)} %get-tuple-element.21.gates_ref, bf16[16,48,256]{2,1,0:T(8,128)(2,1)S(1)} %all-to-all-done.1.back_ref), custom_call_target="tpu_custom_call" | custom-call | bytes 4194304 | tf_op jit(solution)/shard_map/pallas_call | solution.py:206
Async XLA Ops:
  0.6 24.6 %copy-start = (bf16[1,1024,1024]{2,1,0:T(8,128)(2,1)S(1)}, bf16[1,1024,1024]{2,1,0:T(8,128)(2,1)}, u32[]{:S(2)}) copy-start(bf16[1,1024,1024]{2,1,0:T(8,128)(2,1)} %refs_3_.1) | copy-start | bytes 6291460
  0.6 1.4 %copy-start.6 = (bf16[128,4096]{1,0:T(8,128)(2,1)S(1)}, bf16[128,4096]{1,0:T(8,128)(2,1)}, u32[]{:S(2)}) copy-start(bf16[128,4096]{1,0:T(8,128)(2,1)} %tok_ref.1) | copy-start | bytes 3145732
  2.0 1.2 %copy-start.7 = (bf16[128,4096]{1,0:T(8,128)(2,1)S(1)}, bf16[128,4096]{1,0:T(8,128)(2,1)}, u32[]{:S(2)}) copy-start(bf16[128,4096]{1,0:T(8,128)(2,1)} %cot_ref.1) | copy-start | bytes 3145732
  3.2 0.7 copy-start.8
  3.9 0.7 copy-start.9
  25.3 1.6 %copy-start.1 = (bf16[1,1024,1024]{2,1,0:T(8,128)(2,1)S(1)}, bf16[1,1024,1024]{2,1,0:T(8,128)(2,1)}, u32[]{:S(2)}) copy-start(bf16[1,1024,1024]{2,1,0:T(8,128)(2,1)} %refs_4_.1) | copy-start | bytes 6291460
  26.9 1.6 %copy-start.3 = (bf16[1,1024,1024]{2,1,0:T(8,128)(2,1)S(1)}, bf16[1,1024,1024]{2,1,0:T(8,128)(2,1)}, u32[]{:S(2)}) copy-start(bf16[1,1024,1024]{2,1,0:T(8,128)(2,1)} %refs_5_.1) | copy-start | bytes 6291460
  28.5 31.4 %copy-start.2 = (bf16[1,1024,1024]{2,1,0:T(8,128)(2,1)S(1)}, bf16[1,1024,1024]{2,1,0:T(8,128)(2,1)}, u32[]{:S(2)}) copy-start(bf16[1,1024,1024]{2,1,0:T(8,128)(2,1)} %refs_4_.1) | copy-start | bytes 6291460
  30.6 7.7 %collective-permute-start = (bf16[3,96,256]{2,1,0:T(8,128)(2,1)S(1)}, bf16[3,96,256]{2,1,0:T(8,128)(2,1)S(1)}, u32[]{:S(2)}, u32[]{:S(2)}) collective-permute-start(bf16[3,96,256]{2,1,0:T(8,128)(2,1)S(1)} %get-tuple-element.24), channel_id=1, source_target_pairs={{0,1},{1,0},{2,3},{3,2},{4,5},{5,4},{6,7},{7,6},{8,9},{9,8},{10,11... | collective-permute-start | bytes 442376 | tf_op jit(solution)/shard_map/ppermute | solution.py:254
  30.7 14.0 %collective-permute-start.1 = (bf16[3,96,256]{2,1,0:T(8,128)(2,1)S(1)}, bf16[3,96,256]{2,1,0:T(8,128)(2,1)S(1)}, u32[]{:S(2)}, u32[]{:S(2)}) collective-permute-start(bf16[3,96,256]{2,1,0:T(8,128)(2,1)S(1)} %get-tuple-element.25), channel_id=1, source_target_pairs={{0,2},{1,3},{2,0},{3,1},{4,6},{5,7},{6,4},{7,5},{8,10},{9,11},{10,... | collective-permute-start | bytes 442376 | tf_op jit(solution)/shard_map/ppermute | solution.py:254
  32.1 12.6 %collective-permute-start.2 = (bf16[3,96,256]{2,1,0:T(8,128)(2,1)S(1)}, bf16[3,96,256]{2,1,0:T(8,128)(2,1)S(1)}, u32[]{:S(2)}, u32[]{:S(2)}) collective-permute-start(bf16[3,96,256]{2,1,0:T(8,128)(2,1)S(1)} %get-tuple-element.26), channel_id=1, source_target_pairs={{0,3},{1,2},{2,1},{3,0},{4,7},{5,6},{6,5},{7,4},{8,11},{9,10},{10,... | collective-permute-start | bytes 442376 | tf_op jit(solution)/shard_map/ppermute | solution.py:254
  44.8 21.5 %copy-start.10 = (s32[3]{0:T(128)S(1)}, s32[3]{0:T(128)}, u32[]{:S(2)}) copy-start(s32[3]{0:T(128)} %selected_ref.1) | copy-start | bytes 40
  44.8 8.7 %collective-permute-start.5 = (bf16[3,96,256]{2,1,0:T(8,128)(2,1)S(1)}, bf16[3,96,256]{2,1,0:T(8,128)(2,1)S(1)}, u32[]{:S(2)}, u32[]{:S(2)}) collective-permute-start(bf16[3,96,256]{2,1,0:T(8,128)(2,1)S(1)} %shard_map.139.share_ref), channel_id=1, source_target_pairs={{0,3},{1,2},{2,1},{3,0},{4,7},{5,6},{6,5},{7,4},{8,11},{9,10},{10,... | collective-permute-start | bytes 442376 | tf_op jit(solution)/shard_map/ppermute | solution.py:254
  46.4 13.4 %collective-permute-start.4 = (bf16[3,96,256]{2,1,0:T(8,128)(2,1)S(1)}, bf16[3,96,256]{2,1,0:T(8,128)(2,1)S(1)}, u32[]{:S(2)}, u32[]{:S(2)}) collective-permute-start(bf16[3,96,256]{2,1,0:T(8,128)(2,1)S(1)} %shard_map.139.share_ref), channel_id=1, source_target_pairs={{0,2},{1,3},{2,0},{3,1},{4,6},{5,7},{6,4},{7,5},{8,10},{9,11},{10,... | collective-permute-start | bytes 442376 | tf_op jit(solution)/shard_map/ppermute | solution.py:254
  49.1 10.7 %collective-permute-start.3 = (bf16[3,96,256]{2,1,0:T(8,128)(2,1)S(1)}, bf16[3,96,256]{2,1,0:T(8,128)(2,1)S(1)}, u32[]{:S(2)}, u32[]{:S(2)}) collective-permute-start(bf16[3,96,256]{2,1,0:T(8,128)(2,1)S(1)} %shard_map.139.share_ref), channel_id=1, source_target_pairs={{0,1},{1,0},{2,3},{3,2},{4,5},{5,4},{6,7},{7,6},{8,9},{9,8},{10,11... | collective-permute-start | bytes 442376 | tf_op jit(solution)/shard_map/ppermute | solution.py:254
  59.8 6.5 %copy-start.4 = (bf16[1,1024,1024]{2,1,0:T(8,128)(2,1)S(1)}, bf16[1,1024,1024]{2,1,0:T(8,128)(2,1)}, u32[]{:S(2)}) copy-start(bf16[1,1024,1024]{2,1,0:T(8,128)(2,1)} %first_ref.1) | copy-start | bytes 6291460
  62.7 16.5 %all-to-all-start.1 = ((bf16[16,48,256]{2,1,0:T(8,128)(2,1)}), bf16[16,48,256]{2,1,0:T(8,128)(2,1)S(1)}, u32[]{:S(2)}, u32[]{:S(2)}) async-start(bf16[16,48,256]{2,1,0:T(8,128)(2,1)} %get-tuple-element.27), calls=%async_computation.1 | async-start | bytes 786432 | tf_op jit(solution)/shard_map/all_to_all | solution.py:283
  66.3 1.6 %copy-start.5 = (bf16[1,1024,1024]{2,1,0:T(8,128)(2,1)S(1)}, bf16[1,1024,1024]{2,1,0:T(8,128)(2,1)}, u32[]{:S(2)}) copy-start(bf16[1,1024,1024]{2,1,0:T(8,128)(2,1)} %second_ref.1) | copy-start | bytes 6291460

commit v2 on v1

v2 whole, which is shorter than its diff:
```python
import functools

import jax
import jax.numpy as jnp
from jax import lax
from jax.experimental import pallas as pl
from jax.experimental.pallas import tpu as pltpu
from jax.sharding import PartitionSpec as P

CAP = 6
CHUNKS = 4
GROUP = 8
LINES = 2 * CHUNKS * CAP
HALF = CHUNKS * CAP

BETA_ONE = 0.9
BETA_TWO = 0.95
ADAM_EPS = 1e-08

F32 = jnp.float32
BF16 = jnp.bfloat16
VMEM = pl.BlockSpec(memory_space=pltpu.VMEM)
SMEM = pl.BlockSpec(memory_space=pltpu.SMEM)
MIB = 1 << 20
MOST = 60


def iota(shape, dim):
    return lax.broadcasted_iota(jnp.int32, shape, dim)


def dot(a, b, contract=((1,), (0,))):
    return lax.dot_general(a, b, (contract, ((), ())), preferred_element_type=F32)


def onehot(vector, size, dim):
    return (iota(size, dim) == vector).astype(F32).astype(BF16)


def gather_rows(arrived_ref, targets):
    sources, _, width = arrived_ref.shape
    per, size = GROUP * CAP, GROUP * LINES
    line = iota((1, size), 1)
    source, rest = line // LINES, line % LINES
    order = onehot(rest // CAP * per + source * CAP + rest % CAP, (size, size), 0)
    for g in range(sources // GROUP):
        lines = jnp.concatenate([arrived_ref[g * GROUP + i] for i in range(GROUP)], axis=0)
        sorted_lines = dot(order, lines).astype(BF16)
        for half, target in enumerate(targets):
            for c in range(CHUNKS):
                start = (half * CHUNKS + c) * per
                target[g * per : (g + 1) * per, c * width : (c + 1) * width] = sorted_lines[
                    start : start + per
                ]


def scatter_rows(values, sent_ref):
    sources, _, width = sent_ref.shape
    per, size = GROUP * CAP, GROUP * LINES
    row = iota((1, size), 1)
    part, rest = row // per, row % per
    order = onehot(rest // CAP * LINES + part * CAP + rest % CAP, (size, size), 0)
    for g in range(sources // GROUP):
        lines = jnp.concatenate(
            [
                value[g * per : (g + 1) * per, c * width : (c + 1) * width]
                for value in values
                for c in range(CHUNKS)
            ],
            axis=0,
        )
        sorted_lines = dot(order, lines).astype(BF16)
        for i in range(GROUP):
            sent_ref[g * GROUP + i] = sorted_lines[i * LINES : (i + 1) * LINES]


def dispatch_kernel(
    experts, dp, ids_hbm, codes_hbm, tok_hbm, cot_hbm, sent_ref, ones_ref, gates_ref,
    ids_ref, codes_ref, tok_ref, cot_ref, sems,
):
    copies = [
        pltpu.make_async_copy(a, b, sems.at[i])
        for i, (a, b) in enumerate(
            (
                (ids_hbm, ids_ref),
                (codes_hbm, codes_ref),
                (tok_hbm, tok_ref),
                (cot_hbm, cot_ref),
            )
        )
    ]
    for c in copies:
        c.start()
    rows = tok_ref.shape[0]
    width = tok_ref.shape[1] // dp // CHUNKS
    earlier = (iota((rows, rows), 0) < iota((rows, rows), 1)).astype(F32).astype(BF16)
    copies[0].wait()
    copies[1].wait()
    codes = codes_ref[...].astype(F32)
    gates = (2.5 * codes / jnp.sum(codes, axis=0, keepdims=True)).astype(BF16).astype(F32)
    ids = ids_ref[...]
    matched = [ids == e for e in range(experts)]
    counts = jnp.concatenate(
        [jnp.sum(m.astype(F32), axis=0, keepdims=True) for m in matched], axis=0
    )
    gate_each = [jnp.sum(jnp.where(m, gates, 0.0), axis=0, keepdims=True) for m in matched]
    before = dot(counts.astype(BF16), earlier)
    slot8 = iota((8, rows), 0).astype(F32)
    line = iota((HALF, rows), 0)
    slot_of, chunk_of = (line % CAP).astype(F32), line // CAP
    x_rows, dy_rows = [], []
    for e in range(experts):
        taken = counts[e : e + 1] > 0
        at8 = taken & (before[e : e + 1] == slot8)
        ones_ref[e * 8 : e * 8 + 8, :] = at8.astype(F32)
        gates_ref[e * 8 : e * 8 + 8, :] = jnp.where(at8, gate_each[e], 0.0)
        at = taken & (before[e : e + 1] == slot_of)
        x_rows.append(
            jnp.concatenate([(at & (chunk_of == c)).astype(F32) for c in range(CHUNKS)], axis=1)
        )
        dy_rows.append(
            jnp.concatenate(
                [jnp.where(at & (chunk_of == c), gate_each[e], 0.0) for c in range(CHUNKS)], axis=1
            )
        )
    x_rows = jnp.concatenate(x_rows, axis=0).astype(BF16)
    dy_rows = jnp.concatenate(dy_rows, axis=0).astype(BF16)
    for copy, source_ref, weights, half in (
        (copies[2], tok_ref, x_rows, 0),
        (copies[3], cot_ref, dy_rows, HALF),
    ):
        copy.wait()
        for j in range(dp):
            base = j * width * CHUNKS
            lines = jnp.concatenate(
                [
                    source_ref[:, base + c * width : base + (c + 1) * width]
                    for c in range(CHUNKS)
                ],
                axis=0,
            )
            out = dot(weights, lines)
            for e in range(experts):
                sent_ref[e * dp + j, half : half + HALF] = out[
                    e * HALF : (e + 1) * HALF
                ].astype(BF16)


def backward_kernel(arrived_ref, down_w, rows_x, rows_dy, total):
    gather_rows(arrived_ref, (rows_x, rows_dy))
    total[...] = dot(rows_dy[...], down_w[0], ((1,), (1,)))


def forward_kernel(dp, rows_x, grad_ref, gate_w, up_w, own_ref, *refs):
    sent, (total,) = refs[: dp - 1], refs[dp - 1 :]
    total[0] = dot(rows_x[...], gate_w[0])
    total[1] = dot(rows_x[...], up_w[0])
    me = lax.axis_index("dp")
    block = total.shape[2] // dp
    for k in range(dp):
        at = pl.ds(pl.multiple_of(jnp.bitwise_xor(me, k) * block, block), block)
        target = own_ref if k == 0 else sent[k - 1]
        target[:2] = total[:, :, at].astype(target.dtype)
        target[2] = grad_ref[:, at].astype(target.dtype)


def summed(refs, i):
    return sum([r[i].astype(F32) for r in refs[1:]], refs[0][i])


def share_kernel(*refs):
    sums, share_ref = refs[:-1], refs[-1]
    gate, up, grad = [summed(sums, i) for i in range(3)]
    sig = jax.nn.sigmoid(gate)
    share_ref[0] = (gate * sig * up).astype(BF16)
    share_ref[1] = (grad * up * sig * (1.0 + gate * (1.0 - sig))).astype(BF16)
    share_ref[2] = (grad * gate * sig).astype(BF16)


def result_kernel(dp, *refs):
    arrived = refs[:dp]
    gate_w, up_w, down_w, sent_ref, hidden_ref, full = refs[dp:]
    me = lax.axis_index("dp")
    block = arrived[0].shape[2]
    for k in range(dp):
        at = pl.multiple_of(jnp.bitwise_xor(me, k) * block, block)
        hidden_ref[:, pl.ds(at, block)] = arrived[k][0]
        full[:, :, pl.ds(at, block)] = arrived[k][1:]
    out = dot(hidden_ref[...], down_w[0])
    grad = dot(full[0], gate_w[0], ((1,), (1,))) + dot(full[1], up_w[0], ((1,), (1,)))
    scatter_rows((out.astype(BF16), grad.astype(BF16)), sent_ref)


def adam_kernel(selected_ref, hidden_ref, dy_ref, first_ref, second_ref, step_ref, one_ref, two_ref):
    me = lax.axis_index("expert")
    chosen = selected_ref[0] == me
    for i in range(1, selected_ref.shape[0]):
        chosen = chosen | (selected_ref[i] == me)

    @pl.when(chosen)
    def _():
        grad = dot(hidden_ref[...], dy_ref[...], ((0,), (0,)))
        one = BETA_ONE * first_ref[0].astype(F32) + (1.0 - BETA_ONE) * grad
        two = BETA_TWO * second_ref[0].astype(F32) + (1.0 - BETA_TWO) * grad * grad
        step_ref[0] = (one / (jnp.sqrt(two) + ADAM_EPS)).astype(BF16)
        one_ref[0] = one.astype(BF16)
        two_ref[0] = two.astype(BF16)

    @pl.when(jnp.logical_not(chosen))
    def _():
        step_ref[...] = jnp.zeros_like(step_ref)
        one_ref[...] = first_ref[...]
        two_ref[...] = second_ref[...]


def combine_kernel(
    experts, dp, ones_ref, gates_ref, back_ref, mixed_hbm, grad_hbm, mixed_ref, grad_ref, sems
):
    _, lines_each, width = back_ref.shape
    small = (experts * 8, experts * lines_each)
    source, target = iota(small, 0), iota(small, 1)
    same = (source // 8 == target // lines_each) & (source % 8 < CAP)
    within = target % lines_each
    spreads = []
    for half, ref in ((0, gates_ref), (1, ones_ref)):
        weights = ref[...].astype(BF16)
        for c in range(CHUNKS):
            spot = same & (within == half * HALF + c * CAP + source % 8)
            spreads.append(dot(weights, spot.astype(F32).astype(BF16), ((0,), (0,))).astype(BF16))
    copies = []
    for j in range(dp):
        lines = jnp.concatenate([back_ref[e * dp + j] for e in range(experts)], axis=0)
        for half, ref, hbm in ((0, mixed_ref, mixed_hbm), (1, grad_ref, grad_hbm)):
            for c in range(CHUNKS):
                at = (j * CHUNKS + c) * width
                ref[:, at : at + width] = dot(spreads[half * CHUNKS + c], lines).astype(BF16)
            span = pl.ds(j * CHUNKS * width, CHUNKS * width)
            copies.append(
                pltpu.make_async_copy(
                    ref.at[:, span], hbm.at[:, span], sems.at[half, j]
                )
            )
            copies[-1].start()
    for c in copies:
        c.wait()


def call(kernel, outs, operands, in_specs=None, out_specs=None, scratch=(), limit=24, flops=0, traffic=0):
    return pl.pallas_call(
        kernel,
        out_shape=outs,
        in_specs=in_specs or [VMEM] * len(operands),
        out_specs=out_specs or jax.tree.map(lambda _: VMEM, outs),
        scratch_shapes=scratch,
        compiler_params=pltpu.CompilerParams(vmem_limit_bytes=limit * MIB),
        cost_estimate=pl.CostEstimate(flops=flops, bytes_accessed=traffic, transcendentals=0),
    )(*operands)


def local(
    tokens,
    expert_ids,
    gate_codes,
    cotangent,
    gate_weight,
    up_weight,
    down_weight,
    first_moment,
    second_moment,
    selected,
):
    experts = lax.axis_size("expert")
    dp = lax.axis_size("dp")
    tok_rows, model = tokens.shape
    slice_width = model // dp
    width = slice_width // CHUNKS
    hidden_units = gate_weight.shape[2]
    block = hidden_units // dp
    sources = experts * dp
    slots = sources * CAP
    shape = jax.ShapeDtypeStruct
    cube = slots * slice_width * hidden_units
    own_specs = [pl.BlockSpec(memory_space=pltpu.HBM)] * 4

    sent, ones, gates = call(
        functools.partial(dispatch_kernel, experts, dp),
        (
            shape((sources, LINES, width), BF16),
            shape((experts * 8, tok_rows), F32),
            shape((experts * 8, tok_rows), F32),
        ),
        (expert_ids.T, gate_codes.T, tokens, cotangent),
        in_specs=own_specs,
        limit=MOST,
        scratch=[
            pltpu.VMEM(expert_ids.shape[::-1], jnp.int32),
            pltpu.VMEM(gate_codes.shape[::-1], jnp.int32),
            pltpu.VMEM(tokens.shape, BF16),
            pltpu.VMEM(cotangent.shape, BF16),
            pltpu.SemaphoreType.DMA((4,)),
        ],
        traffic=6 * MIB,
    )
    arrived = lax.all_to_all(sent, ("expert", "dp"), split_axis=0, concat_axis=0, tiled=True)
    def swap(value, k):
        return lax.ppermute(value, "dp", [(i, i ^ k) for i in range(dp)])

    def swaps(values):
        return [swap(values[k - 1], k) for k in range(1, dp)]

    weights = (gate_weight, up_weight, down_weight)

    rows_x, rows_dy, grad_parts = call(
        backward_kernel,
        (
            shape((slots, slice_width), BF16),
            shape((slots, slice_width), BF16),
            shape((slots, hidden_units), F32),
        ),
        (arrived, down_weight),
        flops=2 * cube,
        traffic=3 * MIB,
    )
    own, *parts = call(
        functools.partial(forward_kernel, dp),
        (shape((3, slots, block), F32),) + (shape((3, slots, block), BF16),) * (dp - 1),
        (rows_x, grad_parts, gate_weight, up_weight),
        scratch=[pltpu.VMEM((2, slots, hidden_units), F32)],
        flops=4 * cube,
        traffic=6 * MIB,
    )
    sums = [own, *swaps(parts)]
    share = call(
        share_kernel,
        shape((3, slots, block), BF16),
        sums,
        traffic=MIB,
    )
    shares = swaps([share] * (dp - 1))
    results, hidden = call(
        functools.partial(result_kernel, dp),
        (shape((sources, LINES, width), BF16), shape((slots, hidden_units), BF16)),
        (share, *shares, *weights),
        scratch=[pltpu.VMEM((2, slots, hidden_units), BF16)],
        flops=6 * cube,
        traffic=8 * MIB,
    )
    back = lax.all_to_all(results, ("expert", "dp"), split_axis=0, concat_axis=0, tiled=True)

    strip = hidden_units // 8
    moments = pl.BlockSpec((1, strip, slice_width), lambda i: (0, i, 0))
    adam = pl.pallas_call(
        adam_kernel,
        grid=(hidden_units // strip,),
        in_specs=[
            SMEM,
            pl.BlockSpec((slots, strip), lambda i: (0, i)),
            pl.BlockSpec((slots, slice_width), lambda i: (0, 0)),
            moments,
            moments,
        ],
        out_specs=(moments, moments, moments),
        out_shape=(shape(first_moment.shape, BF16),) * 3,
        compiler_params=pltpu.CompilerParams(vmem_limit_bytes=32 * MIB),
        cost_estimate=pl.CostEstimate(
            flops=2 * cube, bytes_accessed=10 * MIB, transcendentals=hidden_units * slice_width
        ),
    )(selected, hidden, rows_dy, first_moment, second_moment)

    mixed, input_grad = call(
        functools.partial(combine_kernel, experts, dp),
        (shape((tok_rows, model), BF16), shape((tok_rows, model), BF16)),
        (ones, gates, back),
        out_specs=(own_specs[0],) * 2,
        scratch=[
            pltpu.VMEM((tok_rows, model), BF16),
            pltpu.VMEM((tok_rows, model), BF16),
            pltpu.SemaphoreType.DMA((2, dp)),
        ],
        traffic=4 * MIB,
    )
    return (mixed, input_grad, *adam)


def solution(mesh):
    placed = (
        P(("groups", "expert", "dp"), None),
        P(("groups", "expert", "dp"), None),
        P(("groups", "expert", "dp"), None),
        P(("groups", "expert", "dp"), None),
        P("expert", "dp", None),
        P("expert", "dp", None),
        P("expert", None, "dp"),
        P(("groups", "expert"), None, "dp"),
        P(("groups", "expert"), None, "dp"),
        P("groups"),
    )
    return jax.shard_map(
        local,
        mesh=mesh,
        in_specs=placed,
        out_specs=(
            P(("groups", "expert", "dp"), None),
            P(("groups", "expert", "dp"), None),
            P(("groups", "expert"), None, "dp"),
            P(("groups", "expert"), None, "dp"),
            P(("groups", "expert"), None, "dp"),
        ),
        check_vma=False,
    )
```

time: 81.7 us -> 78.1 us (0.956)
  local copies, waits for them, and re-layouts: 8.75 us -> 4.8 us
  waiting for transfers between devices: 24.6 us -> 23 us
  Pallas kernels: 14.6 us -> 16.2 us
    unnamed x22 -> x18, local copies, waits for them, and re-layouts: 8.75 us -> 4.8 us
    all_to_all x1, waiting for transfers between devices: 4.45 us -> 2.87 us  [local(): lax.all_to_all(results, ('expert', 'dp'), split_axis=0, concat_axis=0, ti...]
    pallas_call x5 -> x6, Pallas kernels: 7.81 us -> 9.37 us  [call(): pl.pallas_call(kernel, out_shape=outs, in_specs=in_specs or [VMEM] * len(...]
  transfers between devices with their start and end apart: 7 -> 7, of which waited for: 5 -> 5; matrix products, arithmetic and copies ran while one was open for 0% -> 0% of each run, Pallas kernels for 8% -> 9%
where the time goes in v2:
time: 78.1 us; the launch traced here: 77.7 us
  waiting for transfers between devices  23 us (29%)
  blocking collectives  20.4 us (26%)
  Pallas kernels  16.2 us (21%)
  starting transfers between devices  12.5 us (16%)
  local copies, waits for them, and re-layouts  4.8 us (6%)
    all_to_all x1, blocking collectives, local(): lax.all_to_all(sent, ('expert', 'dp'), split_axis=0, concat_axis=0, tiled...  20.4 us
    ppermute x6, waiting for transfers between devices, swap(): return lax.ppermute(value, 'dp', [(i, i ^ k) for i in range(dp)])  20.1 us
    pallas_call x6, Pallas kernels, call(): pl.pallas_call(kernel, out_shape=outs, in_specs=in_specs or [VMEM] * len(...  9.37 us
    ppermute x6, starting transfers between devices, swap(): return lax.ppermute(value, 'dp', [(i, i ^ k) for i in range(dp)])  8.9 us
    pallas_call x1, Pallas kernels, local(): pl.pallas_call(adam_kernel, grid=(hidden_units // strip,), in_specs=[SMEM...  6.81 us
    unnamed x18, local copies, waits for them, and re-layouts  4.8 us
    all_to_all x1, starting transfers between devices, local(): lax.all_to_all(results, ('expert', 'dp'), split_axis=0, concat_axis=0, ti...  3.65 us
    all_to_all x1, waiting for transfers between devices, local(): lax.all_to_all(results, ('expert', 'dp'), split_axis=0, concat_axis=0, ti...  2.87 us
  transfers between devices with their start and end apart: 7, of which 5 were waited for; matrix products, arithmetic and copies ran while one was open for 0% of the time, Pallas kernels for 9%

profile of v2, /device:TPU:0, one launch (start us, length us, event | category | flops | bytes accessed | tf_op | source)
XLA Modules:
  0.0 77.7 jit_solution(17859969969689029418)
XLA Ops:
  0.6 0.0 copy-start.1
  0.6 2.8 %shard_map.137 = (bf16[16,48,256]{2,1,0:T(8,128)(2,1)}, f32[32,128]{1,0:T(8,128)}, f32[32,128]{1,0:T(8,128)}) custom-call(s32[8,128]{1,0:T(8,128)} %bitcast.2, s32[8,128]{1,0:T(8,128)} %bitcast.3, bf16[128,4096]{1,0:T(8,128)(2,1)} %tok_hbm.1, bf16[128,4096]{1,0:T(8,128)(2,1)} %cot_hbm.1), custom_call_target="tpu_custom_call" | custom-call | bytes 6291456 | tf_op jit(solution)/shard_map/pallas_call | solution.py:249
  3.5 0.0 copy-start
  3.5 20.4 %all_to_all.10.arrived_ref = bf16[16,48,256]{2,1,0:T(8,128)(2,1)S(1)} all-to-all(bf16[16,48,256]{2,1,0:T(8,128)(2,1)} %get-tuple-element.24), channel_id=1, replica_groups=mesh['groups'=2,'expert'=4,'dp'=4] {'expert','dp'}, dimensions={0} | all-to-all | bytes 786432 | tf_op jit(solution)/shard_map/all_to_all | solution.py:304
  23.9 0.0 copy-start.2
  23.9 1.6 %copy-done.2 = bf16[1,1024,1024]{2,1,0:T(8,128)(2,1)S(1)} copy-done((bf16[1,1024,1024]{2,1,0:T(8,128)(2,1)S(1)}, bf16[1,1024,1024]{2,1,0:T(8,128)(2,1)}, u32[]{:S(2)}) %copy-start.2) | copy-done | bytes 2097176
  25.5 1.0 %shard_map.138 = (bf16[96,1024]{1,0:T(8,128)(2,1)S(1)}, bf16[96,1024]{1,0:T(8,128)(2,1)S(1)}, f32[96,1024]{1,0:T(8,128)S(1)}) custom-call(bf16[16,48,256]{2,1,0:T(8,128)(2,1)S(1)} %all_to_all.10.arrived_ref, bf16[1,1024,1024]{2,1,0:T(8,128)(2,1)S(1)} %copy-done.2), custom_call_target="tpu_custom_call" | custom-call | flops 201326592 | bytes 3145728 | tf_op jit(solution)/shard_map/pallas_call | solution.py:249
  26.5 0.0 copy-done.1
  26.5 0.0 copy-done
  26.5 0.0 copy-start.3
  26.5 0.9 %shard_map.139 = (f32[3,96,256]{2,1,0:T(8,128)S(1)}, bf16[3,96,256]{2,1,0:T(8,128)(2,1)S(1)}, bf16[3,96,256]{2,1,0:T(8,128)(2,1)S(1)}, bf16[3,96,256]{2,1,0:T(8,128)(2,1)S(1)}) custom-call(bf16[96,1024]{1,0:T(8,128)(2,1)S(1)} %get-tuple-element.25.rows_x, f32[96,1024]{1,0:T(8,128)S(1)} %get-tuple-element.26.grad_ref, bf16[1,1024,1024]{2,1,0:T(8,128)(2,1)S(1)} %copy-done, ...), custom_call_target="tpu_custom_call" | custom-call | flops 402653184 | bytes 6291456 | tf_op jit(solution)/shard_map/pallas_call | solution.py:249
  27.5 0.1 collective-permute-start
  27.5 1.4 %collective-permute-start.1 = (bf16[3,96,256]{2,1,0:T(8,128)(2,1)S(1)}, bf16[3,96,256]{2,1,0:T(8,128)(2,1)S(1)}, u32[]{:S(2)}, u32[]{:S(2)}) collective-permute-start(bf16[3,96,256]{2,1,0:T(8,128)(2,1)S(1)} %get-tuple-element.29), channel_id=1, source_target_pairs={{0,2},{1,3},{2,0},{3,1},{4,6},{5,7},{6,4},{7,5},{8,10},{9,11},{10,... | collective-permute-start | bytes 442376 | tf_op jit(solution)/shard_map/ppermute | solution.py:306
  29.0 2.9 %collective-permute-start.2 = (bf16[3,96,256]{2,1,0:T(8,128)(2,1)S(1)}, bf16[3,96,256]{2,1,0:T(8,128)(2,1)S(1)}, u32[]{:S(2)}, u32[]{:S(2)}) collective-permute-start(bf16[3,96,256]{2,1,0:T(8,128)(2,1)S(1)} %get-tuple-element.30), channel_id=1, source_target_pairs={{0,3},{1,2},{2,1},{3,0},{4,7},{5,6},{6,5},{7,4},{8,11},{9,10},{10,... | collective-permute-start | bytes 442376 | tf_op jit(solution)/shard_map/ppermute | solution.py:306
  31.9 3.2 %collective-permute-done.refs_1_ = bf16[3,96,256]{2,1,0:T(8,128)(2,1)S(1)} collective-permute-done((bf16[3,96,256]{2,1,0:T(8,128)(2,1)S(1)}, bf16[3,96,256]{2,1,0:T(8,128)(2,1)S(1)}, u32[]{:S(2)}, u32[]{:S(2)}) %collective-permute-start) | collective-permute-done | bytes 147488 | tf_op jit(solution)/shard_map/ppermute | solution.py:306
  35.1 6.4 %collective-permute-done.1.refs_2_ = bf16[3,96,256]{2,1,0:T(8,128)(2,1)S(1)} collective-permute-done((bf16[3,96,256]{2,1,0:T(8,128)(2,1)S(1)}, bf16[3,96,256]{2,1,0:T(8,128)(2,1)S(1)}, u32[]{:S(2)}, u32[]{:S(2)}) %collective-permute-start.1) | collective-permute-done | bytes 147488 | tf_op jit(solution)/shard_map/ppermute | solution.py:306
  41.6 0.0 collective-permute-done.2.refs_3_
  41.6 0.1 shard_map.140.refs_0_
  41.7 0.0 copy-start.8
  41.7 1.6 %collective-permute-start.5 = (bf16[3,96,256]{2,1,0:T(8,128)(2,1)S(1)}, bf16[3,96,256]{2,1,0:T(8,128)(2,1)S(1)}, u32[]{:S(2)}, u32[]{:S(2)}) collective-permute-start(bf16[3,96,256]{2,1,0:T(8,128)(2,1)S(1)} %shard_map.140.refs_0_), channel_id=1, source_target_pairs={{0,3},{1,2},{2,1},{3,0},{4,7},{5,6},{6,5},{7,4},{8,11},{9,10},{10,... | collective-permute-start | bytes 442376 | tf_op jit(solution)/shard_map/ppermute | solution.py:306
  43.2 2.7 %collective-permute-start.4 = (bf16[3,96,256]{2,1,0:T(8,128)(2,1)S(1)}, bf16[3,96,256]{2,1,0:T(8,128)(2,1)S(1)}, u32[]{:S(2)}, u32[]{:S(2)}) collective-permute-start(bf16[3,96,256]{2,1,0:T(8,128)(2,1)S(1)} %shard_map.140.refs_0_), channel_id=1, source_target_pairs={{0,2},{1,3},{2,0},{3,1},{4,6},{5,7},{6,4},{7,5},{8,10},{9,11},{10,... | collective-permute-start | bytes 442376 | tf_op jit(solution)/shard_map/ppermute | solution.py:306
  45.9 0.2 collective-permute-start.3
  46.1 4.3 %collective-permute-done.5.refs_3_ = bf16[3,96,256]{2,1,0:T(8,128)(2,1)S(1)} collective-permute-done((bf16[3,96,256]{2,1,0:T(8,128)(2,1)S(1)}, bf16[3,96,256]{2,1,0:T(8,128)(2,1)S(1)}, u32[]{:S(2)}, u32[]{:S(2)}) %collective-permute-start.5) | collective-permute-done | bytes 147488 | tf_op jit(solution)/shard_map/ppermute | solution.py:306
  50.4 6.2 %collective-permute-done.4.refs_2_ = bf16[3,96,256]{2,1,0:T(8,128)(2,1)S(1)} collective-permute-done((bf16[3,96,256]{2,1,0:T(8,128)(2,1)S(1)}, bf16[3,96,256]{2,1,0:T(8,128)(2,1)S(1)}, u32[]{:S(2)}, u32[]{:S(2)}) %collective-permute-start.4) | collective-permute-done | bytes 147488 | tf_op jit(solution)/shard_map/ppermute | solution.py:306
  56.6 0.0 collective-permute-done.3.refs_1_
  56.6 0.0 copy-done.3
  56.6 2.7 %shard_map.141 = (bf16[16,48,256]{2,1,0:T(8,128)(2,1)}, bf16[96,1024]{1,0:T(8,128)(2,1)S(1)}) custom-call(bf16[3,96,256]{2,1,0:T(8,128)(2,1)S(1)} %shard_map.140.refs_0_, bf16[3,96,256]{2,1,0:T(8,128)(2,1)S(1)} %collective-permute-done.3.refs_1_, bf16[3,96,256]{2,1,0:T(8,128)(2,1)S(1)} %collective-permute-done.4.refs_2_, ...), custom_call_target="tpu_custom_call" | custom-call | flops 603979776 | bytes 8388608 | tf_op jit(solution)/shard_map/pallas_call | solution.py:249
  59.4 3.6 %all-to-all-start.1 = ((bf16[16,48,256]{2,1,0:T(8,128)(2,1)}), bf16[16,48,256]{2,1,0:T(8,128)(2,1)S(1)}, u32[]{:S(2)}, u32[]{:S(2)}) async-start(bf16[16,48,256]{2,1,0:T(8,128)(2,1)} %get-tuple-element.31), calls=%async_computation.1 | async-start | bytes 786432 | tf_op jit(solution)/shard_map/all_to_all | solution.py:348
  63.0 0.0 copy-done.8
  63.1 0.0 copy-start.4
  63.1 1.6 %copy-done.4 = bf16[1,1024,1024]{2,1,0:T(8,128)(2,1)S(1)} copy-done((bf16[1,1024,1024]{2,1,0:T(8,128)(2,1)S(1)}, bf16[1,1024,1024]{2,1,0:T(8,128)(2,1)}, u32[]{:S(2)}) %copy-start.4) | copy-done | bytes 2097176
  64.6 0.0 copy-start.5
  64.7 1.6 %copy-done.5 = bf16[1,1024,1024]{2,1,0:T(8,128)(2,1)S(1)} copy-done((bf16[1,1024,1024]{2,1,0:T(8,128)(2,1)S(1)}, bf16[1,1024,1024]{2,1,0:T(8,128)(2,1)}, u32[]{:S(2)}) %copy-start.5) | copy-done | bytes 2097176
  66.2 0.0 copy-start.6
  66.2 0.0 copy-start.7
  66.2 6.8 %shard_map.143 = (bf16[1,1024,1024]{2,1,0:T(8,128)(2,1)}, bf16[1,1024,1024]{2,1,0:T(8,128)(2,1)}, bf16[1,1024,1024]{2,1,0:T(8,128)(2,1)}) custom-call(s32[3]{0:T(128)S(1)} %copy-done.8, bf16[96,1024]{1,0:T(8,128)(2,1)S(1)} %get-tuple-element.34.hidden_ref, bf16[96,1024]{1,0:T(8,128)(2,1)S(1)} %get-tuple-element.35.dy_ref, ...), custom_call_target="tpu_custom_call" | custom-call | flops 201326592 | bytes 10485760 | tf_op jit(solution)/shard_map/pallas_call | solution.py:352
  73.1 2.9 %all-to-all-done.1.back_ref = bf16[16,48,256]{2,1,0:T(8,128)(2,1)S(1)} async-done(((bf16[16,48,256]{2,1,0:T(8,128)(2,1)}), bf16[16,48,256]{2,1,0:T(8,128)(2,1)S(1)}, u32[]{:S(2)}, u32[]{:S(2)}) %all-to-all-start.1) | async-done | bytes 393248 | tf_op jit(solution)/shard_map/all_to_all | solution.py:348
  75.9 0.0 copy-done.6
  75.9 0.0 copy-done.7
  75.9 1.8 %shard_map.142 = (bf16[128,4096]{1,0:T(8,128)(2,1)}, bf16[128,4096]{1,0:T(8,128)(2,1)}) custom-call(f32[32,128]{1,0:T(8,128)S(1)} %copy-done.6, f32[32,128]{1,0:T(8,128)S(1)} %copy-done.7, bf16[16,48,256]{2,1,0:T(8,128)(2,1)S(1)} %all-to-all-done.1.back_ref), custom_call_target="tpu_custom_call" | custom-call | bytes 4194304 | tf_op jit(solution)/shard_map/pallas_call | solution.py:249
Async XLA Ops:
  0.6 25.9 %copy-start.1 = (bf16[1,1024,1024]{2,1,0:T(8,128)(2,1)S(1)}, bf16[1,1024,1024]{2,1,0:T(8,128)(2,1)}, u32[]{:S(2)}) copy-start(bf16[1,1024,1024]{2,1,0:T(8,128)(2,1)} %refs_5_.1) | copy-start | bytes 6291460
  3.5 23.0 %copy-start = (bf16[1,1024,1024]{2,1,0:T(8,128)(2,1)S(1)}, bf16[1,1024,1024]{2,1,0:T(8,128)(2,1)}, u32[]{:S(2)}) copy-start(bf16[1,1024,1024]{2,1,0:T(8,128)(2,1)} %refs_4_.1) | copy-start | bytes 6291460
  23.9 1.6 %copy-start.2 = (bf16[1,1024,1024]{2,1,0:T(8,128)(2,1)S(1)}, bf16[1,1024,1024]{2,1,0:T(8,128)(2,1)}, u32[]{:S(2)}) copy-start(bf16[1,1024,1024]{2,1,0:T(8,128)(2,1)} %refs_6_.1) | copy-start | bytes 6291460
  26.5 30.1 %copy-start.3 = (bf16[1,1024,1024]{2,1,0:T(8,128)(2,1)S(1)}, bf16[1,1024,1024]{2,1,0:T(8,128)(2,1)}, u32[]{:S(2)}) copy-start(bf16[1,1024,1024]{2,1,0:T(8,128)(2,1)} %refs_6_.1) | copy-start | bytes 6291460
  27.5 7.7 %collective-permute-start = (bf16[3,96,256]{2,1,0:T(8,128)(2,1)S(1)}, bf16[3,96,256]{2,1,0:T(8,128)(2,1)S(1)}, u32[]{:S(2)}, u32[]{:S(2)}) collective-permute-start(bf16[3,96,256]{2,1,0:T(8,128)(2,1)S(1)} %get-tuple-element.28), channel_id=1, source_target_pairs={{0,1},{1,0},{2,3},{3,2},{4,5},{5,4},{6,7},{7,6},{8,9},{9,8},{10,11... | collective-permute-start | bytes 442376 | tf_op jit(solution)/shard_map/ppermute | solution.py:306
  27.5 14.0 %collective-permute-start.1 = (bf16[3,96,256]{2,1,0:T(8,128)(2,1)S(1)}, bf16[3,96,256]{2,1,0:T(8,128)(2,1)S(1)}, u32[]{:S(2)}, u32[]{:S(2)}) collective-permute-start(bf16[3,96,256]{2,1,0:T(8,128)(2,1)S(1)} %get-tuple-element.29), channel_id=1, source_target_pairs={{0,2},{1,3},{2,0},{3,1},{4,6},{5,7},{6,4},{7,5},{8,10},{9,11},{10,... | collective-permute-start | bytes 442376 | tf_op jit(solution)/shard_map/ppermute | solution.py:306
  29.0 12.6 %collective-permute-start.2 = (bf16[3,96,256]{2,1,0:T(8,128)(2,1)S(1)}, bf16[3,96,256]{2,1,0:T(8,128)(2,1)S(1)}, u32[]{:S(2)}, u32[]{:S(2)}) collective-permute-start(bf16[3,96,256]{2,1,0:T(8,128)(2,1)S(1)} %get-tuple-element.30), channel_id=1, source_target_pairs={{0,3},{1,2},{2,1},{3,0},{4,7},{5,6},{6,5},{7,4},{8,11},{9,10},{10,... | collective-permute-start | bytes 442376 | tf_op jit(solution)/shard_map/ppermute | solution.py:306
  41.7 21.4 %copy-start.8 = (s32[3]{0:T(128)S(1)}, s32[3]{0:T(128)}, u32[]{:S(2)}) copy-start(s32[3]{0:T(128)} %selected_ref.1) | copy-start | bytes 40
  41.7 8.7 %collective-permute-start.5 = (bf16[3,96,256]{2,1,0:T(8,128)(2,1)S(1)}, bf16[3,96,256]{2,1,0:T(8,128)(2,1)S(1)}, u32[]{:S(2)}, u32[]{:S(2)}) collective-permute-start(bf16[3,96,256]{2,1,0:T(8,128)(2,1)S(1)} %shard_map.140.refs_0_), channel_id=1, source_target_pairs={{0,3},{1,2},{2,1},{3,0},{4,7},{5,6},{6,5},{7,4},{8,11},{9,10},{10,... | collective-permute-start | bytes 442376 | tf_op jit(solution)/shard_map/ppermute | solution.py:306
  43.2 13.4 %collective-permute-start.4 = (bf16[3,96,256]{2,1,0:T(8,128)(2,1)S(1)}, bf16[3,96,256]{2,1,0:T(8,128)(2,1)S(1)}, u32[]{:S(2)}, u32[]{:S(2)}) collective-permute-start(bf16[3,96,256]{2,1,0:T(8,128)(2,1)S(1)} %shard_map.140.refs_0_), channel_id=1, source_target_pairs={{0,2},{1,3},{2,0},{3,1},{4,6},{5,7},{6,4},{7,5},{8,10},{9,11},{10,... | collective-permute-start | bytes 442376 | tf_op jit(solution)/shard_map/ppermute | solution.py:306
  45.9 10.7 %collective-permute-start.3 = (bf16[3,96,256]{2,1,0:T(8,128)(2,1)S(1)}, bf16[3,96,256]{2,1,0:T(8,128)(2,1)S(1)}, u32[]{:S(2)}, u32[]{:S(2)}) collective-permute-start(bf16[3,96,256]{2,1,0:T(8,128)(2,1)S(1)} %shard_map.140.refs_0_), channel_id=1, source_target_pairs={{0,1},{1,0},{2,3},{3,2},{4,5},{5,4},{6,7},{7,6},{8,9},{9,8},{10,11... | collective-permute-start | bytes 442376 | tf_op jit(solution)/shard_map/ppermute | solution.py:306
  59.4 16.5 %all-to-all-start.1 = ((bf16[16,48,256]{2,1,0:T(8,128)(2,1)}), bf16[16,48,256]{2,1,0:T(8,128)(2,1)S(1)}, u32[]{:S(2)}, u32[]{:S(2)}) async-start(bf16[16,48,256]{2,1,0:T(8,128)(2,1)} %get-tuple-element.31), calls=%async_computation.1 | async-start | bytes 786432 | tf_op jit(solution)/shard_map/all_to_all | solution.py:348
  63.1 1.6 %copy-start.4 = (bf16[1,1024,1024]{2,1,0:T(8,128)(2,1)S(1)}, bf16[1,1024,1024]{2,1,0:T(8,128)(2,1)}, u32[]{:S(2)}) copy-start(bf16[1,1024,1024]{2,1,0:T(8,128)(2,1)} %first_ref.1) | copy-start | bytes 6291460
  64.6 1.6 %copy-start.5 = (bf16[1,1024,1024]{2,1,0:T(8,128)(2,1)S(1)}, bf16[1,1024,1024]{2,1,0:T(8,128)(2,1)}, u32[]{:S(2)}) copy-start(bf16[1,1024,1024]{2,1,0:T(8,128)(2,1)} %second_ref.1) | copy-start | bytes 6291460
  66.2 9.7 %copy-start.6 = (f32[32,128]{1,0:T(8,128)S(1)}, f32[32,128]{1,0:T(8,128)}, u32[]{:S(2)}) copy-start(f32[32,128]{1,0:T(8,128)} %get-tuple-element.22.ones_ref) | copy-start | bytes 49156
  66.2 9.7 %copy-start.7 = (f32[32,128]{1,0:T(8,128)S(1)}, f32[32,128]{1,0:T(8,128)}, u32[]{:S(2)}) copy-start(f32[32,128]{1,0:T(8,128)} %get-tuple-element.23.gates_ref) | copy-start | bytes 49156

commit v3 on v2

--- a/solution.py
+++ b/solution.py
@@ -22,7 +22,7 @@
 VMEM = pl.BlockSpec(memory_space=pltpu.VMEM)
 SMEM = pl.BlockSpec(memory_space=pltpu.SMEM)
 MIB = 1 << 20
-MOST = 60
+MOST = 58
 
 
 def iota(shape, dim):
@@ -146,8 +146,11 @@
                 ].astype(BF16)
 
 
-def backward_kernel(arrived_ref, down_w, rows_x, rows_dy, total):
+def gather_kernel(arrived_ref, rows_x, rows_dy):
     gather_rows(arrived_ref, (rows_x, rows_dy))
+
+
+def backward_kernel(rows_dy, down_w, total):
     total[...] = dot(rows_dy[...], down_w[0], ((1,), (1,)))
 
 
@@ -177,6 +180,12 @@
     share_ref[2] = (grad * gate * sig).astype(BF16)
 
 
+def turn_kernel(*refs):
+    count = len(refs) // 2
+    for source, target in zip(refs[:count], refs[count:]):
+        target[...] = source[0].T
+
+
 def result_kernel(dp, *refs):
     arrived = refs[:dp]
     gate_w, up_w, down_w, sent_ref, hidden_ref, full = refs[dp:]
@@ -187,7 +196,7 @@
         hidden_ref[:, pl.ds(at, block)] = arrived[k][0]
         full[:, :, pl.ds(at, block)] = arrived[k][1:]
     out = dot(hidden_ref[...], down_w[0])
-    grad = dot(full[0], gate_w[0], ((1,), (1,))) + dot(full[1], up_w[0], ((1,), (1,)))
+    grad = dot(full[0], gate_w[...]) + dot(full[1], up_w[...])
     scatter_rows((out.astype(BF16), grad.astype(BF16)), sent_ref)
 
 
@@ -216,16 +225,16 @@
 def combine_kernel(
     experts, dp, ones_ref, gates_ref, back_ref, mixed_hbm, grad_hbm, mixed_ref, grad_ref, sems
 ):
-    _, lines_each, width = back_ref.shape
-    small = (experts * 8, experts * lines_each)
+    width = back_ref.shape[2]
+    small = (experts * 8, experts * LINES)
     source, target = iota(small, 0), iota(small, 1)
-    same = (source // 8 == target // lines_each) & (source % 8 < CAP)
-    within = target % lines_each
+    same = (source // 8 == target // LINES) & (source % 8 < CAP)
+    within = target % LINES - source % 8
     spreads = []
     for half, ref in ((0, gates_ref), (1, ones_ref)):
         weights = ref[...].astype(BF16)
         for c in range(CHUNKS):
-            spot = same & (within == half * HALF + c * CAP + source % 8)
+            spot = same & (within == half * HALF + c * CAP)
             spreads.append(dot(weights, spot.astype(F32).astype(BF16), ((0,), (0,))).astype(BF16))
     copies = []
     for j in range(dp):
@@ -235,11 +244,7 @@
                 at = (j * CHUNKS + c) * width
                 ref[:, at : at + width] = dot(spreads[half * CHUNKS + c], lines).astype(BF16)
             span = pl.ds(j * CHUNKS * width, CHUNKS * width)
-            copies.append(
-                pltpu.make_async_copy(
-                    ref.at[:, span], hbm.at[:, span], sems.at[half, j]
-                )
-            )
+            copies.append(pltpu.make_async_copy(ref.at[:, span], hbm.at[:, span], sems.at[half, j]))
             copies[-1].start()
     for c in copies:
         c.wait()
@@ -252,7 +257,7 @@
         in_specs=in_specs or [VMEM] * len(operands),
         out_specs=out_specs or jax.tree.map(lambda _: VMEM, outs),
         scratch_shapes=scratch,
-        compiler_params=pltpu.CompilerParams(vmem_limit_bytes=limit * MIB),
+        compiler_params=pltpu.CompilerParams(vmem_limit_bytes=int(limit * MIB)),
         cost_estimate=pl.CostEstimate(flops=flops, bytes_accessed=traffic, transcendentals=0),
     )(*operands)
 
@@ -310,16 +315,19 @@
 
     weights = (gate_weight, up_weight, down_weight)
 
-    rows_x, rows_dy, grad_parts = call(
+    rows_x, rows_dy = call(
+        gather_kernel,
+        (shape((slots, slice_width), BF16), shape((slots, slice_width), BF16)),
+        (arrived,),
+        flops=5 * 10**8,
+        traffic=MIB // 2,
+    )
+    grad_parts = call(
         backward_kernel,
-        (
-            shape((slots, slice_width), BF16),
-            shape((slots, slice_width), BF16),
-            shape((slots, hidden_units), F32),
-        ),
-        (arrived, down_weight),
-        flops=2 * cube,
-        traffic=3 * MIB,
+        shape((slots, hidden_units), F32),
+        (rows_dy, down_weight),
+        flops=5 * 10**8,
+        traffic=MIB // 8,
     )
     own, *parts = call(
         functools.partial(forward_kernel, dp),
@@ -330,6 +338,14 @@
         traffic=6 * MIB,
     )
     sums = [own, *swaps(parts)]
+    turned = call(
+        turn_kernel,
+        (shape((hidden_units, slice_width), BF16),) * 2,
+        (gate_weight, up_weight),
+        traffic=4 * MIB,
+    )
+    own, *turned = lax.optimization_barrier((own, *turned))
+    sums[0] = own
     share = call(
         share_kernel,
         shape((3, slots, block), BF16),
@@ -340,7 +356,7 @@
     results, hidden = call(
         functools.partial(result_kernel, dp),
         (shape((sources, LINES, width), BF16), shape((slots, hidden_units), BF16)),
-        (share, *shares, *weights),
+        (share, *shares, *turned, down_weight),
         scratch=[pltpu.VMEM((2, slots, hidden_units), BF16)],
         flops=6 * cube,
         traffic=8 * MIB,

time: 78.1 us -> 76.9 us (0.985)
  local copies, waits for them, and re-layouts: 4.8 us -> 2.67 us
    unnamed x18 -> x16, local copies, waits for them, and re-layouts: 4.8 us -> 2.67 us
    all_to_all x1, waiting for transfers between devices: 2.87 us -> 4.45 us  [local(): lax.all_to_all(results, ('expert', 'dp'), split_axis=0, concat_axis=0, ti...]
    ppermute x6, waiting for transfers between devices: 20.1 us -> 18.9 us  [swap(): return lax.ppermute(value, 'dp', [(i, i ^ k) for i in range(dp)])]
    pallas_call x6 -> x8, Pallas kernels: 9.37 us -> 10.1 us  [call(): pl.pallas_call(kernel, out_shape=outs, in_specs=in_specs or [VMEM] * len(...]
  transfers between devices with their start and end apart: 7 -> 7, of which waited for: 5 -> 5; matrix products, arithmetic and copies ran while one was open for 0% -> 0% of each run, Pallas kernels for 9% -> 11%
where the time goes in v3:
time: 76.9 us; the launch traced here: 76.5 us
  waiting for transfers between devices  23.4 us (30%)
  blocking collectives  20.3 us (26%)
  Pallas kernels  16.9 us (22%)
  starting transfers between devices  12.5 us (16%)
  local copies, waits for them, and re-layouts  2.67 us (3%)
    all_to_all x1, blocking collectives, local(): lax.all_to_all(sent, ('expert', 'dp'), split_axis=0, concat_axis=0, tiled...  20.3 us
    ppermute x6, waiting for transfers between devices, swap(): return lax.ppermute(value, 'dp', [(i, i ^ k) for i in range(dp)])  18.9 us
    pallas_call x8, Pallas kernels, call(): pl.pallas_call(kernel, out_shape=outs, in_specs=in_specs or [VMEM] * len(...  10.1 us
    ppermute x6, starting transfers between devices, swap(): return lax.ppermute(value, 'dp', [(i, i ^ k) for i in range(dp)])  8.9 us
    pallas_call x1, Pallas kernels, local(): pl.pallas_call(adam_kernel, grid=(hidden_units // strip,), in_specs=[SMEM...  6.81 us
    all_to_all x1, waiting for transfers between devices, local(): lax.all_to_all(results, ('expert', 'dp'), split_axis=0, concat_axis=0, ti...  4.45 us
    all_to_all x1, starting transfers between devices, local(): lax.all_to_all(results, ('expert', 'dp'), split_axis=0, concat_axis=0, ti...  3.64 us
    unnamed x16, local copies, waits for them, and re-layouts  2.67 us
  transfers between devices with their start and end apart: 7, of which 5 were waited for; matrix products, arithmetic and copies ran while one was open for 0% of the time, Pallas kernels for 11%

profile of v3, /device:TPU:0, one launch (start us, length us, event | category | flops | bytes accessed | tf_op | source)
XLA Modules:
  0.0 76.5 jit_solution(9745837321646976388)
XLA Ops:
  0.6 0.0 copy-start.2
  0.6 2.8 %shard_map.137 = (bf16[16,48,256]{2,1,0:T(8,128)(2,1)}, f32[32,128]{1,0:T(8,128)}, f32[32,128]{1,0:T(8,128)}) custom-call(s32[8,128]{1,0:T(8,128)} %bitcast.2, s32[8,128]{1,0:T(8,128)} %bitcast.3, bf16[128,4096]{1,0:T(8,128)(2,1)} %tok_hbm.1, bf16[128,4096]{1,0:T(8,128)(2,1)} %cot_hbm.1), custom_call_target="tpu_custom_call" | custom-call | bytes 6291456 | tf_op jit(solution)/shard_map/pallas_call | solution.py:254
  3.5 20.3 %all_to_all.10.arrived_ref = bf16[16,48,256]{2,1,0:T(8,128)(2,1)S(1)} all-to-all(bf16[16,48,256]{2,1,0:T(8,128)(2,1)} %get-tuple-element.28), channel_id=1, replica_groups=mesh['groups'=2,'expert'=4,'dp'=4] {'expert','dp'}, dimensions={0} | all-to-all | bytes 786432 | tf_op jit(solution)/shard_map/all_to_all | solution.py:309
  23.7 0.0 copy-start
  23.8 0.0 copy-start.1
  23.8 0.4 shard_map.138
  24.1 0.0 copy-done.2
  24.1 0.8 %shard_map.139.grad_ref = f32[96,1024]{1,0:T(8,128)S(1)} custom-call(bf16[96,1024]{1,0:T(8,128)(2,1)S(1)} %get-tuple-element.30.rows_dy.dy_ref, bf16[1,1024,1024]{2,1,0:T(8,128)(2,1)S(1)} %copy-done.2), custom_call_target="tpu_custom_call" | custom-call | flops 500000000 | bytes 131072 | tf_op jit(solution)/shard_map/pallas_call | solution.py:254
  24.9 0.4 copy-done
  25.3 0.6 copy-done.1
  26.0 0.9 %shard_map.140 = (f32[3,96,256]{2,1,0:T(8,128)S(1)}, bf16[3,96,256]{2,1,0:T(8,128)(2,1)S(1)}, bf16[3,96,256]{2,1,0:T(8,128)(2,1)S(1)}, bf16[3,96,256]{2,1,0:T(8,128)(2,1)S(1)}) custom-call(bf16[96,1024]{1,0:T(8,128)(2,1)S(1)} %get-tuple-element.29.rows_x, f32[96,1024]{1,0:T(8,128)S(1)} %shard_map.139.grad_ref, bf16[1,1024,1024]{2,1,0:T(8,128)(2,1)S(1)} %copy-done, ...), custom_call_target="tpu_custom_call" | custom-call | flops 402653184 | bytes 6291456 | tf_op jit(solution)/shard_map/pallas_call | solution.py:254
  26.9 0.1 collective-permute-start
  27.0 1.4 %collective-permute-start.1 = (bf16[3,96,256]{2,1,0:T(8,128)(2,1)S(1)}, bf16[3,96,256]{2,1,0:T(8,128)(2,1)S(1)}, u32[]{:S(2)}, u32[]{:S(2)}) collective-permute-start(bf16[3,96,256]{2,1,0:T(8,128)(2,1)S(1)} %get-tuple-element.36), channel_id=1, source_target_pairs={{0,2},{1,3},{2,0},{3,1},{4,6},{5,7},{6,4},{7,5},{8,10},{9,11},{10,... | collective-permute-start | bytes 442376 | tf_op jit(solution)/shard_map/ppermute | solution.py:311
  28.4 2.9 %collective-permute-start.2 = (bf16[3,96,256]{2,1,0:T(8,128)(2,1)S(1)}, bf16[3,96,256]{2,1,0:T(8,128)(2,1)S(1)}, u32[]{:S(2)}, u32[]{:S(2)}) collective-permute-start(bf16[3,96,256]{2,1,0:T(8,128)(2,1)S(1)} %get-tuple-element.37), channel_id=1, source_target_pairs={{0,3},{1,2},{2,1},{3,0},{4,7},{5,6},{6,5},{7,4},{8,11},{9,10},{10,... | collective-permute-start | bytes 442376 | tf_op jit(solution)/shard_map/ppermute | solution.py:311
  31.3 1.2 %shard_map.141 = (bf16[1024,1024]{1,0:T(8,128)(2,1)S(1)}, bf16[1024,1024]{1,0:T(8,128)(2,1)S(1)}) custom-call(bf16[1,1024,1024]{2,1,0:T(8,128)(2,1)S(1)} %copy-done, bf16[1,1024,1024]{2,1,0:T(8,128)(2,1)S(1)} %copy-done.1), custom_call_target="tpu_custom_call" | custom-call | bytes 4194304 | tf_op jit(solution)/shard_map/pallas_call | solution.py:254
  32.6 2.0 %collective-permute-done.refs_1_ = bf16[3,96,256]{2,1,0:T(8,128)(2,1)S(1)} collective-permute-done((bf16[3,96,256]{2,1,0:T(8,128)(2,1)S(1)}, bf16[3,96,256]{2,1,0:T(8,128)(2,1)S(1)}, u32[]{:S(2)}, u32[]{:S(2)}) %collective-permute-start) | collective-permute-done | bytes 147488 | tf_op jit(solution)/shard_map/ppermute | solution.py:311
  34.6 6.4 %collective-permute-done.1.refs_2_ = bf16[3,96,256]{2,1,0:T(8,128)(2,1)S(1)} collective-permute-done((bf16[3,96,256]{2,1,0:T(8,128)(2,1)S(1)}, bf16[3,96,256]{2,1,0:T(8,128)(2,1)S(1)}, u32[]{:S(2)}, u32[]{:S(2)}) %collective-permute-start.1) | collective-permute-done | bytes 147488 | tf_op jit(solution)/shard_map/ppermute | solution.py:311
  41.0 0.0 collective-permute-done.2.refs_3_
  41.0 0.1 shard_map.142.refs_0_
  41.1 0.0 copy-start.7
  41.1 1.6 %collective-permute-start.5 = (bf16[3,96,256]{2,1,0:T(8,128)(2,1)S(1)}, bf16[3,96,256]{2,1,0:T(8,128)(2,1)S(1)}, u32[]{:S(2)}, u32[]{:S(2)}) collective-permute-start(bf16[3,96,256]{2,1,0:T(8,128)(2,1)S(1)} %shard_map.142.refs_0_), channel_id=1, source_target_pairs={{0,3},{1,2},{2,1},{3,0},{4,7},{5,6},{6,5},{7,4},{8,11},{9,10},{10,... | collective-permute-start | bytes 442376 | tf_op jit(solution)/shard_map/ppermute | solution.py:311
  42.7 2.7 %collective-permute-start.4 = (bf16[3,96,256]{2,1,0:T(8,128)(2,1)S(1)}, bf16[3,96,256]{2,1,0:T(8,128)(2,1)S(1)}, u32[]{:S(2)}, u32[]{:S(2)}) collective-permute-start(bf16[3,96,256]{2,1,0:T(8,128)(2,1)S(1)} %shard_map.142.refs_0_), channel_id=1, source_target_pairs={{0,2},{1,3},{2,0},{3,1},{4,6},{5,7},{6,4},{7,5},{8,10},{9,11},{10,... | collective-permute-start | bytes 442376 | tf_op jit(solution)/shard_map/ppermute | solution.py:311
  45.4 0.2 collective-permute-start.3
  45.6 4.3 %collective-permute-done.5.refs_3_ = bf16[3,96,256]{2,1,0:T(8,128)(2,1)S(1)} collective-permute-done((bf16[3,96,256]{2,1,0:T(8,128)(2,1)S(1)}, bf16[3,96,256]{2,1,0:T(8,128)(2,1)S(1)}, u32[]{:S(2)}, u32[]{:S(2)}) %collective-permute-start.5) | collective-permute-done | bytes 147488 | tf_op jit(solution)/shard_map/ppermute | solution.py:311
  49.8 6.2 %collective-permute-done.4.refs_2_ = bf16[3,96,256]{2,1,0:T(8,128)(2,1)S(1)} collective-permute-done((bf16[3,96,256]{2,1,0:T(8,128)(2,1)S(1)}, bf16[3,96,256]{2,1,0:T(8,128)(2,1)S(1)}, u32[]{:S(2)}, u32[]{:S(2)}) %collective-permute-start.4) | collective-permute-done | bytes 147488 | tf_op jit(solution)/shard_map/ppermute | solution.py:311
  56.1 0.0 collective-permute-done.3.refs_1_
  56.1 0.0 copy-start.3
  56.1 2.1 %shard_map.143 = (bf16[16,48,256]{2,1,0:T(8,128)(2,1)}, bf16[96,1024]{1,0:T(8,128)(2,1)S(1)}) custom-call(bf16[3,96,256]{2,1,0:T(8,128)(2,1)S(1)} %shard_map.142.refs_0_, bf16[3,96,256]{2,1,0:T(8,128)(2,1)S(1)} %collective-permute-done.3.refs_1_, bf16[3,96,256]{2,1,0:T(8,128)(2,1)S(1)} %collective-permute-done.4.refs_2_, ...), custom_call_target="tpu_custom_call" | custom-call | flops 603979776 | bytes 8388608 | tf_op jit(solution)/shard_map/pallas_call | solution.py:254
  58.2 3.6 %all-to-all-start.1 = ((bf16[16,48,256]{2,1,0:T(8,128)(2,1)}), bf16[16,48,256]{2,1,0:T(8,128)(2,1)S(1)}, u32[]{:S(2)}, u32[]{:S(2)}) async-start(bf16[16,48,256]{2,1,0:T(8,128)(2,1)} %get-tuple-element.40), calls=%async_computation.1 | async-start | bytes 786432 | tf_op jit(solution)/shard_map/all_to_all | solution.py:364
  61.9 0.0 copy-done.7
  61.9 0.0 copy-done.3
  61.9 0.0 copy-start.4
  61.9 1.6 %copy-done.4 = bf16[1,1024,1024]{2,1,0:T(8,128)(2,1)S(1)} copy-done((bf16[1,1024,1024]{2,1,0:T(8,128)(2,1)S(1)}, bf16[1,1024,1024]{2,1,0:T(8,128)(2,1)}, u32[]{:S(2)}) %copy-start.4) | copy-done | bytes 2097176
  63.5 0.0 copy-start.5
  63.5 0.0 copy-start.6
  63.5 6.8 %shard_map.145 = (bf16[1,1024,1024]{2,1,0:T(8,128)(2,1)}, bf16[1,1024,1024]{2,1,0:T(8,128)(2,1)}, bf16[1,1024,1024]{2,1,0:T(8,128)(2,1)}) custom-call(s32[3]{0:T(128)S(1)} %copy-done.7, bf16[96,1024]{1,0:T(8,128)(2,1)S(1)} %get-tuple-element.43.hidden_ref, bf16[96,1024]{1,0:T(8,128)(2,1)S(1)} %get-tuple-element.30.rows_dy.dy_ref, ...), custom_call_target="tpu_custom_call" | custom-call | flops 201326592 | bytes 10485760 | tf_op jit(solution)/shard_map/pallas_call | solution.py:368
  70.3 4.4 %all-to-all-done.1.back_ref = bf16[16,48,256]{2,1,0:T(8,128)(2,1)S(1)} async-done(((bf16[16,48,256]{2,1,0:T(8,128)(2,1)}), bf16[16,48,256]{2,1,0:T(8,128)(2,1)S(1)}, u32[]{:S(2)}, u32[]{:S(2)}) %all-to-all-start.1) | async-done | bytes 393248 | tf_op jit(solution)/shard_map/all_to_all | solution.py:364
  74.8 0.0 copy-done.5
  74.8 0.0 copy-done.6
  74.8 1.8 %shard_map.144 = (bf16[128,4096]{1,0:T(8,128)(2,1)}, bf16[128,4096]{1,0:T(8,128)(2,1)}) custom-call(f32[32,128]{1,0:T(8,128)S(1)} %copy-done.5, f32[32,128]{1,0:T(8,128)S(1)} %copy-done.6, bf16[16,48,256]{2,1,0:T(8,128)(2,1)S(1)} %all-to-all-done.1.back_ref), custom_call_target="tpu_custom_call" | custom-call | bytes 4194304 | tf_op jit(solution)/shard_map/pallas_call | solution.py:254
Async XLA Ops:
  0.6 23.5 %copy-start.2 = (bf16[1,1024,1024]{2,1,0:T(8,128)(2,1)S(1)}, bf16[1,1024,1024]{2,1,0:T(8,128)(2,1)}, u32[]{:S(2)}) copy-start(bf16[1,1024,1024]{2,1,0:T(8,128)(2,1)} %refs_6_.1) | copy-start | bytes 6291460
  23.7 1.6 %copy-start = (bf16[1,1024,1024]{2,1,0:T(8,128)(2,1)S(1)}, bf16[1,1024,1024]{2,1,0:T(8,128)(2,1)}, u32[]{:S(2)}) copy-start(bf16[1,1024,1024]{2,1,0:T(8,128)(2,1)} %refs_0_.1) | copy-start | bytes 6291460
  23.8 2.2 %copy-start.1 = (bf16[1,1024,1024]{2,1,0:T(8,128)(2,1)S(1)}, bf16[1,1024,1024]{2,1,0:T(8,128)(2,1)}, u32[]{:S(2)}) copy-start(bf16[1,1024,1024]{2,1,0:T(8,128)(2,1)} %refs_1_.1) | copy-start | bytes 6291460
  26.9 7.7 %collective-permute-start = (bf16[3,96,256]{2,1,0:T(8,128)(2,1)S(1)}, bf16[3,96,256]{2,1,0:T(8,128)(2,1)S(1)}, u32[]{:S(2)}, u32[]{:S(2)}) collective-permute-start(bf16[3,96,256]{2,1,0:T(8,128)(2,1)S(1)} %get-tuple-element.35), channel_id=1, source_target_pairs={{0,1},{1,0},{2,3},{3,2},{4,5},{5,4},{6,7},{7,6},{8,9},{9,8},{10,11... | collective-permute-start | bytes 442376 | tf_op jit(solution)/shard_map/ppermute | solution.py:311
  27.0 14.0 %collective-permute-start.1 = (bf16[3,96,256]{2,1,0:T(8,128)(2,1)S(1)}, bf16[3,96,256]{2,1,0:T(8,128)(2,1)S(1)}, u32[]{:S(2)}, u32[]{:S(2)}) collective-permute-start(bf16[3,96,256]{2,1,0:T(8,128)(2,1)S(1)} %get-tuple-element.36), channel_id=1, source_target_pairs={{0,2},{1,3},{2,0},{3,1},{4,6},{5,7},{6,4},{7,5},{8,10},{9,11},{10,... | collective-permute-start | bytes 442376 | tf_op jit(solution)/shard_map/ppermute | solution.py:311
  28.4 12.6 %collective-permute-start.2 = (bf16[3,96,256]{2,1,0:T(8,128)(2,1)S(1)}, bf16[3,96,256]{2,1,0:T(8,128)(2,1)S(1)}, u32[]{:S(2)}, u32[]{:S(2)}) collective-permute-start(bf16[3,96,256]{2,1,0:T(8,128)(2,1)S(1)} %get-tuple-element.37), channel_id=1, source_target_pairs={{0,3},{1,2},{2,1},{3,0},{4,7},{5,6},{6,5},{7,4},{8,11},{9,10},{10,... | collective-permute-start | bytes 442376 | tf_op jit(solution)/shard_map/ppermute | solution.py:311
  41.1 20.8 %copy-start.7 = (s32[3]{0:T(128)S(1)}, s32[3]{0:T(128)}, u32[]{:S(2)}) copy-start(s32[3]{0:T(128)} %selected_ref.1) | copy-start | bytes 40
  41.1 8.7 %collective-permute-start.5 = (bf16[3,96,256]{2,1,0:T(8,128)(2,1)S(1)}, bf16[3,96,256]{2,1,0:T(8,128)(2,1)S(1)}, u32[]{:S(2)}, u32[]{:S(2)}) collective-permute-start(bf16[3,96,256]{2,1,0:T(8,128)(2,1)S(1)} %shard_map.142.refs_0_), channel_id=1, source_target_pairs={{0,3},{1,2},{2,1},{3,0},{4,7},{5,6},{6,5},{7,4},{8,11},{9,10},{10,... | collective-permute-start | bytes 442376 | tf_op jit(solution)/shard_map/ppermute | solution.py:311
  42.7 13.4 %collective-permute-start.4 = (bf16[3,96,256]{2,1,0:T(8,128)(2,1)S(1)}, bf16[3,96,256]{2,1,0:T(8,128)(2,1)S(1)}, u32[]{:S(2)}, u32[]{:S(2)}) collective-permute-start(bf16[3,96,256]{2,1,0:T(8,128)(2,1)S(1)} %shard_map.142.refs_0_), channel_id=1, source_target_pairs={{0,2},{1,3},{2,0},{3,1},{4,6},{5,7},{6,4},{7,5},{8,10},{9,11},{10,... | collective-permute-start | bytes 442376 | tf_op jit(solution)/shard_map/ppermute | solution.py:311
  45.4 10.7 %collective-permute-start.3 = (bf16[3,96,256]{2,1,0:T(8,128)(2,1)S(1)}, bf16[3,96,256]{2,1,0:T(8,128)(2,1)S(1)}, u32[]{:S(2)}, u32[]{:S(2)}) collective-permute-start(bf16[3,96,256]{2,1,0:T(8,128)(2,1)S(1)} %shard_map.142.refs_0_), channel_id=1, source_target_pairs={{0,1},{1,0},{2,3},{3,2},{4,5},{5,4},{6,7},{7,6},{8,9},{9,8},{10,11... | collective-permute-start | bytes 442376 | tf_op jit(solution)/shard_map/ppermute | solution.py:311
  56.1 5.8 %copy-start.3 = (bf16[1,1024,1024]{2,1,0:T(8,128)(2,1)S(1)}, bf16[1,1024,1024]{2,1,0:T(8,128)(2,1)}, u32[]{:S(2)}) copy-start(bf16[1,1024,1024]{2,1,0:T(8,128)(2,1)} %first_ref.1) | copy-start | bytes 6291460
  58.2 16.5 %all-to-all-start.1 = ((bf16[16,48,256]{2,1,0:T(8,128)(2,1)}), bf16[16,48,256]{2,1,0:T(8,128)(2,1)S(1)}, u32[]{:S(2)}, u32[]{:S(2)}) async-start(bf16[16,48,256]{2,1,0:T(8,128)(2,1)} %get-tuple-element.40), calls=%async_computation.1 | async-start | bytes 786432 | tf_op jit(solution)/shard_map/all_to_all | solution.py:364
  61.9 1.6 %copy-start.4 = (bf16[1,1024,1024]{2,1,0:T(8,128)(2,1)S(1)}, bf16[1,1024,1024]{2,1,0:T(8,128)(2,1)}, u32[]{:S(2)}) copy-start(bf16[1,1024,1024]{2,1,0:T(8,128)(2,1)} %second_ref.1) | copy-start | bytes 6291460
  63.5 11.3 %copy-start.5 = (f32[32,128]{1,0:T(8,128)S(1)}, f32[32,128]{1,0:T(8,128)}, u32[]{:S(2)}) copy-start(f32[32,128]{1,0:T(8,128)} %get-tuple-element.26.ones_ref) | copy-start | bytes 49156
  63.5 11.3 %copy-start.6 = (f32[32,128]{1,0:T(8,128)S(1)}, f32[32,128]{1,0:T(8,128)}, u32[]{:S(2)}) copy-start(f32[32,128]{1,0:T(8,128)} %get-tuple-element.27.gates_ref) | copy-start | bytes 49156

commit v4 on v3

--- a/solution.py
+++ b/solution.py
@@ -23,6 +23,8 @@
 SMEM = pl.BlockSpec(memory_space=pltpu.SMEM)
 MIB = 1 << 20
 MOST = 58
+GF = 5 * 10**8
+GU = 3 * 10**8
 
 
 def iota(shape, dim):
@@ -150,21 +152,21 @@
     gather_rows(arrived_ref, (rows_x, rows_dy))
 
 
-def backward_kernel(rows_dy, down_w, total):
-    total[...] = dot(rows_dy[...], down_w[0], ((1,), (1,)))
-
-
-def forward_kernel(dp, rows_x, grad_ref, gate_w, up_w, own_ref, *refs):
-    sent, (total,) = refs[: dp - 1], refs[dp - 1 :]
+def forward_kernel(rows_x, gate_w, up_w, total):
     total[0] = dot(rows_x[...], gate_w[0])
     total[1] = dot(rows_x[...], up_w[0])
+
+
+def backward_kernel(dp, rows_dy, pre_ref, down_w, own_ref, *refs):
+    sent, (total,) = refs[: dp - 1], refs[dp - 1 :]
+    total[...] = dot(rows_dy[...], down_w[0], ((1,), (1,)))
     me = lax.axis_index("dp")
-    block = total.shape[2] // dp
+    block = total.shape[1] // dp
     for k in range(dp):
         at = pl.ds(pl.multiple_of(jnp.bitwise_xor(me, k) * block, block), block)
         target = own_ref if k == 0 else sent[k - 1]
-        target[:2] = total[:, :, at].astype(target.dtype)
-        target[2] = grad_ref[:, at].astype(target.dtype)
+        target[:2] = pre_ref[:, :, at].astype(target.dtype)
+        target[2] = total[:, at].astype(target.dtype)
 
 
 def summed(refs, i):
@@ -319,23 +321,23 @@
         gather_kernel,
         (shape((slots, slice_width), BF16), shape((slots, slice_width), BF16)),
         (arrived,),
-        flops=5 * 10**8,
+        flops=GF,
         traffic=MIB // 2,
     )
-    grad_parts = call(
-        backward_kernel,
-        shape((slots, hidden_units), F32),
-        (rows_dy, down_weight),
+    pre_parts = call(
+        forward_kernel,
+        shape((2, slots, hidden_units), F32),
+        (rows_x, gate_weight, up_weight),
+        flops=GU,
+        traffic=MIB // 8,
+    )
+    own, *parts = call(
+        functools.partial(backward_kernel, dp),
+        (shape((3, slots, block), F32),) + (shape((3, slots, block), BF16),) * (dp - 1),
+        (rows_dy, pre_parts, down_weight),
+        scratch=[pltpu.VMEM((slots, hidden_units), F32)],
         flops=5 * 10**8,
         traffic=MIB // 8,
-    )
-    own, *parts = call(
-        functools.partial(forward_kernel, dp),
-        (shape((3, slots, block), F32),) + (shape((3, slots, block), BF16),) * (dp - 1),
-        (rows_x, grad_parts, gate_weight, up_weight),
-        scratch=[pltpu.VMEM((2, slots, hidden_units), F32)],
-        flops=4 * cube,
-        traffic=6 * MIB,
     )
     sums = [own, *swaps(parts)]
     turned = call(

time: 76.9 us -> 76.6 us (level)
  Pallas kernels: 16.9 us -> 14.6 us
  waiting for transfers between devices: 23.4 us -> 25.6 us
    pallas_call x1, Pallas kernels: 6.81 us -> 4.61 us  [local(): pl.pallas_call(adam_kernel, grid=(hidden_units // strip,), in_specs=[SMEM...]
    all_to_all x1, waiting for transfers between devices: 4.45 us -> 6.65 us  [local(): lax.all_to_all(results, ('expert', 'dp'), split_axis=0, concat_axis=0, ti...]
  transfers between devices with their start and end apart: 7 -> 7, of which waited for: 5 -> 5; matrix products, arithmetic and copies ran while one was open for 0% -> 0% of each run, Pallas kernels for 11% -> 8%
where the time goes in v4:
time: 76.6 us; the launch traced here: 76.2 us
  waiting for transfers between devices  25.6 us (33%)
  blocking collectives  20.3 us (27%)
  Pallas kernels  14.6 us (19%)
  starting transfers between devices  12.5 us (16%)
  local copies, waits for them, and re-layouts  2.4 us (3%)
  between operations  0.77 us (1%)
    all_to_all x1, blocking collectives, local(): lax.all_to_all(sent, ('expert', 'dp'), split_axis=0, concat_axis=0, tiled...  20.3 us
    ppermute x6, waiting for transfers between devices, swap(): return lax.ppermute(value, 'dp', [(i, i ^ k) for i in range(dp)])  18.9 us
    pallas_call x8, Pallas kernels, call(): pl.pallas_call(kernel, out_shape=outs, in_specs=in_specs or [VMEM] * len(...  10 us
    ppermute x6, starting transfers between devices, swap(): return lax.ppermute(value, 'dp', [(i, i ^ k) for i in range(dp)])  8.9 us
    all_to_all x1, waiting for transfers between devices, local(): lax.all_to_all(results, ('expert', 'dp'), split_axis=0, concat_axis=0, ti...  6.65 us
    pallas_call x1, Pallas kernels, local(): pl.pallas_call(adam_kernel, grid=(hidden_units // strip,), in_specs=[SMEM...  4.61 us
    all_to_all x1, starting transfers between devices, local(): lax.all_to_all(results, ('expert', 'dp'), split_axis=0, concat_axis=0, ti...  3.64 us
    unnamed x16, local copies, waits for them, and re-layouts  2.4 us
  transfers between devices with their start and end apart: 7, of which 5 were waited for; matrix products, arithmetic and copies ran while one was open for 0% of the time, Pallas kernels for 8%

profile of v4, /device:TPU:0, one launch (start us, length us, event | category | flops | bytes accessed | tf_op | source)
XLA Modules:
  0.0 76.2 jit_solution(4569315770439740196)
XLA Ops:
  0.6 0.0 copy-start
  0.6 0.0 copy-start.1
  0.7 2.8 %shard_map.137 = (bf16[16,48,256]{2,1,0:T(8,128)(2,1)}, f32[32,128]{1,0:T(8,128)}, f32[32,128]{1,0:T(8,128)}) custom-call(s32[8,128]{1,0:T(8,128)} %bitcast.2, s32[8,128]{1,0:T(8,128)} %bitcast.3, bf16[128,4096]{1,0:T(8,128)(2,1)} %tok_hbm.1, bf16[128,4096]{1,0:T(8,128)(2,1)} %cot_hbm.1), custom_call_target="tpu_custom_call" | custom-call | bytes 6291456 | tf_op jit(solution)/shard_map/pallas_call | solution.py:256
  3.5 20.3 %all_to_all.10.arrived_ref = bf16[16,48,256]{2,1,0:T(8,128)(2,1)S(1)} all-to-all(bf16[16,48,256]{2,1,0:T(8,128)(2,1)} %get-tuple-element.28), channel_id=1, replica_groups=mesh['groups'=2,'expert'=4,'dp'=4] {'expert','dp'}, dimensions={0} | all-to-all | bytes 786432 | tf_op jit(solution)/shard_map/all_to_all | solution.py:311
  23.8 0.4 shard_map.138
  24.1 0.0 copy-done
  24.1 0.0 copy-done.1
  24.2 0.0 copy-start.2
  24.2 0.8 %shard_map.139.pre_ref = f32[2,96,1024]{2,1,0:T(8,128)S(1)} custom-call(bf16[96,1024]{1,0:T(8,128)(2,1)S(1)} %get-tuple-element.30.rows_x, bf16[1,1024,1024]{2,1,0:T(8,128)(2,1)S(1)} %copy-done, bf16[1,1024,1024]{2,1,0:T(8,128)(2,1)S(1)} %copy-done.1), custom_call_target="tpu_custom_call" | custom-call | flops 300000000 | bytes 131072 | tf_op jit(solution)/shard_map/pallas_call | solution.py:256
  25.0 0.8 %copy-done.2 = bf16[1,1024,1024]{2,1,0:T(8,128)(2,1)S(1)} copy-done((bf16[1,1024,1024]{2,1,0:T(8,128)(2,1)S(1)}, bf16[1,1024,1024]{2,1,0:T(8,128)(2,1)}, u32[]{:S(2)}) %copy-start.2) | copy-done | bytes 2097176
  25.8 0.8 %shard_map.140 = (f32[3,96,256]{2,1,0:T(8,128)S(1)}, bf16[3,96,256]{2,1,0:T(8,128)(2,1)S(1)}, bf16[3,96,256]{2,1,0:T(8,128)(2,1)S(1)}, bf16[3,96,256]{2,1,0:T(8,128)(2,1)S(1)}) custom-call(bf16[96,1024]{1,0:T(8,128)(2,1)S(1)} %get-tuple-element.29.rows_dy.dy_ref, f32[2,96,1024]{2,1,0:T(8,128)S(1)} %shard_map.139.pre_ref, bf16[1,1024,1024]{2,1,0:T(8,128)(2,1)S(1)} %copy-done.2), custom_call_target="tpu_custom_call" | custom-call | flops 500000000 | bytes 131072 | tf_op jit(solution)/shard_map/pallas_call | solution.py:256
  26.6 0.1 collective-permute-start
  26.7 1.4 %collective-permute-start.1 = (bf16[3,96,256]{2,1,0:T(8,128)(2,1)S(1)}, bf16[3,96,256]{2,1,0:T(8,128)(2,1)S(1)}, u32[]{:S(2)}, u32[]{:S(2)}) collective-permute-start(bf16[3,96,256]{2,1,0:T(8,128)(2,1)S(1)} %get-tuple-element.36), channel_id=1, source_target_pairs={{0,2},{1,3},{2,0},{3,1},{4,6},{5,7},{6,4},{7,5},{8,10},{9,11},{10,... | collective-permute-start | bytes 442376 | tf_op jit(solution)/shard_map/ppermute | solution.py:313
  28.1 2.9 %collective-permute-start.2 = (bf16[3,96,256]{2,1,0:T(8,128)(2,1)S(1)}, bf16[3,96,256]{2,1,0:T(8,128)(2,1)S(1)}, u32[]{:S(2)}, u32[]{:S(2)}) collective-permute-start(bf16[3,96,256]{2,1,0:T(8,128)(2,1)S(1)} %get-tuple-element.37), channel_id=1, source_target_pairs={{0,3},{1,2},{2,1},{3,0},{4,7},{5,6},{6,5},{7,4},{8,11},{9,10},{10,... | collective-permute-start | bytes 442376 | tf_op jit(solution)/shard_map/ppermute | solution.py:313
  31.0 1.2 %shard_map.141 = (bf16[1024,1024]{1,0:T(8,128)(2,1)S(1)}, bf16[1024,1024]{1,0:T(8,128)(2,1)S(1)}) custom-call(bf16[1,1024,1024]{2,1,0:T(8,128)(2,1)S(1)} %copy-done, bf16[1,1024,1024]{2,1,0:T(8,128)(2,1)S(1)} %copy-done.1), custom_call_target="tpu_custom_call" | custom-call | bytes 4194304 | tf_op jit(solution)/shard_map/pallas_call | solution.py:256
  32.3 2.0 %collective-permute-done.refs_1_ = bf16[3,96,256]{2,1,0:T(8,128)(2,1)S(1)} collective-permute-done((bf16[3,96,256]{2,1,0:T(8,128)(2,1)S(1)}, bf16[3,96,256]{2,1,0:T(8,128)(2,1)S(1)}, u32[]{:S(2)}, u32[]{:S(2)}) %collective-permute-start) | collective-permute-done | bytes 147488 | tf_op jit(solution)/shard_map/ppermute | solution.py:313
  34.2 6.4 %collective-permute-done.1.refs_2_ = bf16[3,96,256]{2,1,0:T(8,128)(2,1)S(1)} collective-permute-done((bf16[3,96,256]{2,1,0:T(8,128)(2,1)S(1)}, bf16[3,96,256]{2,1,0:T(8,128)(2,1)S(1)}, u32[]{:S(2)}, u32[]{:S(2)}) %collective-permute-start.1) | collective-permute-done | bytes 147488 | tf_op jit(solution)/shard_map/ppermute | solution.py:313
  40.7 0.0 collective-permute-done.2.refs_3_
  40.7 0.1 shard_map.142.refs_0_
  40.8 0.0 copy-start.7
  40.8 1.5 %collective-permute-start.5 = (bf16[3,96,256]{2,1,0:T(8,128)(2,1)S(1)}, bf16[3,96,256]{2,1,0:T(8,128)(2,1)S(1)}, u32[]{:S(2)}, u32[]{:S(2)}) collective-permute-start(bf16[3,96,256]{2,1,0:T(8,128)(2,1)S(1)} %shard_map.142.refs_0_), channel_id=1, source_target_pairs={{0,3},{1,2},{2,1},{3,0},{4,7},{5,6},{6,5},{7,4},{8,11},{9,10},{10,... | collective-permute-start | bytes 442376 | tf_op jit(solution)/shard_map/ppermute | solution.py:313
  42.3 2.7 %collective-permute-start.4 = (bf16[3,96,256]{2,1,0:T(8,128)(2,1)S(1)}, bf16[3,96,256]{2,1,0:T(8,128)(2,1)S(1)}, u32[]{:S(2)}, u32[]{:S(2)}) collective-permute-start(bf16[3,96,256]{2,1,0:T(8,128)(2,1)S(1)} %shard_map.142.refs_0_), channel_id=1, source_target_pairs={{0,2},{1,3},{2,0},{3,1},{4,6},{5,7},{6,4},{7,5},{8,10},{9,11},{10,... | collective-permute-start | bytes 442376 | tf_op jit(solution)/shard_map/ppermute | solution.py:313
  45.0 0.2 collective-permute-start.3
  45.3 4.3 %collective-permute-done.5.refs_3_ = bf16[3,96,256]{2,1,0:T(8,128)(2,1)S(1)} collective-permute-done((bf16[3,96,256]{2,1,0:T(8,128)(2,1)S(1)}, bf16[3,96,256]{2,1,0:T(8,128)(2,1)S(1)}, u32[]{:S(2)}, u32[]{:S(2)}) %collective-permute-start.5) | collective-permute-done | bytes 147488 | tf_op jit(solution)/shard_map/ppermute | solution.py:313
  49.5 6.2 %collective-permute-done.4.refs_2_ = bf16[3,96,256]{2,1,0:T(8,128)(2,1)S(1)} collective-permute-done((bf16[3,96,256]{2,1,0:T(8,128)(2,1)S(1)}, bf16[3,96,256]{2,1,0:T(8,128)(2,1)S(1)}, u32[]{:S(2)}, u32[]{:S(2)}) %collective-permute-start.4) | collective-permute-done | bytes 147488 | tf_op jit(solution)/shard_map/ppermute | solution.py:313
  55.8 0.0 collective-permute-done.3.refs_1_
  55.8 0.0 copy-start.3
  55.8 2.1 %shard_map.143 = (bf16[16,48,256]{2,1,0:T(8,128)(2,1)}, bf16[96,1024]{1,0:T(8,128)(2,1)S(1)}) custom-call(bf16[3,96,256]{2,1,0:T(8,128)(2,1)S(1)} %shard_map.142.refs_0_, bf16[3,96,256]{2,1,0:T(8,128)(2,1)S(1)} %collective-permute-done.3.refs_1_, bf16[3,96,256]{2,1,0:T(8,128)(2,1)S(1)} %collective-permute-done.4.refs_2_, ...), custom_call_target="tpu_custom_call" | custom-call | flops 603979776 | bytes 8388608 | tf_op jit(solution)/shard_map/pallas_call | solution.py:256
  57.9 3.6 %all-to-all-start.1 = ((bf16[16,48,256]{2,1,0:T(8,128)(2,1)}), bf16[16,48,256]{2,1,0:T(8,128)(2,1)S(1)}, u32[]{:S(2)}, u32[]{:S(2)}) async-start(bf16[16,48,256]{2,1,0:T(8,128)(2,1)} %get-tuple-element.40), calls=%async_computation.1 | async-start | bytes 786432 | tf_op jit(solution)/shard_map/all_to_all | solution.py:366
  61.5 0.0 copy-done.7
  61.5 0.0 copy-done.3
  61.6 0.0 copy-start.4
  61.6 1.6 %copy-done.4 = bf16[1,1024,1024]{2,1,0:T(8,128)(2,1)S(1)} copy-done((bf16[1,1024,1024]{2,1,0:T(8,128)(2,1)S(1)}, bf16[1,1024,1024]{2,1,0:T(8,128)(2,1)}, u32[]{:S(2)}) %copy-start.4) | copy-done | bytes 2097176
  63.2 0.0 copy-start.5
  63.2 0.0 copy-start.6
  63.2 4.6 %shard_map.145 = (bf16[1,1024,1024]{2,1,0:T(8,128)(2,1)}, bf16[1,1024,1024]{2,1,0:T(8,128)(2,1)}, bf16[1,1024,1024]{2,1,0:T(8,128)(2,1)}) custom-call(s32[3]{0:T(128)S(1)} %copy-done.7, bf16[96,1024]{1,0:T(8,128)(2,1)S(1)} %get-tuple-element.43.hidden_ref, bf16[96,1024]{1,0:T(8,128)(2,1)S(1)} %get-tuple-element.29.rows_dy.dy_ref, ...), custom_call_target="tpu_custom_call" | custom-call | flops 201326592 | bytes 10485760 | tf_op jit(solution)/shard_map/pallas_call | solution.py:370
  67.8 6.6 %all-to-all-done.1.back_ref = bf16[16,48,256]{2,1,0:T(8,128)(2,1)S(1)} async-done(((bf16[16,48,256]{2,1,0:T(8,128)(2,1)}), bf16[16,48,256]{2,1,0:T(8,128)(2,1)S(1)}, u32[]{:S(2)}, u32[]{:S(2)}) %all-to-all-start.1) | async-done | bytes 393248 | tf_op jit(solution)/shard_map/all_to_all | solution.py:366
  74.4 0.0 copy-done.5
  74.4 0.0 copy-done.6
  74.4 1.8 %shard_map.144 = (bf16[128,4096]{1,0:T(8,128)(2,1)}, bf16[128,4096]{1,0:T(8,128)(2,1)}) custom-call(f32[32,128]{1,0:T(8,128)S(1)} %copy-done.5, f32[32,128]{1,0:T(8,128)S(1)} %copy-done.6, bf16[16,48,256]{2,1,0:T(8,128)(2,1)S(1)} %all-to-all-done.1.back_ref), custom_call_target="tpu_custom_call" | custom-call | bytes 4194304 | tf_op jit(solution)/shard_map/pallas_call | solution.py:256
Async XLA Ops:
  0.6 23.5 %copy-start = (bf16[1,1024,1024]{2,1,0:T(8,128)(2,1)S(1)}, bf16[1,1024,1024]{2,1,0:T(8,128)(2,1)}, u32[]{:S(2)}) copy-start(bf16[1,1024,1024]{2,1,0:T(8,128)(2,1)} %refs_0_.1) | copy-start | bytes 6291460
  0.6 23.5 %copy-start.1 = (bf16[1,1024,1024]{2,1,0:T(8,128)(2,1)S(1)}, bf16[1,1024,1024]{2,1,0:T(8,128)(2,1)}, u32[]{:S(2)}) copy-start(bf16[1,1024,1024]{2,1,0:T(8,128)(2,1)} %refs_1_.1) | copy-start | bytes 6291460
  24.2 1.6 %copy-start.2 = (bf16[1,1024,1024]{2,1,0:T(8,128)(2,1)S(1)}, bf16[1,1024,1024]{2,1,0:T(8,128)(2,1)}, u32[]{:S(2)}) copy-start(bf16[1,1024,1024]{2,1,0:T(8,128)(2,1)} %refs_6_.1) | copy-start | bytes 6291460
  26.6 7.7 %collective-permute-start = (bf16[3,96,256]{2,1,0:T(8,128)(2,1)S(1)}, bf16[3,96,256]{2,1,0:T(8,128)(2,1)S(1)}, u32[]{:S(2)}, u32[]{:S(2)}) collective-permute-start(bf16[3,96,256]{2,1,0:T(8,128)(2,1)S(1)} %get-tuple-element.35), channel_id=1, source_target_pairs={{0,1},{1,0},{2,3},{3,2},{4,5},{5,4},{6,7},{7,6},{8,9},{9,8},{10,11... | collective-permute-start | bytes 442376 | tf_op jit(solution)/shard_map/ppermute | solution.py:313
  26.7 14.0 %collective-permute-start.1 = (bf16[3,96,256]{2,1,0:T(8,128)(2,1)S(1)}, bf16[3,96,256]{2,1,0:T(8,128)(2,1)S(1)}, u32[]{:S(2)}, u32[]{:S(2)}) collective-permute-start(bf16[3,96,256]{2,1,0:T(8,128)(2,1)S(1)} %get-tuple-element.36), channel_id=1, source_target_pairs={{0,2},{1,3},{2,0},{3,1},{4,6},{5,7},{6,4},{7,5},{8,10},{9,11},{10,... | collective-permute-start | bytes 442376 | tf_op jit(solution)/shard_map/ppermute | solution.py:313
  28.1 12.6 %collective-permute-start.2 = (bf16[3,96,256]{2,1,0:T(8,128)(2,1)S(1)}, bf16[3,96,256]{2,1,0:T(8,128)(2,1)S(1)}, u32[]{:S(2)}, u32[]{:S(2)}) collective-permute-start(bf16[3,96,256]{2,1,0:T(8,128)(2,1)S(1)} %get-tuple-element.37), channel_id=1, source_target_pairs={{0,3},{1,2},{2,1},{3,0},{4,7},{5,6},{6,5},{7,4},{8,11},{9,10},{10,... | collective-permute-start | bytes 442376 | tf_op jit(solution)/shard_map/ppermute | solution.py:313
  40.8 20.8 %copy-start.7 = (s32[3]{0:T(128)S(1)}, s32[3]{0:T(128)}, u32[]{:S(2)}) copy-start(s32[3]{0:T(128)} %selected_ref.1) | copy-start | bytes 40
  40.8 8.7 %collective-permute-start.5 = (bf16[3,96,256]{2,1,0:T(8,128)(2,1)S(1)}, bf16[3,96,256]{2,1,0:T(8,128)(2,1)S(1)}, u32[]{:S(2)}, u32[]{:S(2)}) collective-permute-start(bf16[3,96,256]{2,1,0:T(8,128)(2,1)S(1)} %shard_map.142.refs_0_), channel_id=1, source_target_pairs={{0,3},{1,2},{2,1},{3,0},{4,7},{5,6},{6,5},{7,4},{8,11},{9,10},{10,... | collective-permute-start | bytes 442376 | tf_op jit(solution)/shard_map/ppermute | solution.py:313
  42.3 13.4 %collective-permute-start.4 = (bf16[3,96,256]{2,1,0:T(8,128)(2,1)S(1)}, bf16[3,96,256]{2,1,0:T(8,128)(2,1)S(1)}, u32[]{:S(2)}, u32[]{:S(2)}) collective-permute-start(bf16[3,96,256]{2,1,0:T(8,128)(2,1)S(1)} %shard_map.142.refs_0_), channel_id=1, source_target_pairs={{0,2},{1,3},{2,0},{3,1},{4,6},{5,7},{6,4},{7,5},{8,10},{9,11},{10,... | collective-permute-start | bytes 442376 | tf_op jit(solution)/shard_map/ppermute | solution.py:313
  45.0 10.7 %collective-permute-start.3 = (bf16[3,96,256]{2,1,0:T(8,128)(2,1)S(1)}, bf16[3,96,256]{2,1,0:T(8,128)(2,1)S(1)}, u32[]{:S(2)}, u32[]{:S(2)}) collective-permute-start(bf16[3,96,256]{2,1,0:T(8,128)(2,1)S(1)} %shard_map.142.refs_0_), channel_id=1, source_target_pairs={{0,1},{1,0},{2,3},{3,2},{4,5},{5,4},{6,7},{7,6},{8,9},{9,8},{10,11... | collective-permute-start | bytes 442376 | tf_op jit(solution)/shard_map/ppermute | solution.py:313
  55.8 5.8 %copy-start.3 = (bf16[1,1024,1024]{2,1,0:T(8,128)(2,1)S(1)}, bf16[1,1024,1024]{2,1,0:T(8,128)(2,1)}, u32[]{:S(2)}) copy-start(bf16[1,1024,1024]{2,1,0:T(8,128)(2,1)} %first_ref.1) | copy-start | bytes 6291460
  57.9 16.5 %all-to-all-start.1 = ((bf16[16,48,256]{2,1,0:T(8,128)(2,1)}), bf16[16,48,256]{2,1,0:T(8,128)(2,1)S(1)}, u32[]{:S(2)}, u32[]{:S(2)}) async-start(bf16[16,48,256]{2,1,0:T(8,128)(2,1)} %get-tuple-element.40), calls=%async_computation.1 | async-start | bytes 786432 | tf_op jit(solution)/shard_map/all_to_all | solution.py:366
  61.6 1.6 %copy-start.4 = (bf16[1,1024,1024]{2,1,0:T(8,128)(2,1)S(1)}, bf16[1,1024,1024]{2,1,0:T(8,128)(2,1)}, u32[]{:S(2)}) copy-start(bf16[1,1024,1024]{2,1,0:T(8,128)(2,1)} %second_ref.1) | copy-start | bytes 6291460
  63.2 11.3 %copy-start.5 = (f32[32,128]{1,0:T(8,128)S(1)}, f32[32,128]{1,0:T(8,128)}, u32[]{:S(2)}) copy-start(f32[32,128]{1,0:T(8,128)} %get-tuple-element.26.ones_ref) | copy-start | bytes 49156
  63.2 11.3 %copy-start.6 = (f32[32,128]{1,0:T(8,128)S(1)}, f32[32,128]{1,0:T(8,128)}, u32[]{:S(2)}) copy-start(f32[32,128]{1,0:T(8,128)} %get-tuple-element.27.gates_ref) | copy-start | bytes 49156

commit v5 on v4

--- a/solution.py
+++ b/solution.py
@@ -22,9 +22,15 @@
 VMEM = pl.BlockSpec(memory_space=pltpu.VMEM)
 SMEM = pl.BlockSpec(memory_space=pltpu.SMEM)
 MIB = 1 << 20
+RS = (3, 2, 1)
+AG = (2, 1, 3)
 MOST = 58
 GF = 5 * 10**8
 GU = 3 * 10**8
+
+
+def turns(dp, order):
+    return order if dp == len(order) + 1 else tuple(range(1, dp))
 
 
 def iota(shape, dim):
@@ -190,13 +196,14 @@
 
 def result_kernel(dp, *refs):
     arrived = refs[:dp]
+    order = (0, *turns(dp, AG))
     gate_w, up_w, down_w, sent_ref, hidden_ref, full = refs[dp:]
     me = lax.axis_index("dp")
     block = arrived[0].shape[2]
-    for k in range(dp):
+    for i, k in enumerate(order):
         at = pl.multiple_of(jnp.bitwise_xor(me, k) * block, block)
-        hidden_ref[:, pl.ds(at, block)] = arrived[k][0]
-        full[:, :, pl.ds(at, block)] = arrived[k][1:]
+        hidden_ref[:, pl.ds(at, block)] = arrived[i][0]
+        full[:, :, pl.ds(at, block)] = arrived[i][1:]
     out = dot(hidden_ref[...], down_w[0])
     grad = dot(full[0], gate_w[...]) + dot(full[1], up_w[...])
     scatter_rows((out.astype(BF16), grad.astype(BF16)), sent_ref)
@@ -339,7 +346,7 @@
         flops=5 * 10**8,
         traffic=MIB // 8,
     )
-    sums = [own, *swaps(parts)]
+    sums = [own, *[swap(parts[k - 1], k) for k in turns(dp, RS)]]
     turned = call(
         turn_kernel,
         (shape((hidden_units, slice_width), BF16),) * 2,
@@ -354,7 +361,7 @@
         sums,
         traffic=MIB,
     )
-    shares = swaps([share] * (dp - 1))
+    shares = [swap(share, k) for k in turns(dp, AG)]
     results, hidden = call(
         functools.partial(result_kernel, dp),
         (shape((sources, LINES, width), BF16), shape((slots, hidden_units), BF16)),

time: 76.6 us -> 75.9 us (level)
  waiting for transfers between devices: 25.6 us -> 22.8 us
  Pallas kernels: 14.6 us -> 16.8 us
    all_to_all x1, waiting for transfers between devices: 6.65 us -> 4.4 us  [local(): lax.all_to_all(results, ('expert', 'dp'), split_axis=0, concat_axis=0, ti...]
    pallas_call x1, Pallas kernels: 4.61 us -> 6.81 us  [local(): pl.pallas_call(adam_kernel, grid=(hidden_units // strip,), in_specs=[SMEM...]
  transfers between devices with their start and end apart: 7 -> 7, of which waited for: 5 -> 6; matrix products, arithmetic and copies ran while one was open for 0% -> 0% of each run, Pallas kernels for 8% -> 11%
where the time goes in v5:
time: 75.9 us; the launch traced here: 75.5 us
  waiting for transfers between devices  22.8 us (30%)
  blocking collectives  20.3 us (27%)
  Pallas kernels  16.8 us (22%)
  starting transfers between devices  12.5 us (16%)
  local copies, waits for them, and re-layouts  2.4 us (3%)
  between operations  0.77 us (1%)
    all_to_all x1, blocking collectives, local(): lax.all_to_all(sent, ('expert', 'dp'), split_axis=0, concat_axis=0, tiled...  20.3 us
    ppermute x6, waiting for transfers between devices, swap(): return lax.ppermute(value, 'dp', [(i, i ^ k) for i in range(dp)])  18.4 us
    pallas_call x8, Pallas kernels, call(): pl.pallas_call(kernel, out_shape=outs, in_specs=in_specs or [VMEM] * len(...  10 us
    ppermute x6, starting transfers between devices, swap(): return lax.ppermute(value, 'dp', [(i, i ^ k) for i in range(dp)])  8.91 us
    pallas_call x1, Pallas kernels, local(): pl.pallas_call(adam_kernel, grid=(hidden_units // strip,), in_specs=[SMEM...  6.81 us
    all_to_all x1, waiting for transfers between devices, local(): lax.all_to_all(results, ('expert', 'dp'), split_axis=0, concat_axis=0, ti...  4.4 us
    all_to_all x1, starting transfers between devices, local(): lax.all_to_all(results, ('expert', 'dp'), split_axis=0, concat_axis=0, ti...  3.55 us
    unnamed x16, local copies, waits for them, and re-layouts  2.4 us
  transfers between devices with their start and end apart: 7, of which 6 were waited for; matrix products, arithmetic and copies ran while one was open for 0% of the time, Pallas kernels for 11%

profile of v5, /device:TPU:0, one launch (start us, length us, event | category | flops | bytes accessed | tf_op | source)
XLA Modules:
  0.0 75.5 jit_solution(7631283788729294707)
XLA Ops:
  0.6 0.0 copy-start
  0.6 0.0 copy-start.1
  0.7 2.8 %shard_map.137 = (bf16[16,48,256]{2,1,0:T(8,128)(2,1)}, f32[32,128]{1,0:T(8,128)}, f32[32,128]{1,0:T(8,128)}) custom-call(s32[8,128]{1,0:T(8,128)} %bitcast.2, s32[8,128]{1,0:T(8,128)} %bitcast.3, bf16[128,4096]{1,0:T(8,128)(2,1)} %tok_hbm.1, bf16[128,4096]{1,0:T(8,128)(2,1)} %cot_hbm.1), custom_call_target="tpu_custom_call" | custom-call | bytes 6291456 | tf_op jit(solution)/shard_map/pallas_call | solution.py:263
  3.5 20.3 %all_to_all.10.arrived_ref = bf16[16,48,256]{2,1,0:T(8,128)(2,1)S(1)} all-to-all(bf16[16,48,256]{2,1,0:T(8,128)(2,1)} %get-tuple-element.28), channel_id=1, replica_groups=mesh['groups'=2,'expert'=4,'dp'=4] {'expert','dp'}, dimensions={0} | all-to-all | bytes 786432 | tf_op jit(solution)/shard_map/all_to_all | solution.py:318
  23.8 0.4 shard_map.138
  24.1 0.0 copy-done
  24.1 0.0 copy-done.1
  24.2 0.0 copy-start.2
  24.2 0.8 %shard_map.139.pre_ref = f32[2,96,1024]{2,1,0:T(8,128)S(1)} custom-call(bf16[96,1024]{1,0:T(8,128)(2,1)S(1)} %get-tuple-element.30.rows_x, bf16[1,1024,1024]{2,1,0:T(8,128)(2,1)S(1)} %copy-done, bf16[1,1024,1024]{2,1,0:T(8,128)(2,1)S(1)} %copy-done.1), custom_call_target="tpu_custom_call" | custom-call | flops 300000000 | bytes 131072 | tf_op jit(solution)/shard_map/pallas_call | solution.py:263
  25.0 0.8 %copy-done.2 = bf16[1,1024,1024]{2,1,0:T(8,128)(2,1)S(1)} copy-done((bf16[1,1024,1024]{2,1,0:T(8,128)(2,1)S(1)}, bf16[1,1024,1024]{2,1,0:T(8,128)(2,1)}, u32[]{:S(2)}) %copy-start.2) | copy-done | bytes 2097176
  25.8 0.8 %shard_map.140 = (f32[3,96,256]{2,1,0:T(8,128)S(1)}, bf16[3,96,256]{2,1,0:T(8,128)(2,1)S(1)}, bf16[3,96,256]{2,1,0:T(8,128)(2,1)S(1)}, bf16[3,96,256]{2,1,0:T(8,128)(2,1)S(1)}) custom-call(bf16[96,1024]{1,0:T(8,128)(2,1)S(1)} %get-tuple-element.29.rows_dy.dy_ref, f32[2,96,1024]{2,1,0:T(8,128)S(1)} %shard_map.139.pre_ref, bf16[1,1024,1024]{2,1,0:T(8,128)(2,1)S(1)} %copy-done.2), custom_call_target="tpu_custom_call" | custom-call | flops 500000000 | bytes 131072 | tf_op jit(solution)/shard_map/pallas_call | solution.py:263
  26.6 1.0 %collective-permute-start = (bf16[3,96,256]{2,1,0:T(8,128)(2,1)S(1)}, bf16[3,96,256]{2,1,0:T(8,128)(2,1)S(1)}, u32[]{:S(2)}, u32[]{:S(2)}) collective-permute-start(bf16[3,96,256]{2,1,0:T(8,128)(2,1)S(1)} %get-tuple-element.35), channel_id=1, source_target_pairs={{0,3},{1,2},{2,1},{3,0},{4,7},{5,6},{6,5},{7,4},{8,11},{9,10},{10,... | collective-permute-start | bytes 442376 | tf_op jit(solution)/shard_map/ppermute | solution.py:320
  27.5 0.5 collective-permute-start.1
  28.0 3.0 %collective-permute-start.2 = (bf16[3,96,256]{2,1,0:T(8,128)(2,1)S(1)}, bf16[3,96,256]{2,1,0:T(8,128)(2,1)S(1)}, u32[]{:S(2)}, u32[]{:S(2)}) collective-permute-start(bf16[3,96,256]{2,1,0:T(8,128)(2,1)S(1)} %get-tuple-element.37), channel_id=1, source_target_pairs={{0,1},{1,0},{2,3},{3,2},{4,5},{5,4},{6,7},{7,6},{8,9},{9,8},{10,11... | collective-permute-start | bytes 442376 | tf_op jit(solution)/shard_map/ppermute | solution.py:320
  31.0 1.2 %shard_map.141 = (bf16[1024,1024]{1,0:T(8,128)(2,1)S(1)}, bf16[1024,1024]{1,0:T(8,128)(2,1)S(1)}) custom-call(bf16[1,1024,1024]{2,1,0:T(8,128)(2,1)S(1)} %copy-done, bf16[1,1024,1024]{2,1,0:T(8,128)(2,1)S(1)} %copy-done.1), custom_call_target="tpu_custom_call" | custom-call | bytes 4194304 | tf_op jit(solution)/shard_map/pallas_call | solution.py:263
  32.3 3.0 %collective-permute-done.refs_1_ = bf16[3,96,256]{2,1,0:T(8,128)(2,1)S(1)} collective-permute-done((bf16[3,96,256]{2,1,0:T(8,128)(2,1)S(1)}, bf16[3,96,256]{2,1,0:T(8,128)(2,1)S(1)}, u32[]{:S(2)}, u32[]{:S(2)}) %collective-permute-start) | collective-permute-done | bytes 147488 | tf_op jit(solution)/shard_map/ppermute | solution.py:320
  35.3 6.3 %collective-permute-done.1.refs_2_ = bf16[3,96,256]{2,1,0:T(8,128)(2,1)S(1)} collective-permute-done((bf16[3,96,256]{2,1,0:T(8,128)(2,1)S(1)}, bf16[3,96,256]{2,1,0:T(8,128)(2,1)S(1)}, u32[]{:S(2)}, u32[]{:S(2)}) %collective-permute-start.1) | collective-permute-done | bytes 147488 | tf_op jit(solution)/shard_map/ppermute | solution.py:320
  41.6 0.0 collective-permute-done.2.refs_3_
  41.6 0.1 shard_map.142.refs_0_
  41.7 0.0 copy-start.7
  41.7 1.7 %collective-permute-start.5 = (bf16[3,96,256]{2,1,0:T(8,128)(2,1)S(1)}, bf16[3,96,256]{2,1,0:T(8,128)(2,1)S(1)}, u32[]{:S(2)}, u32[]{:S(2)}) collective-permute-start(bf16[3,96,256]{2,1,0:T(8,128)(2,1)S(1)} %shard_map.142.refs_0_), channel_id=1, source_target_pairs={{0,3},{1,2},{2,1},{3,0},{4,7},{5,6},{6,5},{7,4},{8,11},{9,10},{10,... | collective-permute-start | bytes 442376 | tf_op jit(solution)/shard_map/ppermute | solution.py:320
  43.4 0.0 collective-permute-start.4
  43.4 2.8 %collective-permute-start.3 = (bf16[3,96,256]{2,1,0:T(8,128)(2,1)S(1)}, bf16[3,96,256]{2,1,0:T(8,128)(2,1)S(1)}, u32[]{:S(2)}, u32[]{:S(2)}) collective-permute-start(bf16[3,96,256]{2,1,0:T(8,128)(2,1)S(1)} %shard_map.142.refs_0_), channel_id=1, source_target_pairs={{0,2},{1,3},{2,0},{3,1},{4,6},{5,7},{6,4},{7,5},{8,10},{9,11},{10,... | collective-permute-start | bytes 442376 | tf_op jit(solution)/shard_map/ppermute | solution.py:320
  46.2 4.2 %collective-permute-done.5.refs_3_ = bf16[3,96,256]{2,1,0:T(8,128)(2,1)S(1)} collective-permute-done((bf16[3,96,256]{2,1,0:T(8,128)(2,1)S(1)}, bf16[3,96,256]{2,1,0:T(8,128)(2,1)S(1)}, u32[]{:S(2)}, u32[]{:S(2)}) %collective-permute-start.5) | collective-permute-done | bytes 147488 | tf_op jit(solution)/shard_map/ppermute | solution.py:320
  50.4 4.3 %collective-permute-done.4.refs_2_ = bf16[3,96,256]{2,1,0:T(8,128)(2,1)S(1)} collective-permute-done((bf16[3,96,256]{2,1,0:T(8,128)(2,1)S(1)}, bf16[3,96,256]{2,1,0:T(8,128)(2,1)S(1)}, u32[]{:S(2)}, u32[]{:S(2)}) %collective-permute-start.4) | collective-permute-done | bytes 147488 | tf_op jit(solution)/shard_map/ppermute | solution.py:320
  54.7 0.5 collective-permute-done.3.refs_1_
  55.2 0.0 copy-start.3
  55.2 2.1 %shard_map.143 = (bf16[16,48,256]{2,1,0:T(8,128)(2,1)}, bf16[96,1024]{1,0:T(8,128)(2,1)S(1)}) custom-call(bf16[3,96,256]{2,1,0:T(8,128)(2,1)S(1)} %shard_map.142.refs_0_, bf16[3,96,256]{2,1,0:T(8,128)(2,1)S(1)} %collective-permute-done.3.refs_1_, bf16[3,96,256]{2,1,0:T(8,128)(2,1)S(1)} %collective-permute-done.4.refs_2_, ...), custom_call_target="tpu_custom_call" | custom-call | flops 603979776 | bytes 8388608 | tf_op jit(solution)/shard_map/pallas_call | solution.py:263
  57.4 3.6 %all-to-all-start.1 = ((bf16[16,48,256]{2,1,0:T(8,128)(2,1)}), bf16[16,48,256]{2,1,0:T(8,128)(2,1)S(1)}, u32[]{:S(2)}, u32[]{:S(2)}) async-start(bf16[16,48,256]{2,1,0:T(8,128)(2,1)} %get-tuple-element.40), calls=%async_computation.1 | async-start | bytes 786432 | tf_op jit(solution)/shard_map/all_to_all | solution.py:373
  60.9 0.0 copy-done.7
  60.9 0.0 copy-done.3
  60.9 0.0 copy-start.4
  61.0 1.6 %copy-done.4 = bf16[1,1024,1024]{2,1,0:T(8,128)(2,1)S(1)} copy-done((bf16[1,1024,1024]{2,1,0:T(8,128)(2,1)S(1)}, bf16[1,1024,1024]{2,1,0:T(8,128)(2,1)}, u32[]{:S(2)}) %copy-start.4) | copy-done | bytes 2097176
  62.5 0.0 copy-start.5
  62.5 0.0 copy-start.6
  62.5 6.8 %shard_map.145 = (bf16[1,1024,1024]{2,1,0:T(8,128)(2,1)}, bf16[1,1024,1024]{2,1,0:T(8,128)(2,1)}, bf16[1,1024,1024]{2,1,0:T(8,128)(2,1)}) custom-call(s32[3]{0:T(128)S(1)} %copy-done.7, bf16[96,1024]{1,0:T(8,128)(2,1)S(1)} %get-tuple-element.43.hidden_ref, bf16[96,1024]{1,0:T(8,128)(2,1)S(1)} %get-tuple-element.29.rows_dy.dy_ref, ...), custom_call_target="tpu_custom_call" | custom-call | flops 201326592 | bytes 10485760 | tf_op jit(solution)/shard_map/pallas_call | solution.py:377
  69.4 4.4 %all-to-all-done.1.back_ref = bf16[16,48,256]{2,1,0:T(8,128)(2,1)S(1)} async-done(((bf16[16,48,256]{2,1,0:T(8,128)(2,1)}), bf16[16,48,256]{2,1,0:T(8,128)(2,1)S(1)}, u32[]{:S(2)}, u32[]{:S(2)}) %all-to-all-start.1) | async-done | bytes 393248 | tf_op jit(solution)/shard_map/all_to_all | solution.py:373
  73.8 0.0 copy-done.5
  73.8 0.0 copy-done.6
  73.8 1.8 %shard_map.144 = (bf16[128,4096]{1,0:T(8,128)(2,1)}, bf16[128,4096]{1,0:T(8,128)(2,1)}) custom-call(f32[32,128]{1,0:T(8,128)S(1)} %copy-done.5, f32[32,128]{1,0:T(8,128)S(1)} %copy-done.6, bf16[16,48,256]{2,1,0:T(8,128)(2,1)S(1)} %all-to-all-done.1.back_ref), custom_call_target="tpu_custom_call" | custom-call | bytes 4194304 | tf_op jit(solution)/shard_map/pallas_call | solution.py:263
Async XLA Ops:
  0.6 23.5 %copy-start = (bf16[1,1024,1024]{2,1,0:T(8,128)(2,1)S(1)}, bf16[1,1024,1024]{2,1,0:T(8,128)(2,1)}, u32[]{:S(2)}) copy-start(bf16[1,1024,1024]{2,1,0:T(8,128)(2,1)} %refs_0_.1) | copy-start | bytes 6291460
  0.6 23.5 %copy-start.1 = (bf16[1,1024,1024]{2,1,0:T(8,128)(2,1)S(1)}, bf16[1,1024,1024]{2,1,0:T(8,128)(2,1)}, u32[]{:S(2)}) copy-start(bf16[1,1024,1024]{2,1,0:T(8,128)(2,1)} %refs_1_.1) | copy-start | bytes 6291460
  24.2 1.6 %copy-start.2 = (bf16[1,1024,1024]{2,1,0:T(8,128)(2,1)S(1)}, bf16[1,1024,1024]{2,1,0:T(8,128)(2,1)}, u32[]{:S(2)}) copy-start(bf16[1,1024,1024]{2,1,0:T(8,128)(2,1)} %refs_6_.1) | copy-start | bytes 6291460
  26.6 8.7 %collective-permute-start = (bf16[3,96,256]{2,1,0:T(8,128)(2,1)S(1)}, bf16[3,96,256]{2,1,0:T(8,128)(2,1)S(1)}, u32[]{:S(2)}, u32[]{:S(2)}) collective-permute-start(bf16[3,96,256]{2,1,0:T(8,128)(2,1)S(1)} %get-tuple-element.35), channel_id=1, source_target_pairs={{0,3},{1,2},{2,1},{3,0},{4,7},{5,6},{6,5},{7,4},{8,11},{9,10},{10,... | collective-permute-start | bytes 442376 | tf_op jit(solution)/shard_map/ppermute | solution.py:320
  27.5 14.1 %collective-permute-start.1 = (bf16[3,96,256]{2,1,0:T(8,128)(2,1)S(1)}, bf16[3,96,256]{2,1,0:T(8,128)(2,1)S(1)}, u32[]{:S(2)}, u32[]{:S(2)}) collective-permute-start(bf16[3,96,256]{2,1,0:T(8,128)(2,1)S(1)} %get-tuple-element.36), channel_id=1, source_target_pairs={{0,2},{1,3},{2,0},{3,1},{4,6},{5,7},{6,4},{7,5},{8,10},{9,11},{10,... | collective-permute-start | bytes 442376 | tf_op jit(solution)/shard_map/ppermute | solution.py:320
  28.0 13.6 %collective-permute-start.2 = (bf16[3,96,256]{2,1,0:T(8,128)(2,1)S(1)}, bf16[3,96,256]{2,1,0:T(8,128)(2,1)S(1)}, u32[]{:S(2)}, u32[]{:S(2)}) collective-permute-start(bf16[3,96,256]{2,1,0:T(8,128)(2,1)S(1)} %get-tuple-element.37), channel_id=1, source_target_pairs={{0,1},{1,0},{2,3},{3,2},{4,5},{5,4},{6,7},{7,6},{8,9},{9,8},{10,11... | collective-permute-start | bytes 442376 | tf_op jit(solution)/shard_map/ppermute | solution.py:320
  41.7 19.2 %copy-start.7 = (s32[3]{0:T(128)S(1)}, s32[3]{0:T(128)}, u32[]{:S(2)}) copy-start(s32[3]{0:T(128)} %selected_ref.1) | copy-start | bytes 40
  41.7 8.7 %collective-permute-start.5 = (bf16[3,96,256]{2,1,0:T(8,128)(2,1)S(1)}, bf16[3,96,256]{2,1,0:T(8,128)(2,1)S(1)}, u32[]{:S(2)}, u32[]{:S(2)}) collective-permute-start(bf16[3,96,256]{2,1,0:T(8,128)(2,1)S(1)} %shard_map.142.refs_0_), channel_id=1, source_target_pairs={{0,3},{1,2},{2,1},{3,0},{4,7},{5,6},{6,5},{7,4},{8,11},{9,10},{10,... | collective-permute-start | bytes 442376 | tf_op jit(solution)/shard_map/ppermute | solution.py:320
  43.4 11.3 %collective-permute-start.4 = (bf16[3,96,256]{2,1,0:T(8,128)(2,1)S(1)}, bf16[3,96,256]{2,1,0:T(8,128)(2,1)S(1)}, u32[]{:S(2)}, u32[]{:S(2)}) collective-permute-start(bf16[3,96,256]{2,1,0:T(8,128)(2,1)S(1)} %shard_map.142.refs_0_), channel_id=1, source_target_pairs={{0,1},{1,0},{2,3},{3,2},{4,5},{5,4},{6,7},{7,6},{8,9},{9,8},{10,11... | collective-permute-start | bytes 442376 | tf_op jit(solution)/shard_map/ppermute | solution.py:320
  43.4 11.8 %collective-permute-start.3 = (bf16[3,96,256]{2,1,0:T(8,128)(2,1)S(1)}, bf16[3,96,256]{2,1,0:T(8,128)(2,1)S(1)}, u32[]{:S(2)}, u32[]{:S(2)}) collective-permute-start(bf16[3,96,256]{2,1,0:T(8,128)(2,1)S(1)} %shard_map.142.refs_0_), channel_id=1, source_target_pairs={{0,2},{1,3},{2,0},{3,1},{4,6},{5,7},{6,4},{7,5},{8,10},{9,11},{10,... | collective-permute-start | bytes 442376 | tf_op jit(solution)/shard_map/ppermute | solution.py:320
  55.2 5.7 %copy-start.3 = (bf16[1,1024,1024]{2,1,0:T(8,128)(2,1)S(1)}, bf16[1,1024,1024]{2,1,0:T(8,128)(2,1)}, u32[]{:S(2)}) copy-start(bf16[1,1024,1024]{2,1,0:T(8,128)(2,1)} %first_ref.1) | copy-start | bytes 6291460
  57.4 16.4 %all-to-all-start.1 = ((bf16[16,48,256]{2,1,0:T(8,128)(2,1)}), bf16[16,48,256]{2,1,0:T(8,128)(2,1)S(1)}, u32[]{:S(2)}, u32[]{:S(2)}) async-start(bf16[16,48,256]{2,1,0:T(8,128)(2,1)} %get-tuple-element.40), calls=%async_computation.1 | async-start | bytes 786432 | tf_op jit(solution)/shard_map/all_to_all | solution.py:373
  60.9 1.6 %copy-start.4 = (bf16[1,1024,1024]{2,1,0:T(8,128)(2,1)S(1)}, bf16[1,1024,1024]{2,1,0:T(8,128)(2,1)}, u32[]{:S(2)}) copy-start(bf16[1,1024,1024]{2,1,0:T(8,128)(2,1)} %second_ref.1) | copy-start | bytes 6291460
  62.5 11.2 %copy-start.5 = (f32[32,128]{1,0:T(8,128)S(1)}, f32[32,128]{1,0:T(8,128)}, u32[]{:S(2)}) copy-start(f32[32,128]{1,0:T(8,128)} %get-tuple-element.26.ones_ref) | copy-start | bytes 49156
  62.5 11.2 %copy-start.6 = (f32[32,128]{1,0:T(8,128)S(1)}, f32[32,128]{1,0:T(8,128)}, u32[]{:S(2)}) copy-start(f32[32,128]{1,0:T(8,128)} %get-tuple-element.27.gates_ref) | copy-start | bytes 49156

commit v6 on v5

--- a/solution.py
+++ b/solution.py
@@ -231,27 +231,28 @@
         two_ref[...] = second_ref[...]
 
 
-def combine_kernel(
-    experts, dp, ones_ref, gates_ref, back_ref, mixed_hbm, grad_hbm, mixed_ref, grad_ref, sems
-):
-    width = back_ref.shape[2]
+def spread_kernel(experts, ones_ref, gates_ref, spread_ref):
     small = (experts * 8, experts * LINES)
     source, target = iota(small, 0), iota(small, 1)
     same = (source // 8 == target // LINES) & (source % 8 < CAP)
     within = target % LINES - source % 8
-    spreads = []
-    for half, ref in ((0, gates_ref), (1, ones_ref)):
+    for half, ref in enumerate((gates_ref, ones_ref)):
         weights = ref[...].astype(BF16)
         for c in range(CHUNKS):
             spot = same & (within == half * HALF + c * CAP)
-            spreads.append(dot(weights, spot.astype(F32).astype(BF16), ((0,), (0,))).astype(BF16))
+            spread = dot(weights, spot.astype(F32).astype(BF16), ((0,), (0,)))
+            spread_ref[half * CHUNKS + c] = spread.astype(BF16)
+
+
+def combine_kernel(experts, dp, spread_ref, back_ref, mixed_hbm, grad_hbm, mixed_ref, grad_ref, sems):
+    width = back_ref.shape[2]
     copies = []
     for j in range(dp):
         lines = jnp.concatenate([back_ref[e * dp + j] for e in range(experts)], axis=0)
         for half, ref, hbm in ((0, mixed_ref, mixed_hbm), (1, grad_ref, grad_hbm)):
             for c in range(CHUNKS):
                 at = (j * CHUNKS + c) * width
-                ref[:, at : at + width] = dot(spreads[half * CHUNKS + c], lines).astype(BF16)
+                ref[:, at : at + width] = dot(spread_ref[half * CHUNKS + c], lines).astype(BF16)
             span = pl.ds(j * CHUNKS * width, CHUNKS * width)
             copies.append(pltpu.make_async_copy(ref.at[:, span], hbm.at[:, span], sems.at[half, j]))
             copies[-1].start()
@@ -353,7 +354,13 @@
         (gate_weight, up_weight),
         traffic=4 * MIB,
     )
-    own, *turned = lax.optimization_barrier((own, *turned))
+    spread = call(
+        functools.partial(spread_kernel, experts),
+        shape((2 * CHUNKS, tok_rows, experts * LINES), BF16),
+        (ones, gates),
+        traffic=MIB // 2,
+    )
+    own, spread, *turned = lax.optimization_barrier((own, spread, *turned))
     sums[0] = own
     share = call(
         share_kernel,
@@ -395,7 +402,7 @@
     mixed, input_grad = call(
         functools.partial(combine_kernel, experts, dp),
         (shape((tok_rows, model), BF16), shape((tok_rows, model), BF16)),
-        (ones, gates, back),
+        (spread, back),
         out_specs=(own_specs[0],) * 2,
         scratch=[
             pltpu.VMEM((tok_rows, model), BF16),

time: 75.9 us -> 75.7 us (level)
  Pallas kernels: 16.8 us -> 14 us
  waiting for transfers between devices: 22.8 us -> 24.7 us
    all_to_all x1, waiting for transfers between devices: 4.4 us -> 6.6 us  [local(): lax.all_to_all(results, ('expert', 'dp'), split_axis=0, concat_axis=0, ti...]
    pallas_call x1, Pallas kernels: 6.81 us -> 4.61 us  [local(): pl.pallas_call(adam_kernel, grid=(hidden_units // strip,), in_specs=[SMEM...]
    unnamed x16 -> x18, local copies, waits for them, and re-layouts: 2.4 us -> 3.14 us
    pallas_call x8 -> x9, Pallas kernels: 10 us -> 9.42 us  [call(): pl.pallas_call(kernel, out_shape=outs, in_specs=in_specs or [VMEM] * len(...]
  transfers between devices with their start and end apart: 7 -> 7, of which waited for: 6 -> 6; matrix products, arithmetic and copies ran while one was open for 0% -> 0% of each run, Pallas kernels for 11% -> 8%
where the time goes in v6:
time: 75.7 us; the launch traced here: 75.4 us
  waiting for transfers between devices  24.7 us (33%)
  blocking collectives  20.3 us (27%)
  Pallas kernels  14 us (18%)
  starting transfers between devices  12.5 us (17%)
  local copies, waits for them, and re-layouts  3.14 us (4%)
  between operations  0.8 us (1%)
    all_to_all x1, blocking collectives, local(): lax.all_to_all(sent, ('expert', 'dp'), split_axis=0, concat_axis=0, tiled...  20.3 us
    ppermute x6, waiting for transfers between devices, swap(): return lax.ppermute(value, 'dp', [(i, i ^ k) for i in range(dp)])  18 us
    pallas_call x9, Pallas kernels, call(): pl.pallas_call(kernel, out_shape=outs, in_specs=in_specs or [VMEM] * len(...  9.42 us
    ppermute x6, starting transfers between devices, swap(): return lax.ppermute(value, 'dp', [(i, i ^ k) for i in range(dp)])  8.91 us
    all_to_all x1, waiting for transfers between devices, local(): lax.all_to_all(results, ('expert', 'dp'), split_axis=0, concat_axis=0, ti...  6.6 us
    pallas_call x1, Pallas kernels, local(): pl.pallas_call(adam_kernel, grid=(hidden_units // strip,), in_specs=[SMEM...  4.61 us
    all_to_all x1, starting transfers between devices, local(): lax.all_to_all(results, ('expert', 'dp'), split_axis=0, concat_axis=0, ti...  3.55 us
    unnamed x18, local copies, waits for them, and re-layouts  3.14 us
  transfers between devices with their start and end apart: 7, of which 6 were waited for; matrix products, arithmetic and copies ran while one was open for 0% of the time, Pallas kernels for 8%

profile of v6, /device:TPU:0, one launch (start us, length us, event | category | flops | bytes accessed | tf_op | source)
XLA Modules:
  0.0 75.4 jit_solution(733632118865667749)
XLA Ops:
  0.6 0.0 copy-start
  0.6 0.0 copy-start.1
  0.7 2.8 %shard_map.137 = (bf16[16,48,256]{2,1,0:T(8,128)(2,1)}, f32[32,128]{1,0:T(8,128)}, f32[32,128]{1,0:T(8,128)}) custom-call(s32[8,128]{1,0:T(8,128)} %bitcast.2, s32[8,128]{1,0:T(8,128)} %bitcast.3, bf16[128,4096]{1,0:T(8,128)(2,1)} %tok_hbm.1, bf16[128,4096]{1,0:T(8,128)(2,1)} %cot_hbm.1), custom_call_target="tpu_custom_call" | custom-call | bytes 6291456 | tf_op jit(solution)/shard_map/pallas_call | solution.py:264
  3.5 20.3 %all_to_all.10.arrived_ref = bf16[16,48,256]{2,1,0:T(8,128)(2,1)S(1)} all-to-all(bf16[16,48,256]{2,1,0:T(8,128)(2,1)} %get-tuple-element.27), channel_id=1, replica_groups=mesh['groups'=2,'expert'=4,'dp'=4] {'expert','dp'}, dimensions={0} | all-to-all | bytes 786432 | tf_op jit(solution)/shard_map/all_to_all | solution.py:319
  23.8 0.4 shard_map.138
  24.1 0.0 copy-done
  24.1 0.0 copy-done.1
  24.2 0.0 copy-start.2
  24.2 0.8 %shard_map.139.pre_ref = f32[2,96,1024]{2,1,0:T(8,128)S(1)} custom-call(bf16[96,1024]{1,0:T(8,128)(2,1)S(1)} %get-tuple-element.29.rows_x, bf16[1,1024,1024]{2,1,0:T(8,128)(2,1)S(1)} %copy-done, bf16[1,1024,1024]{2,1,0:T(8,128)(2,1)S(1)} %copy-done.1), custom_call_target="tpu_custom_call" | custom-call | flops 300000000 | bytes 131072 | tf_op jit(solution)/shard_map/pallas_call | solution.py:264
  25.0 0.8 %copy-done.2 = bf16[1,1024,1024]{2,1,0:T(8,128)(2,1)S(1)} copy-done((bf16[1,1024,1024]{2,1,0:T(8,128)(2,1)S(1)}, bf16[1,1024,1024]{2,1,0:T(8,128)(2,1)}, u32[]{:S(2)}) %copy-start.2) | copy-done | bytes 2097176
  25.8 0.8 %shard_map.140 = (f32[3,96,256]{2,1,0:T(8,128)S(1)}, bf16[3,96,256]{2,1,0:T(8,128)(2,1)S(1)}, bf16[3,96,256]{2,1,0:T(8,128)(2,1)S(1)}, bf16[3,96,256]{2,1,0:T(8,128)(2,1)S(1)}) custom-call(bf16[96,1024]{1,0:T(8,128)(2,1)S(1)} %get-tuple-element.28.rows_dy.dy_ref, f32[2,96,1024]{2,1,0:T(8,128)S(1)} %shard_map.139.pre_ref, bf16[1,1024,1024]{2,1,0:T(8,128)(2,1)S(1)} %copy-done.2), custom_call_target="tpu_custom_call" | custom-call | flops 500000000 | bytes 131072 | tf_op jit(solution)/shard_map/pallas_call | solution.py:264
  26.6 1.0 %collective-permute-start = (bf16[3,96,256]{2,1,0:T(8,128)(2,1)S(1)}, bf16[3,96,256]{2,1,0:T(8,128)(2,1)S(1)}, u32[]{:S(2)}, u32[]{:S(2)}) collective-permute-start(bf16[3,96,256]{2,1,0:T(8,128)(2,1)S(1)} %get-tuple-element.37), channel_id=1, source_target_pairs={{0,3},{1,2},{2,1},{3,0},{4,7},{5,6},{6,5},{7,4},{8,11},{9,10},{10,... | collective-permute-start | bytes 442376 | tf_op jit(solution)/shard_map/ppermute | solution.py:321
  27.5 0.5 collective-permute-start.1
  28.0 0.0 copy-start.6
  28.0 0.0 copy-start.7
  28.0 3.0 %collective-permute-start.2 = (bf16[3,96,256]{2,1,0:T(8,128)(2,1)S(1)}, bf16[3,96,256]{2,1,0:T(8,128)(2,1)S(1)}, u32[]{:S(2)}, u32[]{:S(2)}) collective-permute-start(bf16[3,96,256]{2,1,0:T(8,128)(2,1)S(1)} %get-tuple-element.39), channel_id=1, source_target_pairs={{0,1},{1,0},{2,3},{3,2},{4,5},{5,4},{6,7},{7,6},{8,9},{9,8},{10,11... | collective-permute-start | bytes 442376 | tf_op jit(solution)/shard_map/ppermute | solution.py:321
  31.0 1.2 %shard_map.142 = (bf16[1024,1024]{1,0:T(8,128)(2,1)S(1)}, bf16[1024,1024]{1,0:T(8,128)(2,1)S(1)}) custom-call(bf16[1,1024,1024]{2,1,0:T(8,128)(2,1)S(1)} %copy-done, bf16[1,1024,1024]{2,1,0:T(8,128)(2,1)S(1)} %copy-done.1), custom_call_target="tpu_custom_call" | custom-call | bytes 4194304 | tf_op jit(solution)/shard_map/pallas_call | solution.py:264
  32.3 0.0 copy-done.6
  32.3 0.0 copy-done.7
  32.3 0.3 shard_map.141.spread_ref
  32.6 2.7 %collective-permute-done.refs_1_ = bf16[3,96,256]{2,1,0:T(8,128)(2,1)S(1)} collective-permute-done((bf16[3,96,256]{2,1,0:T(8,128)(2,1)S(1)}, bf16[3,96,256]{2,1,0:T(8,128)(2,1)S(1)}, u32[]{:S(2)}, u32[]{:S(2)}) %collective-permute-start) | collective-permute-done | bytes 147488 | tf_op jit(solution)/shard_map/ppermute | solution.py:321
  35.3 6.3 %collective-permute-done.1.refs_2_ = bf16[3,96,256]{2,1,0:T(8,128)(2,1)S(1)} collective-permute-done((bf16[3,96,256]{2,1,0:T(8,128)(2,1)S(1)}, bf16[3,96,256]{2,1,0:T(8,128)(2,1)S(1)}, u32[]{:S(2)}, u32[]{:S(2)}) %collective-permute-start.1) | collective-permute-done | bytes 147488 | tf_op jit(solution)/shard_map/ppermute | solution.py:321
  41.6 0.0 collective-permute-done.2.refs_3_
  41.6 0.1 shard_map.143.refs_0_
  41.7 0.0 copy-start.8
  41.7 1.7 %collective-permute-start.5 = (bf16[3,96,256]{2,1,0:T(8,128)(2,1)S(1)}, bf16[3,96,256]{2,1,0:T(8,128)(2,1)S(1)}, u32[]{:S(2)}, u32[]{:S(2)}) collective-permute-start(bf16[3,96,256]{2,1,0:T(8,128)(2,1)S(1)} %shard_map.143.refs_0_), channel_id=1, source_target_pairs={{0,3},{1,2},{2,1},{3,0},{4,7},{5,6},{6,5},{7,4},{8,11},{9,10},{10,... | collective-permute-start | bytes 442376 | tf_op jit(solution)/shard_map/ppermute | solution.py:321
  43.4 0.0 collective-permute-start.4
  43.4 2.8 %collective-permute-start.3 = (bf16[3,96,256]{2,1,0:T(8,128)(2,1)S(1)}, bf16[3,96,256]{2,1,0:T(8,128)(2,1)S(1)}, u32[]{:S(2)}, u32[]{:S(2)}) collective-permute-start(bf16[3,96,256]{2,1,0:T(8,128)(2,1)S(1)} %shard_map.143.refs_0_), channel_id=1, source_target_pairs={{0,2},{1,3},{2,0},{3,1},{4,6},{5,7},{6,4},{7,5},{8,10},{9,11},{10,... | collective-permute-start | bytes 442376 | tf_op jit(solution)/shard_map/ppermute | solution.py:321
  46.2 4.2 %collective-permute-done.5.refs_3_ = bf16[3,96,256]{2,1,0:T(8,128)(2,1)S(1)} collective-permute-done((bf16[3,96,256]{2,1,0:T(8,128)(2,1)S(1)}, bf16[3,96,256]{2,1,0:T(8,128)(2,1)S(1)}, u32[]{:S(2)}, u32[]{:S(2)}) %collective-permute-start.5) | collective-permute-done | bytes 147488 | tf_op jit(solution)/shard_map/ppermute | solution.py:321
  50.4 4.3 %collective-permute-done.4.refs_2_ = bf16[3,96,256]{2,1,0:T(8,128)(2,1)S(1)} collective-permute-done((bf16[3,96,256]{2,1,0:T(8,128)(2,1)S(1)}, bf16[3,96,256]{2,1,0:T(8,128)(2,1)S(1)}, u32[]{:S(2)}, u32[]{:S(2)}) %collective-permute-start.4) | collective-permute-done | bytes 147488 | tf_op jit(solution)/shard_map/ppermute | solution.py:321
  54.7 0.5 collective-permute-done.3.refs_1_
  55.2 0.0 copy-start.3
  55.2 1.4 %shard_map.144 = (bf16[16,48,256]{2,1,0:T(8,128)(2,1)S(1)}, bf16[96,1024]{1,0:T(8,128)(2,1)S(1)}) custom-call(bf16[3,96,256]{2,1,0:T(8,128)(2,1)S(1)} %shard_map.143.refs_0_, bf16[3,96,256]{2,1,0:T(8,128)(2,1)S(1)} %collective-permute-done.3.refs_1_, bf16[3,96,256]{2,1,0:T(8,128)(2,1)S(1)} %collective-permute-done.4.refs_2_, ...), custom_call_target="tpu_custom_call" | custom-call | flops 603979776 | bytes 8388608 | tf_op jit(solution)/shard_map/pallas_call | solution.py:264
  56.6 0.0 copy-start.5
  56.6 0.7 copy-done.5
  57.4 3.6 %all-to-all-start.1 = ((bf16[16,48,256]{2,1,0:T(8,128)(2,1)}), bf16[16,48,256]{2,1,0:T(8,128)(2,1)S(1)}, u32[]{:S(2)}, u32[]{:S(2)}) async-start(bf16[16,48,256]{2,1,0:T(8,128)(2,1)} %copy-done.5), calls=%async_computation.1 | async-start | bytes 786432 | tf_op jit(solution)/shard_map/all_to_all | solution.py:380
  60.9 0.0 copy-done.8
  60.9 0.0 copy-done.3
  61.0 0.0 copy-start.4
  61.0 1.6 %copy-done.4 = bf16[1,1024,1024]{2,1,0:T(8,128)(2,1)S(1)} copy-done((bf16[1,1024,1024]{2,1,0:T(8,128)(2,1)S(1)}, bf16[1,1024,1024]{2,1,0:T(8,128)(2,1)}, u32[]{:S(2)}) %copy-start.4) | copy-done | bytes 2097176
  62.5 4.6 %shard_map.146 = (bf16[1,1024,1024]{2,1,0:T(8,128)(2,1)}, bf16[1,1024,1024]{2,1,0:T(8,128)(2,1)}, bf16[1,1024,1024]{2,1,0:T(8,128)(2,1)}) custom-call(s32[3]{0:T(128)S(1)} %copy-done.8, bf16[96,1024]{1,0:T(8,128)(2,1)S(1)} %get-tuple-element.45.hidden_ref, bf16[96,1024]{1,0:T(8,128)(2,1)S(1)} %get-tuple-element.28.rows_dy.dy_ref, ...), custom_call_target="tpu_custom_call" | custom-call | flops 201326592 | bytes 10485760 | tf_op jit(solution)/shard_map/pallas_call | solution.py:384
  67.2 6.6 %all-to-all-done.1.back_ref = bf16[16,48,256]{2,1,0:T(8,128)(2,1)S(1)} async-done(((bf16[16,48,256]{2,1,0:T(8,128)(2,1)}), bf16[16,48,256]{2,1,0:T(8,128)(2,1)S(1)}, u32[]{:S(2)}, u32[]{:S(2)}) %all-to-all-start.1) | async-done | bytes 393248 | tf_op jit(solution)/shard_map/all_to_all | solution.py:380
  73.8 1.6 %shard_map.145 = (bf16[128,4096]{1,0:T(8,128)(2,1)}, bf16[128,4096]{1,0:T(8,128)(2,1)}) custom-call(bf16[8,128,192]{2,1,0:T(8,128)(2,1)S(1)} %shard_map.141.spread_ref, bf16[16,48,256]{2,1,0:T(8,128)(2,1)S(1)} %all-to-all-done.1.back_ref), custom_call_target="tpu_custom_call" | custom-call | bytes 4194304 | tf_op jit(solution)/shard_map/pallas_call | solution.py:264
Async XLA Ops:
  0.6 23.5 %copy-start = (bf16[1,1024,1024]{2,1,0:T(8,128)(2,1)S(1)}, bf16[1,1024,1024]{2,1,0:T(8,128)(2,1)}, u32[]{:S(2)}) copy-start(bf16[1,1024,1024]{2,1,0:T(8,128)(2,1)} %refs_0_.1) | copy-start | bytes 6291460
  0.6 23.5 %copy-start.1 = (bf16[1,1024,1024]{2,1,0:T(8,128)(2,1)S(1)}, bf16[1,1024,1024]{2,1,0:T(8,128)(2,1)}, u32[]{:S(2)}) copy-start(bf16[1,1024,1024]{2,1,0:T(8,128)(2,1)} %refs_1_.1) | copy-start | bytes 6291460
  24.2 1.6 %copy-start.2 = (bf16[1,1024,1024]{2,1,0:T(8,128)(2,1)S(1)}, bf16[1,1024,1024]{2,1,0:T(8,128)(2,1)}, u32[]{:S(2)}) copy-start(bf16[1,1024,1024]{2,1,0:T(8,128)(2,1)} %refs_6_.1) | copy-start | bytes 6291460
  26.6 8.7 %collective-permute-start = (bf16[3,96,256]{2,1,0:T(8,128)(2,1)S(1)}, bf16[3,96,256]{2,1,0:T(8,128)(2,1)S(1)}, u32[]{:S(2)}, u32[]{:S(2)}) collective-permute-start(bf16[3,96,256]{2,1,0:T(8,128)(2,1)S(1)} %get-tuple-element.37), channel_id=1, source_target_pairs={{0,3},{1,2},{2,1},{3,0},{4,7},{5,6},{6,5},{7,4},{8,11},{9,10},{10,... | collective-permute-start | bytes 442376 | tf_op jit(solution)/shard_map/ppermute | solution.py:321
  27.5 14.1 %collective-permute-start.1 = (bf16[3,96,256]{2,1,0:T(8,128)(2,1)S(1)}, bf16[3,96,256]{2,1,0:T(8,128)(2,1)S(1)}, u32[]{:S(2)}, u32[]{:S(2)}) collective-permute-start(bf16[3,96,256]{2,1,0:T(8,128)(2,1)S(1)} %get-tuple-element.38), channel_id=1, source_target_pairs={{0,2},{1,3},{2,0},{3,1},{4,6},{5,7},{6,4},{7,5},{8,10},{9,11},{10,... | collective-permute-start | bytes 442376 | tf_op jit(solution)/shard_map/ppermute | solution.py:321
  28.0 4.2 %copy-start.6 = (f32[32,128]{1,0:T(8,128)S(1)}, f32[32,128]{1,0:T(8,128)}, u32[]{:S(2)}) copy-start(f32[32,128]{1,0:T(8,128)} %get-tuple-element.31.ones_ref) | copy-start | bytes 49156
  28.0 4.2 %copy-start.7 = (f32[32,128]{1,0:T(8,128)S(1)}, f32[32,128]{1,0:T(8,128)}, u32[]{:S(2)}) copy-start(f32[32,128]{1,0:T(8,128)} %get-tuple-element.32.gates_ref) | copy-start | bytes 49156
  28.0 13.5 %collective-permute-start.2 = (bf16[3,96,256]{2,1,0:T(8,128)(2,1)S(1)}, bf16[3,96,256]{2,1,0:T(8,128)(2,1)S(1)}, u32[]{:S(2)}, u32[]{:S(2)}) collective-permute-start(bf16[3,96,256]{2,1,0:T(8,128)(2,1)S(1)} %get-tuple-element.39), channel_id=1, source_target_pairs={{0,1},{1,0},{2,3},{3,2},{4,5},{5,4},{6,7},{7,6},{8,9},{9,8},{10,11... | collective-permute-start | bytes 442376 | tf_op jit(solution)/shard_map/ppermute | solution.py:321
  41.7 19.2 %copy-start.8 = (s32[3]{0:T(128)S(1)}, s32[3]{0:T(128)}, u32[]{:S(2)}) copy-start(s32[3]{0:T(128)} %selected_ref.1) | copy-start | bytes 40
  41.7 8.7 %collective-permute-start.5 = (bf16[3,96,256]{2,1,0:T(8,128)(2,1)S(1)}, bf16[3,96,256]{2,1,0:T(8,128)(2,1)S(1)}, u32[]{:S(2)}, u32[]{:S(2)}) collective-permute-start(bf16[3,96,256]{2,1,0:T(8,128)(2,1)S(1)} %shard_map.143.refs_0_), channel_id=1, source_target_pairs={{0,3},{1,2},{2,1},{3,0},{4,7},{5,6},{6,5},{7,4},{8,11},{9,10},{10,... | collective-permute-start | bytes 442376 | tf_op jit(solution)/shard_map/ppermute | solution.py:321
  43.4 11.3 %collective-permute-start.4 = (bf16[3,96,256]{2,1,0:T(8,128)(2,1)S(1)}, bf16[3,96,256]{2,1,0:T(8,128)(2,1)S(1)}, u32[]{:S(2)}, u32[]{:S(2)}) collective-permute-start(bf16[3,96,256]{2,1,0:T(8,128)(2,1)S(1)} %shard_map.143.refs_0_), channel_id=1, source_target_pairs={{0,1},{1,0},{2,3},{3,2},{4,5},{5,4},{6,7},{7,6},{8,9},{9,8},{10,11... | collective-permute-start | bytes 442376 | tf_op jit(solution)/shard_map/ppermute | solution.py:321
  43.4 11.8 %collective-permute-start.3 = (bf16[3,96,256]{2,1,0:T(8,128)(2,1)S(1)}, bf16[3,96,256]{2,1,0:T(8,128)(2,1)S(1)}, u32[]{:S(2)}, u32[]{:S(2)}) collective-permute-start(bf16[3,96,256]{2,1,0:T(8,128)(2,1)S(1)} %shard_map.143.refs_0_), channel_id=1, source_target_pairs={{0,2},{1,3},{2,0},{3,1},{4,6},{5,7},{6,4},{7,5},{8,10},{9,11},{10,... | collective-permute-start | bytes 442376 | tf_op jit(solution)/shard_map/ppermute | solution.py:321
  55.2 5.7 %copy-start.3 = (bf16[1,1024,1024]{2,1,0:T(8,128)(2,1)S(1)}, bf16[1,1024,1024]{2,1,0:T(8,128)(2,1)}, u32[]{:S(2)}) copy-start(bf16[1,1024,1024]{2,1,0:T(8,128)(2,1)} %first_ref.1) | copy-start | bytes 6291460
  56.6 0.7 copy-start.5
  57.4 16.4 %all-to-all-start.1 = ((bf16[16,48,256]{2,1,0:T(8,128)(2,1)}), bf16[16,48,256]{2,1,0:T(8,128)(2,1)S(1)}, u32[]{:S(2)}, u32[]{:S(2)}) async-start(bf16[16,48,256]{2,1,0:T(8,128)(2,1)} %copy-done.5), calls=%async_computation.1 | async-start | bytes 786432 | tf_op jit(solution)/shard_map/all_to_all | solution.py:380
  61.0 1.6 %copy-start.4 = (bf16[1,1024,1024]{2,1,0:T(8,128)(2,1)S(1)}, bf16[1,1024,1024]{2,1,0:T(8,128)(2,1)}, u32[]{:S(2)}) copy-start(bf16[1,1024,1024]{2,1,0:T(8,128)(2,1)} %second_ref.1) | copy-start | bytes 6291460

commit v7 on v6

--- a/solution.py
+++ b/solution.py
@@ -9,7 +9,7 @@
 
 CAP = 6
 CHUNKS = 4
-GROUP = 8
+GROUP = 4
 LINES = 2 * CHUNKS * CAP
 HALF = CHUNKS * CAP
 

time: 75.7 us -> 75.7 us (level)
  no operation moved by 1% of the time
where the time goes in v7:
time: 75.7 us; the launch traced here: 75.3 us
  waiting for transfers between devices  24.7 us (33%)
  blocking collectives  20.3 us (27%)
  Pallas kernels  14 us (18%)
  starting transfers between devices  12.5 us (17%)
  local copies, waits for them, and re-layouts  3.14 us (4%)
  between operations  0.8 us (1%)
    all_to_all x1, blocking collectives, local(): lax.all_to_all(sent, ('expert', 'dp'), split_axis=0, concat_axis=0, tiled...  20.3 us
    ppermute x6, waiting for transfers between devices, swap(): return lax.ppermute(value, 'dp', [(i, i ^ k) for i in range(dp)])  18.1 us
    pallas_call x9, Pallas kernels, call(): pl.pallas_call(kernel, out_shape=outs, in_specs=in_specs or [VMEM] * len(...  9.34 us
    ppermute x6, starting transfers between devices, swap(): return lax.ppermute(value, 'dp', [(i, i ^ k) for i in range(dp)])  8.91 us
    all_to_all x1, waiting for transfers between devices, local(): lax.all_to_all(results, ('expert', 'dp'), split_axis=0, concat_axis=0, ti...  6.6 us
    pallas_call x1, Pallas kernels, local(): pl.pallas_call(adam_kernel, grid=(hidden_units // strip,), in_specs=[SMEM...  4.61 us
    all_to_all x1, starting transfers between devices, local(): lax.all_to_all(results, ('expert', 'dp'), split_axis=0, concat_axis=0, ti...  3.55 us
    unnamed x18, local copies, waits for them, and re-layouts  3.14 us
  transfers between devices with their start and end apart: 7, of which 6 were waited for; matrix products, arithmetic and copies ran while one was open for 0% of the time, Pallas kernels for 8%

profile of v7, /device:TPU:0, one launch (start us, length us, event | category | flops | bytes accessed | tf_op | source)
XLA Modules:
  0.0 75.3 jit_solution(387407202173784999)
XLA Ops:
  0.6 0.0 copy-start
  0.6 0.0 copy-start.1
  0.7 2.8 %shard_map.137 = (bf16[16,48,256]{2,1,0:T(8,128)(2,1)}, f32[32,128]{1,0:T(8,128)}, f32[32,128]{1,0:T(8,128)}) custom-call(s32[8,128]{1,0:T(8,128)} %bitcast.2, s32[8,128]{1,0:T(8,128)} %bitcast.3, bf16[128,4096]{1,0:T(8,128)(2,1)} %tok_hbm.1, bf16[128,4096]{1,0:T(8,128)(2,1)} %cot_hbm.1), custom_call_target="tpu_custom_call" | custom-call | bytes 6291456 | tf_op jit(solution)/shard_map/pallas_call | solution.py:264
  3.5 20.3 %all_to_all.10.arrived_ref = bf16[16,48,256]{2,1,0:T(8,128)(2,1)S(1)} all-to-all(bf16[16,48,256]{2,1,0:T(8,128)(2,1)} %get-tuple-element.27), channel_id=1, replica_groups=mesh['groups'=2,'expert'=4,'dp'=4] {'expert','dp'}, dimensions={0} | all-to-all | bytes 786432 | tf_op jit(solution)/shard_map/all_to_all | solution.py:319
  23.8 0.3 shard_map.138
  24.0 0.0 copy-done
  24.0 0.0 copy-done.1
  24.0 0.0 copy-start.2
  24.1 0.8 %shard_map.139.pre_ref = f32[2,96,1024]{2,1,0:T(8,128)S(1)} custom-call(bf16[96,1024]{1,0:T(8,128)(2,1)S(1)} %get-tuple-element.29.rows_x, bf16[1,1024,1024]{2,1,0:T(8,128)(2,1)S(1)} %copy-done, bf16[1,1024,1024]{2,1,0:T(8,128)(2,1)S(1)} %copy-done.1), custom_call_target="tpu_custom_call" | custom-call | flops 300000000 | bytes 131072 | tf_op jit(solution)/shard_map/pallas_call | solution.py:264
  24.9 0.8 %copy-done.2 = bf16[1,1024,1024]{2,1,0:T(8,128)(2,1)S(1)} copy-done((bf16[1,1024,1024]{2,1,0:T(8,128)(2,1)S(1)}, bf16[1,1024,1024]{2,1,0:T(8,128)(2,1)}, u32[]{:S(2)}) %copy-start.2) | copy-done | bytes 2097176
  25.6 0.8 %shard_map.140 = (f32[3,96,256]{2,1,0:T(8,128)S(1)}, bf16[3,96,256]{2,1,0:T(8,128)(2,1)S(1)}, bf16[3,96,256]{2,1,0:T(8,128)(2,1)S(1)}, bf16[3,96,256]{2,1,0:T(8,128)(2,1)S(1)}) custom-call(bf16[96,1024]{1,0:T(8,128)(2,1)S(1)} %get-tuple-element.28.rows_dy.dy_ref, f32[2,96,1024]{2,1,0:T(8,128)S(1)} %shard_map.139.pre_ref, bf16[1,1024,1024]{2,1,0:T(8,128)(2,1)S(1)} %copy-done.2), custom_call_target="tpu_custom_call" | custom-call | flops 500000000 | bytes 131072 | tf_op jit(solution)/shard_map/pallas_call | solution.py:264
  26.5 1.0 %collective-permute-start = (bf16[3,96,256]{2,1,0:T(8,128)(2,1)S(1)}, bf16[3,96,256]{2,1,0:T(8,128)(2,1)S(1)}, u32[]{:S(2)}, u32[]{:S(2)}) collective-permute-start(bf16[3,96,256]{2,1,0:T(8,128)(2,1)S(1)} %get-tuple-element.37), channel_id=1, source_target_pairs={{0,3},{1,2},{2,1},{3,0},{4,7},{5,6},{6,5},{7,4},{8,11},{9,10},{10,... | collective-permute-start | bytes 442376 | tf_op jit(solution)/shard_map/ppermute | solution.py:321
  27.4 0.5 collective-permute-start.1
  27.9 0.0 copy-start.6
  27.9 0.0 copy-start.7
  27.9 3.0 %collective-permute-start.2 = (bf16[3,96,256]{2,1,0:T(8,128)(2,1)S(1)}, bf16[3,96,256]{2,1,0:T(8,128)(2,1)S(1)}, u32[]{:S(2)}, u32[]{:S(2)}) collective-permute-start(bf16[3,96,256]{2,1,0:T(8,128)(2,1)S(1)} %get-tuple-element.39), channel_id=1, source_target_pairs={{0,1},{1,0},{2,3},{3,2},{4,5},{5,4},{6,7},{7,6},{8,9},{9,8},{10,11... | collective-permute-start | bytes 442376 | tf_op jit(solution)/shard_map/ppermute | solution.py:321
  30.9 1.2 %shard_map.142 = (bf16[1024,1024]{1,0:T(8,128)(2,1)S(1)}, bf16[1024,1024]{1,0:T(8,128)(2,1)S(1)}) custom-call(bf16[1,1024,1024]{2,1,0:T(8,128)(2,1)S(1)} %copy-done, bf16[1,1024,1024]{2,1,0:T(8,128)(2,1)S(1)} %copy-done.1), custom_call_target="tpu_custom_call" | custom-call | bytes 4194304 | tf_op jit(solution)/shard_map/pallas_call | solution.py:264
  32.2 0.0 copy-done.6
  32.2 0.0 copy-done.7
  32.2 0.3 shard_map.141.spread_ref
  32.5 2.7 %collective-permute-done.refs_1_ = bf16[3,96,256]{2,1,0:T(8,128)(2,1)S(1)} collective-permute-done((bf16[3,96,256]{2,1,0:T(8,128)(2,1)S(1)}, bf16[3,96,256]{2,1,0:T(8,128)(2,1)S(1)}, u32[]{:S(2)}, u32[]{:S(2)}) %collective-permute-start) | collective-permute-done | bytes 147488 | tf_op jit(solution)/shard_map/ppermute | solution.py:321
  35.2 6.3 %collective-permute-done.1.refs_2_ = bf16[3,96,256]{2,1,0:T(8,128)(2,1)S(1)} collective-permute-done((bf16[3,96,256]{2,1,0:T(8,128)(2,1)S(1)}, bf16[3,96,256]{2,1,0:T(8,128)(2,1)S(1)}, u32[]{:S(2)}, u32[]{:S(2)}) %collective-permute-start.1) | collective-permute-done | bytes 147488 | tf_op jit(solution)/shard_map/ppermute | solution.py:321
  41.5 0.0 collective-permute-done.2.refs_3_
  41.5 0.1 shard_map.143.refs_0_
  41.6 0.0 copy-start.8
  41.6 1.7 %collective-permute-start.5 = (bf16[3,96,256]{2,1,0:T(8,128)(2,1)S(1)}, bf16[3,96,256]{2,1,0:T(8,128)(2,1)S(1)}, u32[]{:S(2)}, u32[]{:S(2)}) collective-permute-start(bf16[3,96,256]{2,1,0:T(8,128)(2,1)S(1)} %shard_map.143.refs_0_), channel_id=1, source_target_pairs={{0,3},{1,2},{2,1},{3,0},{4,7},{5,6},{6,5},{7,4},{8,11},{9,10},{10,... | collective-permute-start | bytes 442376 | tf_op jit(solution)/shard_map/ppermute | solution.py:321
  43.3 0.0 collective-permute-start.4
  43.3 2.8 %collective-permute-start.3 = (bf16[3,96,256]{2,1,0:T(8,128)(2,1)S(1)}, bf16[3,96,256]{2,1,0:T(8,128)(2,1)S(1)}, u32[]{:S(2)}, u32[]{:S(2)}) collective-permute-start(bf16[3,96,256]{2,1,0:T(8,128)(2,1)S(1)} %shard_map.143.refs_0_), channel_id=1, source_target_pairs={{0,2},{1,3},{2,0},{3,1},{4,6},{5,7},{6,4},{7,5},{8,10},{9,11},{10,... | collective-permute-start | bytes 442376 | tf_op jit(solution)/shard_map/ppermute | solution.py:321
  46.1 4.2 %collective-permute-done.5.refs_3_ = bf16[3,96,256]{2,1,0:T(8,128)(2,1)S(1)} collective-permute-done((bf16[3,96,256]{2,1,0:T(8,128)(2,1)S(1)}, bf16[3,96,256]{2,1,0:T(8,128)(2,1)S(1)}, u32[]{:S(2)}, u32[]{:S(2)}) %collective-permute-start.5) | collective-permute-done | bytes 147488 | tf_op jit(solution)/shard_map/ppermute | solution.py:321
  50.3 4.3 %collective-permute-done.4.refs_2_ = bf16[3,96,256]{2,1,0:T(8,128)(2,1)S(1)} collective-permute-done((bf16[3,96,256]{2,1,0:T(8,128)(2,1)S(1)}, bf16[3,96,256]{2,1,0:T(8,128)(2,1)S(1)}, u32[]{:S(2)}, u32[]{:S(2)}) %collective-permute-start.4) | collective-permute-done | bytes 147488 | tf_op jit(solution)/shard_map/ppermute | solution.py:321
  54.6 0.6 collective-permute-done.3.refs_1_
  55.1 0.0 copy-start.3
  55.1 1.4 %shard_map.144 = (bf16[16,48,256]{2,1,0:T(8,128)(2,1)S(1)}, bf16[96,1024]{1,0:T(8,128)(2,1)S(1)}) custom-call(bf16[3,96,256]{2,1,0:T(8,128)(2,1)S(1)} %shard_map.143.refs_0_, bf16[3,96,256]{2,1,0:T(8,128)(2,1)S(1)} %collective-permute-done.3.refs_1_, bf16[3,96,256]{2,1,0:T(8,128)(2,1)S(1)} %collective-permute-done.4.refs_2_, ...), custom_call_target="tpu_custom_call" | custom-call | flops 603979776 | bytes 8388608 | tf_op jit(solution)/shard_map/pallas_call | solution.py:264
  56.5 0.0 copy-start.5
  56.5 0.7 copy-done.5
  57.3 3.6 %all-to-all-start.1 = ((bf16[16,48,256]{2,1,0:T(8,128)(2,1)}), bf16[16,48,256]{2,1,0:T(8,128)(2,1)S(1)}, u32[]{:S(2)}, u32[]{:S(2)}) async-start(bf16[16,48,256]{2,1,0:T(8,128)(2,1)} %copy-done.5), calls=%async_computation.1 | async-start | bytes 786432 | tf_op jit(solution)/shard_map/all_to_all | solution.py:380
  60.8 0.0 copy-done.8
  60.8 0.0 copy-done.3
  60.9 0.0 copy-start.4
  60.9 1.6 %copy-done.4 = bf16[1,1024,1024]{2,1,0:T(8,128)(2,1)S(1)} copy-done((bf16[1,1024,1024]{2,1,0:T(8,128)(2,1)S(1)}, bf16[1,1024,1024]{2,1,0:T(8,128)(2,1)}, u32[]{:S(2)}) %copy-start.4) | copy-done | bytes 2097176
  62.5 4.6 %shard_map.146 = (bf16[1,1024,1024]{2,1,0:T(8,128)(2,1)}, bf16[1,1024,1024]{2,1,0:T(8,128)(2,1)}, bf16[1,1024,1024]{2,1,0:T(8,128)(2,1)}) custom-call(s32[3]{0:T(128)S(1)} %copy-done.8, bf16[96,1024]{1,0:T(8,128)(2,1)S(1)} %get-tuple-element.45.hidden_ref, bf16[96,1024]{1,0:T(8,128)(2,1)S(1)} %get-tuple-element.28.rows_dy.dy_ref, ...), custom_call_target="tpu_custom_call" | custom-call | flops 201326592 | bytes 10485760 | tf_op jit(solution)/shard_map/pallas_call | solution.py:384
  67.1 6.6 %all-to-all-done.1.back_ref = bf16[16,48,256]{2,1,0:T(8,128)(2,1)S(1)} async-done(((bf16[16,48,256]{2,1,0:T(8,128)(2,1)}), bf16[16,48,256]{2,1,0:T(8,128)(2,1)S(1)}, u32[]{:S(2)}, u32[]{:S(2)}) %all-to-all-start.1) | async-done | bytes 393248 | tf_op jit(solution)/shard_map/all_to_all | solution.py:380
  73.7 1.6 %shard_map.145 = (bf16[128,4096]{1,0:T(8,128)(2,1)}, bf16[128,4096]{1,0:T(8,128)(2,1)}) custom-call(bf16[8,128,192]{2,1,0:T(8,128)(2,1)S(1)} %shard_map.141.spread_ref, bf16[16,48,256]{2,1,0:T(8,128)(2,1)S(1)} %all-to-all-done.1.back_ref), custom_call_target="tpu_custom_call" | custom-call | bytes 4194304 | tf_op jit(solution)/shard_map/pallas_call | solution.py:264
Async XLA Ops:
  0.6 23.4 %copy-start = (bf16[1,1024,1024]{2,1,0:T(8,128)(2,1)S(1)}, bf16[1,1024,1024]{2,1,0:T(8,128)(2,1)}, u32[]{:S(2)}) copy-start(bf16[1,1024,1024]{2,1,0:T(8,128)(2,1)} %refs_0_.1) | copy-start | bytes 6291460
  0.6 23.4 %copy-start.1 = (bf16[1,1024,1024]{2,1,0:T(8,128)(2,1)S(1)}, bf16[1,1024,1024]{2,1,0:T(8,128)(2,1)}, u32[]{:S(2)}) copy-start(bf16[1,1024,1024]{2,1,0:T(8,128)(2,1)} %refs_1_.1) | copy-start | bytes 6291460
  24.0 1.6 %copy-start.2 = (bf16[1,1024,1024]{2,1,0:T(8,128)(2,1)S(1)}, bf16[1,1024,1024]{2,1,0:T(8,128)(2,1)}, u32[]{:S(2)}) copy-start(bf16[1,1024,1024]{2,1,0:T(8,128)(2,1)} %refs_6_.1) | copy-start | bytes 6291460
  26.5 8.7 %collective-permute-start = (bf16[3,96,256]{2,1,0:T(8,128)(2,1)S(1)}, bf16[3,96,256]{2,1,0:T(8,128)(2,1)S(1)}, u32[]{:S(2)}, u32[]{:S(2)}) collective-permute-start(bf16[3,96,256]{2,1,0:T(8,128)(2,1)S(1)} %get-tuple-element.37), channel_id=1, source_target_pairs={{0,3},{1,2},{2,1},{3,0},{4,7},{5,6},{6,5},{7,4},{8,11},{9,10},{10,... | collective-permute-start | bytes 442376 | tf_op jit(solution)/shard_map/ppermute | solution.py:321
  27.4 14.1 %collective-permute-start.1 = (bf16[3,96,256]{2,1,0:T(8,128)(2,1)S(1)}, bf16[3,96,256]{2,1,0:T(8,128)(2,1)S(1)}, u32[]{:S(2)}, u32[]{:S(2)}) collective-permute-start(bf16[3,96,256]{2,1,0:T(8,128)(2,1)S(1)} %get-tuple-element.38), channel_id=1, source_target_pairs={{0,2},{1,3},{2,0},{3,1},{4,6},{5,7},{6,4},{7,5},{8,10},{9,11},{10,... | collective-permute-start | bytes 442376 | tf_op jit(solution)/shard_map/ppermute | solution.py:321
  27.9 4.2 %copy-start.6 = (f32[32,128]{1,0:T(8,128)S(1)}, f32[32,128]{1,0:T(8,128)}, u32[]{:S(2)}) copy-start(f32[32,128]{1,0:T(8,128)} %get-tuple-element.31.ones_ref) | copy-start | bytes 49156
  27.9 4.2 %copy-start.7 = (f32[32,128]{1,0:T(8,128)S(1)}, f32[32,128]{1,0:T(8,128)}, u32[]{:S(2)}) copy-start(f32[32,128]{1,0:T(8,128)} %get-tuple-element.32.gates_ref) | copy-start | bytes 49156
  27.9 13.5 %collective-permute-start.2 = (bf16[3,96,256]{2,1,0:T(8,128)(2,1)S(1)}, bf16[3,96,256]{2,1,0:T(8,128)(2,1)S(1)}, u32[]{:S(2)}, u32[]{:S(2)}) collective-permute-start(bf16[3,96,256]{2,1,0:T(8,128)(2,1)S(1)} %get-tuple-element.39), channel_id=1, source_target_pairs={{0,1},{1,0},{2,3},{3,2},{4,5},{5,4},{6,7},{7,6},{8,9},{9,8},{10,11... | collective-permute-start | bytes 442376 | tf_op jit(solution)/shard_map/ppermute | solution.py:321
  41.6 19.2 %copy-start.8 = (s32[3]{0:T(128)S(1)}, s32[3]{0:T(128)}, u32[]{:S(2)}) copy-start(s32[3]{0:T(128)} %selected_ref.1) | copy-start | bytes 40
  41.6 8.7 %collective-permute-start.5 = (bf16[3,96,256]{2,1,0:T(8,128)(2,1)S(1)}, bf16[3,96,256]{2,1,0:T(8,128)(2,1)S(1)}, u32[]{:S(2)}, u32[]{:S(2)}) collective-permute-start(bf16[3,96,256]{2,1,0:T(8,128)(2,1)S(1)} %shard_map.143.refs_0_), channel_id=1, source_target_pairs={{0,3},{1,2},{2,1},{3,0},{4,7},{5,6},{6,5},{7,4},{8,11},{9,10},{10,... | collective-permute-start | bytes 442376 | tf_op jit(solution)/shard_map/ppermute | solution.py:321
  43.3 11.3 %collective-permute-start.4 = (bf16[3,96,256]{2,1,0:T(8,128)(2,1)S(1)}, bf16[3,96,256]{2,1,0:T(8,128)(2,1)S(1)}, u32[]{:S(2)}, u32[]{:S(2)}) collective-permute-start(bf16[3,96,256]{2,1,0:T(8,128)(2,1)S(1)} %shard_map.143.refs_0_), channel_id=1, source_target_pairs={{0,1},{1,0},{2,3},{3,2},{4,5},{5,4},{6,7},{7,6},{8,9},{9,8},{10,11... | collective-permute-start | bytes 442376 | tf_op jit(solution)/shard_map/ppermute | solution.py:321
  43.3 11.8 %collective-permute-start.3 = (bf16[3,96,256]{2,1,0:T(8,128)(2,1)S(1)}, bf16[3,96,256]{2,1,0:T(8,128)(2,1)S(1)}, u32[]{:S(2)}, u32[]{:S(2)}) collective-permute-start(bf16[3,96,256]{2,1,0:T(8,128)(2,1)S(1)} %shard_map.143.refs_0_), channel_id=1, source_target_pairs={{0,2},{1,3},{2,0},{3,1},{4,6},{5,7},{6,4},{7,5},{8,10},{9,11},{10,... | collective-permute-start | bytes 442376 | tf_op jit(solution)/shard_map/ppermute | solution.py:321
  55.1 5.7 %copy-start.3 = (bf16[1,1024,1024]{2,1,0:T(8,128)(2,1)S(1)}, bf16[1,1024,1024]{2,1,0:T(8,128)(2,1)}, u32[]{:S(2)}) copy-start(bf16[1,1024,1024]{2,1,0:T(8,128)(2,1)} %first_ref.1) | copy-start | bytes 6291460
  56.5 0.7 copy-start.5
  57.3 16.4 %all-to-all-start.1 = ((bf16[16,48,256]{2,1,0:T(8,128)(2,1)}), bf16[16,48,256]{2,1,0:T(8,128)(2,1)S(1)}, u32[]{:S(2)}, u32[]{:S(2)}) async-start(bf16[16,48,256]{2,1,0:T(8,128)(2,1)} %copy-done.5), calls=%async_computation.1 | async-start | bytes 786432 | tf_op jit(solution)/shard_map/all_to_all | solution.py:380
  60.9 1.6 %copy-start.4 = (bf16[1,1024,1024]{2,1,0:T(8,128)(2,1)S(1)}, bf16[1,1024,1024]{2,1,0:T(8,128)(2,1)}, u32[]{:S(2)}) copy-start(bf16[1,1024,1024]{2,1,0:T(8,128)(2,1)} %second_ref.1) | copy-start | bytes 6291460
